TPU v7x, 128 devices: a whole 4x4x4 slice. The times are simulated.
128 devices in a mesh: rep: 16 (over y, z_lo, core), ep: 8 (over x, z_hi).
Axes of the slice: x: 4, y: 4, z: 4 (z_hi: 2, z_lo: 2; z = z_hi * 2 + z_lo), core: 2. Of those that a mesh axis runs over, the one named last changes fastest.
Arguments:
- tokens: bfloat16 [16384, 1280], P(('rep', 'ep')), may hold values from -6 to 6
- cotangent: bfloat16 [16384, 1280], P(('rep', 'ep')), may hold values from -6 to 6
- lengths: int32 [16], P('rep'), may hold values from 128 to 1024, as said below
- token_mask: int32 [16384], P(('rep', 'ep')), may hold values 0 or 1
- routes: int32 [16384, 7], P(('rep', 'ep')), may hold values from 0 to 15, all different within a row; in each aligned block of 128 rows (0 to 127, 128 to 255, ...) at most 88 rows name the same one
- w_query: bfloat16 [1280, 1280], P(('rep', 'ep')), may hold values from -0.15625 to 0.15625
- w_key: bfloat16 [1280, 1280], P(('rep', 'ep')), may hold values from -0.15625 to 0.15625
- w_value: bfloat16 [1280, 1280], P(('rep', 'ep')), may hold values from -0.15625 to 0.15625
- w_output: bfloat16 [1280, 1280], P(('rep', 'ep')), may hold values from -1.25 to 1.25
- w_router: bfloat16 [1280, 16], P(('rep', 'ep')), may hold values from -0.078125 to 0.078125
- shared_gate: bfloat16 [1280, 896], P(('rep', 'ep')), may hold values from -0.15625 to 0.15625
- shared_up: bfloat16 [1280, 896], P(('rep', 'ep')), may hold values from -0.15625 to 0.15625
- shared_down: bfloat16 [896, 1280], P(('rep', 'ep')), may hold values from -0.375 to 0.375
- norm_attn: bfloat16 [1280], P(('rep', 'ep')), may hold values from 0.5 to 1.5
- norm_ffn: bfloat16 [1280], P(('rep', 'ep')), may hold values from 0.5 to 1.5
- expert_gate: bfloat16 [16, 1280, 896], P('ep'), may hold values from -0.15625 to 0.15625
- expert_up: bfloat16 [16, 1280, 896], P('ep'), may hold values from -0.15625 to 0.15625
- expert_down: bfloat16 [16, 896, 1280], P('ep'), may hold values from -1.5 to 1.5
Outputs:
- out: bfloat16 [16384, 1280], P(('rep', 'ep'))
- d_tokens: float32 [16384, 1280], P(('rep', 'ep'))
- d_query: float32 [1280, 1280], P(('rep', 'ep'))
- d_key: float32 [1280, 1280], P(('rep', 'ep'))
- d_value: float32 [1280, 1280], P(('rep', 'ep'))
- d_output: float32 [1280, 1280], P(('rep', 'ep'))
- d_router: float32 [1280, 16], P(('rep', 'ep'))
- d_shared_gate: float32 [1280, 896], P(('rep', 'ep'))
- d_shared_up: float32 [1280, 896], P(('rep', 'ep'))
- d_shared_down: float32 [896, 1280], P(('rep', 'ep'))
- d_norm_attn: float32 [1280], P(('rep', 'ep'))
- d_norm_ffn: float32 [1280], P(('rep', 'ep'))
- d_expert_gate: float32 [16, 1280, 896], P('ep')
- d_expert_up: float32 [16, 1280, 896], P('ep')
- d_expert_down: float32 [16, 896, 1280], P('ep')
Inputs may be any that keep to these rules, and one draw needn't show every extreme that they name: `lengths`: in every draw some sequence has length 1024. `routes`: each token names 7 different experts. Among the rows of one device, no expert is named more than 88 times, a bound that some block reaches.
All inputs are finite; a program needn't handle non-finite values. No bound on the sum of `token_mask` on one device may be relied on, other than what follows from the above.
Results may differ from a plain program's by a relative error of at most 0.024.
Values may be sent and summed in bfloat16 or wider, within the bound.
A program may use at most 320 MiB of HBM per device.

v0:
```python
import jax
import jax.numpy as jnp
from jax import lax
from jax.sharding import PartitionSpec as P

HD = 128


epsilon = 1e-06
highest = lax.Precision.HIGHEST


def normalize(values, gain_vector):
    return (
        values
        * lax.rsqrt(jnp.mean(values * values, axis=-1, keepdims=True) + epsilon)
        * gain_vector
    )


def rotate(values, cosine, sine_table):
    half_dim = values.shape[-1] // 2
    front_half = values[..., :half_dim]
    back_half = values[..., half_dim:]
    cos_part = cosine[:, None, :]
    sin_part = sine_table[:, None, :]
    return jnp.concatenate(
        [
            front_half * cos_part - back_half * sin_part,
            back_half * cos_part + front_half * sin_part,
        ],
        axis=-1,
    )


def swiglu(gate_part, lift_part):
    return jax.nn.silu(gate_part) * lift_part


def route_weights(logits, routes, token_live):
    return (
        jnp.take_along_axis(jax.nn.softmax(logits, axis=-1), routes, axis=1) * token_live[:, None]
    )


def matmul(operand, matrix):
    return jnp.dot(operand, matrix, preferred_element_type=jnp.float32)


def body(
    tokens,
    cotangent,
    lengths,
    token_mask,
    routes,
    w_query,
    w_key,
    w_value,
    w_output,
    w_router,
    shared_gate,
    shared_up,
    shared_down,
    norm_attn,
    norm_ffn,
    expert_gate,
    expert_up,
    expert_down,
):
    tok_dev = tokens.shape[0]
    model_width = tokens.shape[1]
    head_count = model_width // HD
    top_count = routes.shape[1]
    ep_count = lax.axis_size("ep")
    ep_index = lax.axis_index("ep")
    group_tokens = tok_dev * ep_count
    exp_dev = expert_gate.shape[0]
    experts = exp_dev * ep_count
    capacity = min(tok_dev, (tok_dev * top_count * 3 // (2 * experts) + 7) // 8 * 8)
    score_scale = HD ** (-0.5)
    row_count = tok_dev * top_count
    position = ep_index * tok_dev + jnp.arange(tok_dev, dtype=jnp.int32)
    token_live = ((position < lengths[0]) & (token_mask == 1)).astype(jnp.float32)
    half_dim = HD // 2
    frequency = 10000.0 ** (-(jnp.arange(half_dim, dtype=jnp.float32) * 2.0 / HD))
    angles = position.astype(jnp.float32)[:, None] * frequency[None, :]
    cosine = jnp.cos(angles)
    sine_table = jnp.sin(angles)
    (
        full_query,
        full_key,
        full_value,
        full_output,
        full_router,
        full_gate,
        full_lift,
        full_down,
        first_gain,
        second_gain,
    ) = (
        lax.all_gather(w_query, ("rep", "ep"), axis=0, tiled=True),
        lax.all_gather(w_key, ("rep", "ep"), axis=0, tiled=True),
        lax.all_gather(w_value, ("rep", "ep"), axis=0, tiled=True),
        lax.all_gather(w_output, ("rep", "ep"), axis=0, tiled=True),
        lax.all_gather(w_router, ("rep", "ep"), axis=0, tiled=True),
        lax.all_gather(shared_gate, ("rep", "ep"), axis=0, tiled=True),
        lax.all_gather(shared_up, ("rep", "ep"), axis=0, tiled=True),
        lax.all_gather(shared_down, ("rep", "ep"), axis=0, tiled=True),
        lax.all_gather(norm_attn, ("rep", "ep"), axis=0, tiled=True),
        lax.all_gather(norm_ffn, ("rep", "ep"), axis=0, tiled=True),
    )
    inputs = tokens.astype(jnp.float32)
    hidden_one = normalize(inputs, first_gain.astype(jnp.float32)).astype(jnp.bfloat16)
    query_raw = matmul(hidden_one, full_query).reshape(tok_dev, head_count, HD)
    key_raw = matmul(hidden_one, full_key).reshape(tok_dev, head_count, HD)
    value_low = matmul(hidden_one, full_value).astype(jnp.bfloat16).reshape(tok_dev, head_count, HD)
    query_rot = rotate(query_raw, cosine, sine_table).astype(jnp.bfloat16)
    key_rot = rotate(key_raw, cosine, sine_table).astype(jnp.bfloat16)
    keys_all, values_all, live_all = (
        lax.all_gather(key_rot, "ep", axis=0, tiled=True),
        lax.all_gather(value_low, "ep", axis=0, tiled=True),
        lax.all_gather(token_live.astype(jnp.bfloat16), "ep", axis=0, tiled=True),
    )
    query_pos = position[:, None]
    key_pos = jnp.arange(group_tokens, dtype=jnp.int32)[None, :]
    allowed = (key_pos <= query_pos) & ((live_all[None, :] > 0.5) | (key_pos == query_pos))
    scores = (
        jnp.einsum("qhd,khd->hqk", query_rot, keys_all, preferred_element_type=jnp.float32)
        * score_scale
    )
    scores = jnp.where(allowed[None], scores, -1e30)
    top_score = jnp.max(scores, axis=-1, keepdims=True)
    exponent = jnp.exp(scores - top_score)
    row_total = jnp.sum(exponent, axis=-1, keepdims=True)
    attention_probs = exponent / row_total
    log_total = top_score + jnp.log(row_total)
    attend = jnp.einsum(
        "hqk,khd->qhd",
        attention_probs.astype(jnp.bfloat16),
        values_all,
        preferred_element_type=jnp.float32,
    )
    attend_low = attend.reshape(tok_dev, model_width).astype(jnp.bfloat16)
    branch = matmul(attend_low, full_output)
    residual = inputs + token_live[:, None] * branch
    second_float = second_gain.astype(jnp.float32)
    hidden_two = normalize(residual, second_float).astype(jnp.bfloat16)
    hidden_float = hidden_two.astype(jnp.float32)
    router_float = full_router.astype(jnp.float32)
    logits = jnp.dot(
        hidden_float, router_float, precision=highest, preferred_element_type=jnp.float32
    )
    gate_weights = route_weights(logits, routes, token_live)
    shared_gval = matmul(hidden_two, full_gate)
    shared_lval = matmul(hidden_two, full_lift)
    shared_act = swiglu(shared_gval, shared_lval).astype(jnp.bfloat16)
    shared_out = matmul(shared_act, full_down)
    flat_expert = routes.reshape(-1)
    one_hot = (flat_expert[:, None] == jnp.arange(experts, dtype=jnp.int32)[None, :]).astype(
        jnp.int32
    )
    slot_index = jnp.sum((jnp.cumsum(one_hot, axis=0) - 1) * one_hot, axis=1)
    destination = flat_expert * capacity + slot_index
    source_row = (
        jnp.full((experts * capacity,), row_count, jnp.int32)
        .at[destination]
        .set(jnp.arange(row_count, dtype=jnp.int32))
    )
    source_token = jnp.where(source_row < row_count, source_row // top_count, tok_dev)
    padded_hidden = jnp.concatenate([hidden_two, jnp.zeros((1, model_width), jnp.bfloat16)], axis=0)
    outgoing = padded_hidden[source_token].reshape(ep_count, exp_dev, capacity, model_width)
    incoming = lax.all_to_all(outgoing, "ep", split_axis=0, concat_axis=0, tiled=True)
    expert_gval = jnp.einsum(
        "sekd,edf->sekf", incoming, expert_gate, preferred_element_type=jnp.float32
    )
    expert_lval = jnp.einsum(
        "sekd,edf->sekf", incoming, expert_up, preferred_element_type=jnp.float32
    )
    expert_act = swiglu(expert_gval, expert_lval).astype(jnp.bfloat16)
    expert_res = jnp.einsum(
        "sekf,efd->sekd", expert_act, expert_down, preferred_element_type=jnp.float32
    ).astype(jnp.bfloat16)
    returned = lax.all_to_all(expert_res, "ep", split_axis=0, concat_axis=0, tiled=True).reshape(
        experts * capacity, model_width
    )
    chosen_rows = returned[destination].reshape(tok_dev, top_count, model_width).astype(jnp.float32)
    routed = jnp.sum(gate_weights[:, :, None] * chosen_rows, axis=1)
    result = residual + token_live[:, None] * shared_out + routed
    grad_out = cotangent.astype(jnp.float32)
    grad_rows = (
        (gate_weights[:, :, None] * grad_out[:, None, :])
        .astype(jnp.bfloat16)
        .reshape(row_count, model_width)
    )
    padded_grad = jnp.concatenate([grad_rows, jnp.zeros((1, model_width), jnp.bfloat16)], axis=0)
    grad_outgoing = padded_grad[source_row].reshape(ep_count, exp_dev, capacity, model_width)
    grad_incoming = lax.all_to_all(grad_outgoing, "ep", split_axis=0, concat_axis=0, tiled=True)
    grad_gates = jnp.sum(grad_out[:, None, :] * chosen_rows, axis=2)
    grad_act = jnp.einsum(
        "sekd,efd->sekf", grad_incoming, expert_down, preferred_element_type=jnp.float32
    )
    grad_edown = jnp.einsum(
        "sekf,sekd->efd", expert_act, grad_incoming, preferred_element_type=jnp.float32
    )
    _, expert_back = jax.vjp(swiglu, expert_gval, expert_lval)
    grad_gval, grad_lval = expert_back(grad_act)
    grad_gval = grad_gval.astype(jnp.bfloat16)
    grad_lval = grad_lval.astype(jnp.bfloat16)
    grad_egate = jnp.einsum(
        "sekd,sekf->edf", incoming, grad_gval, preferred_element_type=jnp.float32
    )
    grad_elift = jnp.einsum(
        "sekd,sekf->edf", incoming, grad_lval, preferred_element_type=jnp.float32
    )
    grad_inrows = jnp.einsum(
        "sekf,edf->sekd", grad_gval, expert_gate, preferred_element_type=jnp.float32
    ) + jnp.einsum("sekf,edf->sekd", grad_lval, expert_up, preferred_element_type=jnp.float32)
    grad_back = lax.all_to_all(
        grad_inrows.astype(jnp.bfloat16), "ep", split_axis=0, concat_axis=0, tiled=True
    ).reshape(experts * capacity, model_width)
    grad_hidden = jnp.sum(
        grad_back[destination].reshape(tok_dev, top_count, model_width).astype(jnp.float32), axis=1
    )
    expert_sums = (
        lax.psum(grad_egate.astype(jnp.bfloat16), "rep").astype(jnp.float32),
        lax.psum(grad_elift.astype(jnp.bfloat16), "rep").astype(jnp.float32),
        lax.psum(grad_edown.astype(jnp.bfloat16), "rep").astype(jnp.float32),
    )

    def pick_gates(values):
        return route_weights(values, routes, token_live)

    _, route_back = jax.vjp(pick_gates, logits)
    (grad_logits,) = route_back(grad_gates)
    grad_router = jnp.dot(
        hidden_float.T, grad_logits, precision=highest, preferred_element_type=jnp.float32
    )
    grad_hidden = grad_hidden + jnp.dot(
        grad_logits, router_float.T, precision=highest, preferred_element_type=jnp.float32
    )
    grad_shared = (token_live[:, None] * grad_out).astype(jnp.bfloat16)
    grad_sdown = matmul(shared_act.T, grad_shared)
    grad_sact = matmul(grad_shared, full_down.T)
    _, shared_back = jax.vjp(swiglu, shared_gval, shared_lval)
    grad_sgval, grad_slval = shared_back(grad_sact)
    grad_sgval = grad_sgval.astype(jnp.bfloat16)
    grad_slval = grad_slval.astype(jnp.bfloat16)
    grad_sgate = matmul(hidden_two.T, grad_sgval)
    grad_slift = matmul(hidden_two.T, grad_slval)
    grad_hidden = grad_hidden + matmul(grad_sgval, full_gate.T) + matmul(grad_slval, full_lift.T)
    _, norm_two_back = jax.vjp(normalize, residual, second_float)
    grad_resid_norm, grad_second = norm_two_back(grad_hidden)
    grad_residual = grad_out + grad_resid_norm
    grad_branch = (token_live[:, None] * grad_residual).astype(jnp.bfloat16)
    grad_output = matmul(attend_low.T, grad_branch)
    grad_attend = (
        matmul(grad_branch, full_output.T).astype(jnp.bfloat16).reshape(tok_dev, head_count, HD)
    )
    scores_again = (
        jnp.einsum("qhd,khd->hqk", query_rot, keys_all, preferred_element_type=jnp.float32)
        * score_scale
    )
    probs_again = jnp.where(allowed[None], jnp.exp(scores_again - log_total), 0.0)
    grad_probs = jnp.einsum(
        "qhd,khd->hqk", grad_attend, values_all, preferred_element_type=jnp.float32
    )
    row_delta = jnp.sum(probs_again * grad_probs, axis=-1, keepdims=True)
    grad_scores = probs_again * (grad_probs - row_delta)
    grad_scores = jnp.where(allowed[None], grad_scores, 0.0).astype(jnp.bfloat16)
    grad_query = (
        jnp.einsum("hqk,khd->qhd", grad_scores, keys_all, preferred_element_type=jnp.float32)
        * score_scale
    )
    grad_values_all = jnp.einsum(
        "hqk,qhd->khd",
        probs_again.astype(jnp.bfloat16),
        grad_attend,
        preferred_element_type=jnp.float32,
    )
    grad_keys_all = (
        jnp.einsum("hqk,qhd->khd", grad_scores, query_rot, preferred_element_type=jnp.float32)
        * score_scale
    )
    grad_key_local, grad_value_local = (
        lax.psum_scatter(
            grad_keys_all.astype(jnp.bfloat16), "ep", scatter_dimension=0, tiled=True
        ).astype(jnp.float32),
        lax.psum_scatter(
            grad_values_all.astype(jnp.bfloat16), "ep", scatter_dimension=0, tiled=True
        ).astype(jnp.float32),
    )

    def turn(values):
        return rotate(values, cosine, sine_table)

    _, turn_back = jax.vjp(turn, query_raw)
    grad_qraw = turn_back(grad_query)[0].astype(jnp.bfloat16).reshape(tok_dev, model_width)
    grad_kraw = turn_back(grad_key_local)[0].astype(jnp.bfloat16).reshape(tok_dev, model_width)
    grad_vraw = grad_value_local.astype(jnp.bfloat16).reshape(tok_dev, model_width)
    grad_wquery = matmul(hidden_one.T, grad_qraw)
    grad_wkey = matmul(hidden_one.T, grad_kraw)
    grad_wvalue = matmul(hidden_one.T, grad_vraw)
    grad_hidden_one = (
        matmul(grad_qraw, full_query.T)
        + matmul(grad_kraw, full_key.T)
        + matmul(grad_vraw, full_value.T)
    )
    _, norm_one_back = jax.vjp(normalize, inputs, first_gain.astype(jnp.float32))
    grad_inputs_norm, grad_first = norm_one_back(grad_hidden_one)
    grad_tokens = grad_residual + grad_inputs_norm
    dense_parts = (
        lax.psum_scatter(grad_wquery, ("rep", "ep"), scatter_dimension=0, tiled=True),
        lax.psum_scatter(grad_wkey, ("rep", "ep"), scatter_dimension=0, tiled=True),
        lax.psum_scatter(grad_wvalue, ("rep", "ep"), scatter_dimension=0, tiled=True),
        lax.psum_scatter(grad_output, ("rep", "ep"), scatter_dimension=0, tiled=True),
        lax.psum_scatter(grad_router, ("rep", "ep"), scatter_dimension=0, tiled=True),
        lax.psum_scatter(grad_sgate, ("rep", "ep"), scatter_dimension=0, tiled=True),
        lax.psum_scatter(grad_slift, ("rep", "ep"), scatter_dimension=0, tiled=True),
        lax.psum_scatter(grad_sdown, ("rep", "ep"), scatter_dimension=0, tiled=True),
        lax.psum_scatter(grad_first, ("rep", "ep"), scatter_dimension=0, tiled=True),
        lax.psum_scatter(grad_second, ("rep", "ep"), scatter_dimension=0, tiled=True),
    )
    return (
        result.astype(jnp.bfloat16),
        grad_tokens,
        dense_parts[0],
        dense_parts[1],
        dense_parts[2],
        dense_parts[3],
        dense_parts[4],
        dense_parts[5],
        dense_parts[6],
        dense_parts[7],
        dense_parts[8],
        dense_parts[9],
        expert_sums[0],
        expert_sums[1],
        expert_sums[2],
    )


def solution(mesh):
    in_specs = (
        P(("rep", "ep"), None),
        P(("rep", "ep"), None),
        P("rep"),
        P(("rep", "ep")),
        P(("rep", "ep"), None),
        P(("rep", "ep"), None),
        P(("rep", "ep"), None),
        P(("rep", "ep"), None),
        P(("rep", "ep"), None),
        P(("rep", "ep"), None),
        P(("rep", "ep"), None),
        P(("rep", "ep"), None),
        P(("rep", "ep"), None),
        P(("rep", "ep")),
        P(("rep", "ep")),
        P("ep", None, None),
        P("ep", None, None),
        P("ep", None, None),
    )
    out_specs = (
        P(("rep", "ep"), None),
        P(("rep", "ep"), None),
        P(("rep", "ep"), None),
        P(("rep", "ep"), None),
        P(("rep", "ep"), None),
        P(("rep", "ep"), None),
        P(("rep", "ep"), None),
        P(("rep", "ep"), None),
        P(("rep", "ep"), None),
        P(("rep", "ep"), None),
        P(("rep", "ep")),
        P(("rep", "ep")),
        P("ep", None, None),
        P("ep", None, None),
        P("ep", None, None),
    )
    return jax.shard_map(body, mesh=mesh, in_specs=in_specs, out_specs=out_specs, check_vma=False)
```

profile of v0, /device:TPU:1, one launch (start us, length us, event | category | flops | bytes accessed | tf_op | source)
XLA Modules:
  0.0 3505.6 jit_solution(4378690039074113485)
XLA Ops:
  11.7 68.9 %all-reduce.21 = (bf16[1280]{0:T(1024)(128)(2,1)S(1)}, bf16[1280]{0:T(1024)(128)(2,1)S(1)}) all-reduce(bf16[1280]{0:T(1024)(128)(2,1)S(1)} %dynamic-update-slice, bf16[1280]{0:T(1024)(128)(2,1)S(1)} %dynamic-update-slice.1), channel_id=1, replica_groups=mesh['rep'=16,'ep'=8] {'rep','ep'}, use_global_device_ids=true, to_apply=%add.6 | all-reduce | flops 2560 | bytes 10240
  82.7 238.5 %all-gather.25.cloned.1.call-done = bf16[128,10,1280]{2,1,0:T(8,128)(2,1)} async-done(((bf16[1,10,1280]{2,1,0:T(8,128)(2,1)}), bf16[128,10,1280]{2,1,0:T(8,128)(2,1)}) %all-gather.25.cloned.1.call-update) | async-done | bytes 3276816 | tf_op jit(solution)/shard_map/all_gather | solution.py:101
  332.1 300.2 %all-gather.27.cloned.1.call-done = bf16[128,10,1280]{2,1,0:T(8,128)(2,1)} async-done(((bf16[1,10,1280]{2,1,0:T(8,128)(2,1)}), bf16[128,10,1280]{2,1,0:T(8,128)(2,1)}) %all-gather.27.cloned.1.call-update) | async-done | bytes 3276816 | tf_op jit(solution)/shard_map/all_gather | solution.py:102
  645.3 299.6 %all-gather.23.cloned.1.call-done = bf16[128,10,1280]{2,1,0:T(8,128)(2,1)} async-done(((bf16[1,10,1280]{2,1,0:T(8,128)(2,1)}), bf16[128,10,1280]{2,1,0:T(8,128)(2,1)}) %all-gather.23.cloned.1.call-update) | async-done | bytes 3276816 | tf_op jit(solution)/shard_map/all_gather | solution.py:103
  957.4 20.1 all-gather.1
  986.1 269.7 %all-gather.29.cloned.1.call-done = bf16[128,10,1280]{2,1,0:T(8,128)(2,1)} async-done(((bf16[1,10,1280]{2,1,0:T(8,128)(2,1)}), bf16[128,10,1280]{2,1,0:T(8,128)(2,1)}) %all-gather.29.cloned.1.call-update) | async-done | bytes 3276816 | tf_op jit(solution)/shard_map/all_gather | solution.py:104
  1262.8 54.3 %all-gather.21.cloned.1.call-done = bf16[1024,10,128]{2,0,1:T(8,128)(2,1)} async-done(((bf16[128,10,128]{2,0,1:T(8,128)(2,1)}), bf16[1024,10,128]{2,0,1:T(8,128)(2,1)}) %all-gather.21.cloned.1.call-update) | async-done | bytes 2621456 | tf_op jit(solution)/shard_map/all_gather | solution.py:120
  1323.4 57.5 %all-gather.19.cloned.1.call-done = bf16[1024,10,128]{0,2,1:T(8,128)(2,1)} async-done(((bf16[128,10,128]{0,2,1:T(8,128)(2,1)}), bf16[1024,10,128]{0,2,1:T(8,128)(2,1)}) %all-gather.19.cloned.1.call-update) | async-done | bytes 2621456 | tf_op jit(solution)/shard_map/all_gather | solution.py:121
  1406.5 339.7 %all-gather.8 = bf16[128,10,16]{2,1,0:T(8,128)(2,1)S(1)} all-gather(bf16[1,10,16]{2,1,0:T(8,128)(2,1)S(1)} %bitcast.213), channel_id=1, replica_groups=mesh['rep'=16,'ep'=8] {'rep','ep'}, dimensions={0}, use_global_device_ids=true | all-gather | bytes 41280 | tf_op jit(solution)/shard_map/all_gather | solution.py:105
  1768.2 9.7 fusion.16
  1785.4 24.7 all-to-all-done.2
  1810.1 11.3 fusion.6
  1851.2 30.0 all-to-all-done.1
  1892.6 279.1 %all-gather.33.cloned.1.call-done = bf16[128,10,896]{2,1,0:T(8,128)(2,1)} async-done(((bf16[1,10,896]{2,1,0:T(8,128)(2,1)}), bf16[128,10,896]{2,1,0:T(8,128)(2,1)}) %all-gather.33.cloned.1.call-update) | async-done | bytes 2293776 | tf_op jit(solution)/shard_map/all_gather | solution.py:107
  2175.5 318.9 %all-gather.35.cloned.1.call-done = bf16[128,7,1280]{2,1,0:T(8,128)(2,1)} async-done(((bf16[1,7,1280]{2,1,0:T(8,128)(2,1)}), bf16[128,7,1280]{2,1,0:T(8,128)(2,1)}) %all-gather.35.cloned.1.call-update) | async-done | bytes 2293776 | tf_op jit(solution)/shard_map/all_gather | solution.py:108
  2503.8 8.9 gather_fusion.1
  2517.3 8.8 gather_fusion.3
  2541.9 46.9 %scatter_fusion = f32[128,16]{0,1:T(8,128)S(1)} fusion(f32[128,16]{0,1:T(8,128)S(1)} %broadcast_in_dim.52, s32[896]{0:T(1024)S(1)} %reshape.395, f32[896]{0:T(1024)S(1)} %reshape.397), kind=kCustom, calls=%fused_computation.6 | custom fusion | flops 896 | bytes 17920 | tf_op jit(solution)/shard_map/transpose(jvp(jit(take_along_axis)))/scatter-add | solution.py:42
  2601.9 11.7 fusion.47
  2623.5 8.8 bitcast_convert_fusion
  2632.3 8.0 bitcast_convert_fusion.2
  2640.3 7.9 bitcast_convert_fusion.1
  2656.5 11.6 fusion.83
  2672.0 18.7 reduce-scatter.7.cloned.1.call-done
  2703.1 68.2 %reduce-scatter.9.cloned.1.call-done = bf16[128,1280]{1,0:T(8,128)(2,1)} async-done(((bf16[1024,1280]{1,0:T(8,128)(2,1)}), bf16[128,1280]{1,0:T(8,128)(2,1)}) %reduce-scatter.9.cloned.1.call-update) | async-done | bytes 327696 | tf_op jit(solution)/shard_map/reshape | solution.py:299
  2780.1 422.7 %fusion = f32[8,1280]{1,0:T(8,128)S(1)} fusion(f32[896,1280]{1,0:T(8,128)} %fusion.101), kind=kCustom, calls=%all-reduce-scatter | all-reduce-scatter fusion | flops 1310721 | bytes 4628480
  3202.8 7.9 collective-permute-start.15
  3216.0 7.5 collective-permute-start.12
  3267.2 24.4 concatenate.24
  3300.5 63.9 %all-reduce.19 = (f32[1280]{0:T(1024)S(1)}, f32[1280]{0:T(1024)S(1)}) all-reduce(f32[1280]{0:T(1024)S(1)} %get-tuple-element.19, f32[1280]{0:T(1024)S(1)} %get-tuple-element.17), channel_id=12, replica_groups=mesh['rep'=16,'ep'=8] {'rep','ep'}, use_global_device_ids=true, to_apply=%region_29.30.clone | all-reduce | flops 2560 | bytes 20480
  3366.6 8.1 convert_element_type.209
  3383.3 105.0 %all-reduce.26.cloned.1.call-done = (f32[1280,1280]{1,0:T(8,128)}, f32[1280,1280]{1,0:T(8,128)}, f32[1280,1280]{1,0:T(8,128)}, f32[1280,1280]{1,0:T(8,128)}, f32...) async-done(((f32[1280,1280]{1,0:T(8,128)}, f32[1280,1280]{1,0:T(8,128)}, f32[1280,1280]{1,0:T(8,128)}, f32[1280,1280]{1,0:T(8,128)}, f32[1280,16]{1,0:T(8,128)}, ...) | async-done | bytes 35471376
  (354 shorter events, 328.2 us)
Async XLA Ops:
  7.2 314.0 %all-gather.25.cloned.1.call-start = ((), (), s32[]{:S(2)}) async-start(), calls=%async_computation.10 | async-start | bytes 5283840 | tf_op jit(solution)/shard_map/all_gather | solution.py:101
  7.9 624.4 %all-gather.27.cloned.1.call-start = ((), (), s32[]{:S(2)}) async-start(), calls=%async_computation.11 | async-start | bytes 5283840 | tf_op jit(solution)/shard_map/all_gather | solution.py:102
  8.7 936.2 %all-gather.23.cloned.1.call-start = ((), (), s32[]{:S(2)}) async-start(), calls=%async_computation.9 | async-start | bytes 5283840 | tf_op jit(solution)/shard_map/all_gather | solution.py:103
  9.4 1246.4 %all-gather.29.cloned.1.call-start = ((), (), s32[]{:S(2)}) async-start(), calls=%async_computation.12 | async-start | bytes 5283840 | tf_op jit(solution)/shard_map/all_gather | solution.py:104
  10.0 1307.2 %all-gather.21.cloned.1.call-start = ((), (), s32[]{:S(2)}) async-start(), calls=%async_computation.7 | async-start | bytes 2949120 | tf_op jit(solution)/shard_map/all_gather | solution.py:120
  645.2 735.6 %all-gather.19.cloned.1.call-start = ((), (), s32[]{:S(2)}) async-start(), calls=%async_computation.6 | async-start | bytes 2949120 | tf_op jit(solution)/shard_map/all_gather | solution.py:121
  955.4 931.8 %all-gather.31.cloned.1.call-start = ((), (), s32[]{:S(2)}) async-start(), calls=%async_computation.13 | async-start | bytes 3698688 | tf_op jit(solution)/shard_map/all_gather | solution.py:106
  1393.9 368.9 %all-to-all-start = ((bf16[8,2,88,1280]{3,2,1,0:T(8,128)(2,1)}), bf16[8,2,88,1280]{3,2,1,0:T(8,128)(2,1)}, u32[]{:S(2)}, u32[]{:S(2)}) async-start(bf16[8,2,88,1280]{3,2,1,0:T(8,128)(2,1)} %bitcast.189), calls=%async_computation | async-start | bytes 7208960 | tf_op jit(solution)/shard_map/all_to_all | solution.py:172
  1762.8 47.3 %all-to-all-start.2 = ((bf16[8,2,88,1280]{3,2,1,0:T(8,128)(2,1)}), bf16[8,2,88,1280]{3,2,1,0:T(8,128)(2,1)}, u32[]{:S(2)}, u32[]{:S(2)}) async-start(bf16[8,2,88,1280]{3,2,1,0:T(8,128)(2,1)} %bitcast.190), calls=%async_computation.2 | async-start | bytes 7208960 | tf_op jit(solution)/shard_map/all_to_all | solution.py:197
  1767.4 404.2 %all-gather.33.cloned.1.call-start = ((), (), s32[]{:S(2)}) async-start(), calls=%async_computation.14 | async-start | bytes 3698688 | tf_op jit(solution)/shard_map/all_gather | solution.py:107
  1830.9 50.4 %all-to-all-start.1 = ((bf16[8,2,88,1280]{3,2,1,0:T(8,128)(2,1)}), bf16[8,2,88,1280]{3,2,1,0:T(8,128)(2,1)}, u32[]{:S(2)}, u32[]{:S(2)}) async-start(bf16[8,2,88,1280]{3,2,1,0:T(8,128)(2,1)} %copy.195), calls=%async_computation.1 | async-start | bytes 7208960 | tf_op jit(solution)/shard_map/all_to_all | solution.py:183
  1835.5 659.0 %all-gather.35.cloned.1.call-start = ((), (), s32[]{:S(2)}) async-start(), calls=%async_computation.15 | async-start | bytes 2641920 | tf_op jit(solution)/shard_map/all_gather | solution.py:108
  1881.3 636.1 %all-to-all-start.3 = ((bf16[8,2,88,1280]{3,2,1,0:T(8,128)(2,1)}), bf16[8,2,88,1280]{3,2,1,0:T(8,128)(2,1)}, u32[]{:S(2)}, u32[]{:S(2)}) async-start(bf16[8,2,88,1280]{3,2,1,0:T(8,128)(2,1)} %copy.198), calls=%async_computation.3 | async-start | bytes 7208960 | tf_op jit(solution)/shard_map/all_to_all | solution.py:218
  1885.8 804.9 %reduce-scatter.7.cloned.1.call-start = ((), (), s32[]{:S(2)}) async-start(), calls=%async_computation.8 | async-start | bytes 2949120 | tf_op jit(solution)/shard_map/reduce_scatter | solution.py:285
  2613.7 157.7 %reduce-scatter.9.cloned.1.call-start = ((), (), s32[]{:S(2)}) async-start(), calls=%async_computation.16 | async-start | bytes 2949120 | tf_op jit(solution)/shard_map/reshape | solution.py:299
  2623.4 743.2 %all-reduce.28.cloned.1.call-start = ((), (), s32[]{:S(2)}) async-start(), calls=%async_computation.18 | async-start | bytes 27525120 | tf_op jit(solution)/shard_map/psum | solution.py:225
  2648.3 840.1 %all-reduce.26.cloned.1.call-start = ((), (), s32[]{:S(2)}) async-start(), calls=%async_computation.17 | async-start | bytes 72089600
  3202.8 23.8 collective-permute-start.15
  3210.7 17.2 collective-permute-start.14
  3213.8 17.8 collective-permute-start.13
  3216.0 20.6 collective-permute-start.12
  3223.5 15.0 collective-permute-start.11
  3226.6 15.7 collective-permute-start.10
  3227.9 16.3 collective-permute-start.9
  3231.6 17.4 collective-permute-start.8
  3236.6 15.6 collective-permute-start.7
  3238.5 15.7 collective-permute-start.6
  3242.3 15.5 collective-permute-start.5
  3244.2 17.5 collective-permute-start.4
  3249.0 12.6 collective-permute-start.3
  3252.2 9.9 collective-permute-start.2
  3257.8 9.4 collective-permute-start
  (72 other events, 6872.1 us)
Sparse Core Ops, SparseCore 0:
  9.7 311.3 all-gather.24
  322.8 309.4 all-gather.26
  634.0 310.8 all-gather.22
  946.4 309.3 all-gather.28
  1258.6 58.5 all-gather.20
  1319.7 61.0 all-gather.18
  1382.5 335.7 all-gather.30
  1770.0 401.5 all-gather.32
  2173.3 321.1 all-gather.34
  2613.8 76.8 reduce-scatter.6
  2694.5 76.7 reduce-scatter.8
  2774.5 398.6 all-reduce.27
  3179.6 308.6 all-reduce.25
where the time goes:
time: 3520 us; the launch traced here: 3510 us
  waiting for transfers between devices  2070 us (59%)
  blocking collectives  915 us (26%)
  matrix products  170 us (5%)
  local copies, waits for them, and re-layouts  161 us (5%)
  other arithmetic  90.8 us (3%)
  starting transfers between devices  78.2 us (2%)
    unnamed x3, blocking collectives  555 us
    all_gather x1, blocking collectives, body(): lax.all_gather(w_router, ('rep', 'ep'), axis=0, tiled=True)  340 us
    all_gather x1, waiting for transfers between devices, body(): lax.all_gather(shared_down, ('rep', 'ep'), axis=0, tiled=True)  319 us
    all_gather x1, waiting for transfers between devices, body(): lax.all_gather(w_key, ('rep', 'ep'), axis=0, tiled=True)  300 us
    all_gather x1, waiting for transfers between devices, body(): lax.all_gather(w_value, ('rep', 'ep'), axis=0, tiled=True)  300 us
    all_gather x1, waiting for transfers between devices, body(): lax.all_gather(shared_up, ('rep', 'ep'), axis=0, tiled=True)  279 us
    all_gather x1, waiting for transfers between devices, body(): lax.all_gather(w_output, ('rep', 'ep'), axis=0, tiled=True)  270 us
    all_gather x1, waiting for transfers between devices, body(): lax.all_gather(w_query, ('rep', 'ep'), axis=0, tiled=True)  238 us
  transfers between devices with their start and end apart: 33, of which 15 were waited for; matrix products, arithmetic and copies ran while one was open for 21% of the time, Pallas kernels for 0%

commit v1 on v0

v1 whole, which is shorter than its diff:
```python
import functools
import itertools

import jax
import jax.numpy as jnp
from jax import lax
from jax.experimental import pallas as pl
from jax.experimental.pallas import tpu as pltpu
from jax.sharding import PartitionSpec as P

HD = 128
EPS = 1e-6
BF = jnp.bfloat16
F32 = jnp.float32
MESH = pl.DeviceIdType.MESH
HIGH = lax.Precision.HIGHEST
HEADS_DEV = 2
EXTRA = 128
ROW_PAD = 16
VMEM_LIMIT = 60 << 20


def dot(a, b):
    return jnp.dot(a, b, preferred_element_type=F32)


def dot_nt(a, b):
    return lax.dot_general(a, b, (((1,), (1,)), ((), ())), preferred_element_type=F32)


def dot_tn(a, b):
    return lax.dot_general(a, b, (((0,), (0,)), ((), ())), preferred_element_type=F32)


class Place:
    def __init__(self):
        self.rep = lax.axis_index("rep")
        self.ep = lax.axis_index("ep")
        self.y = self.rep // 4
        self.zl = (self.rep // 2) % 2
        self.core = self.rep % 2
        self.x = self.ep // 2
        self.zh = self.ep % 2

    def rep_at(self, y, zl, core):
        return (y % 4) * 4 + zl * 2 + core

    def ep_at(self, x, zh):
        return (x % 4) * 2 + zh

    def to_x(self, step):
        return (self.rep, self.ep_at(self.x + step, self.zh))

    def to_zh(self):
        return (self.rep, self.ep_at(self.x, 1 - self.zh))

    def to_ep(self, shift):
        return (self.rep, (self.ep + shift) % 8)

    def to_y(self, step):
        return (self.rep_at(self.y + step, self.zl, self.core), self.ep)

    def to_zl(self):
        return (self.rep_at(self.y, 1 - self.zl, self.core), self.ep)

    def to_core(self):
        return (self.rep_at(self.y, self.zl, 1 - self.core), self.ep)


class Copies:
    def __init__(self, send_sem, recv_sem):
        self.send_sem, self.recv_sem = send_sem, recv_sem
        self.number = itertools.count()
        self.sent, self.open = [], []

    def send(self, src, dst, device):
        i = next(self.number)
        copy = pltpu.make_async_remote_copy(
            src_ref=src,
            dst_ref=dst,
            send_sem=self.send_sem.at[i],
            recv_sem=self.recv_sem.at[i],
            device_id=device,
            device_id_type=MESH,
        )
        copy.start()
        self.sent.append(copy)
        self.open.append(copy)
        return copy

    def local(self, src, dst):
        i = next(self.number)
        copy = pltpu.make_async_copy(src, dst, self.recv_sem.at[i])
        copy.start()
        self.open.append(copy)
        return copy

    def arrived(self, copy):
        if any(copy is c for c in self.sent):
            copy.wait_recv()
        else:
            copy.wait()
        self.open = [c for c in self.open if c is not copy]

    def sent_off(self, copy):
        copy.wait_send()
        self.sent = [c for c in self.sent if c is not copy]

    def finish(self):
        for copy in list(self.open):
            self.arrived(copy)
        for copy in self.sent:
            copy.wait_send()


def greet(devices):
    barrier = pltpu.get_barrier_semaphore()
    for device in devices:
        pl.semaphore_signal(barrier, inc=1, device_id=device, device_id_type=MESH)
    pl.semaphore_wait(barrier, len(devices))


def run_streams(*streams):
    live = list(streams)
    while live:
        for stream in list(live):
            try:
                next(stream)
            except StopIteration:
                live.remove(stream)


def half_columns(columns):
    return (columns // 128 + 1) // 2 * 128


def ep_peers(place):
    return [place.to_ep(k) for k in range(1, 8)]


def rep_peers(place):
    return [place.to_y(1), place.to_y(-1), place.to_zl(), place.to_core()]


def gather_ep(cp, place, src, dst, columns):
    cut = half_columns(columns)
    lo, hi = pl.ds(0, cut), pl.ds(cut, columns - cut)
    mine = place.ep
    own = cp.local(src, dst.at[mine])
    right = cp.send(src, dst.at[mine], place.to_x(1))
    left = cp.send(src, dst.at[mine], place.to_x(-1))
    over = cp.send(src, dst.at[mine], place.to_zh())
    yield
    from_left = place.ep_at(place.x - 1, place.zh)
    from_right = place.ep_at(place.x + 1, place.zh)
    from_over = place.ep_at(place.x, 1 - place.zh)
    far = place.ep_at(place.x + 2, place.zh)
    cp.arrived(right)
    half_a = cp.send(dst.at[from_left, :, lo], dst.at[from_left, :, lo], place.to_x(1))
    cp.arrived(left)
    half_b = cp.send(dst.at[from_right, :, hi], dst.at[from_right, :, hi], place.to_x(-1))
    yield
    cp.arrived(over)
    cp.send(dst.at[from_over], dst.at[from_over], place.to_x(1))
    cp.send(dst.at[from_over], dst.at[from_over], place.to_x(-1))
    yield
    cp.arrived(half_a)
    cp.arrived(half_b)
    cp.send(dst.at[far], dst.at[far], place.to_zh())
    yield
    cp.arrived(own)


def gather_ring_y(cp, place, src, dst, columns, slot):
    cut = half_columns(columns)
    lo, hi = pl.ds(0, cut), pl.ds(cut, columns - cut)
    up = cp.send(src, dst.at[slot(place.y)], place.to_y(1))
    down = cp.send(src, dst.at[slot(place.y)], place.to_y(-1))
    yield
    cp.arrived(up)
    below = slot(place.y - 1)
    half_a = cp.send(dst.at[below, :, lo], dst.at[below, :, lo], place.to_y(1))
    cp.arrived(down)
    above = slot(place.y + 1)
    half_b = cp.send(dst.at[above, :, hi], dst.at[above, :, hi], place.to_y(-1))
    yield
    cp.arrived(half_a)
    cp.arrived(half_b)


def gather_rep(cp, place, src, dst, columns, z_first):
    mine = place.rep
    own = cp.local(src, dst.at[mine])
    cp.send(src, dst.at[mine], place.to_core())

    def slot(zl):
        return lambda y: place.rep_at(y, zl, place.core)

    def pass_core(index):
        cp.send(dst.at[index], dst.at[index], place.to_core())

    here, there = slot(place.zl), slot(1 - place.zl)
    if z_first:
        over = cp.send(src, dst.at[mine], place.to_zl())
        first = gather_ring_y(cp, place, src, dst, columns, here)
        next(first)
        yield
        cp.arrived(over)
        second = gather_ring_y(
            cp, place, dst.at[there(place.y)], dst, columns, there
        )
        next(second)
        pass_core(there(place.y))
        yield
        next(first)
        for k in (-1, 1):
            pass_core(here(place.y + k))
        yield
        next(second)
        for k in (-1, 1):
            pass_core(there(place.y + k))
        yield
        next(first, None)
        pass_core(here(place.y + 2))
        yield
        next(second, None)
        pass_core(there(place.y + 2))
    else:
        over = [cp.send(src, dst.at[mine], place.to_zl())]
        ring = gather_ring_y(cp, place, src, dst, columns, here)
        next(ring)
        yield
        next(ring)
        for k in (-1, 1):
            block = dst.at[here(place.y + k)]
            over.append(cp.send(block, block, place.to_zl()))
            pass_core(here(place.y + k))
        yield
        next(ring, None)
        block = dst.at[here(place.y + 2)]
        over.append(cp.send(block, block, place.to_zl()))
        pass_core(here(place.y + 2))
        yield
        for copy, k in zip(over, (0, -1, 1, 2)):
            cp.arrived(copy)
            pass_core(there(place.y + k))
            yield
    cp.arrived(own)


def spread_matrix(rows, blocks, used):
    shape = (rows, blocks * ROW_PAD)
    to = lax.broadcasted_iota(jnp.int32, shape, 0)
    at = lax.broadcasted_iota(jnp.int32, shape, 1)
    return jnp.where((at // ROW_PAD) * used + at % ROW_PAD == to, 1.0, 0.0) * jnp.where(
        at % ROW_PAD < used, 1.0, 0.0
    )


def kernel_a(
    slices, whole, down, tok, cot,
    tok_all, cot_all, w_slices, w_whole, w_down,
    land_slices, land_whole, pack_slices, pack_whole, send_sem, recv_sem,
):
    place = Place()
    cp = Copies(send_sem, recv_sem)
    greet(ep_peers(place) + rep_peers(place))
    first = []
    mine = place.ep
    first.append(cp.local(slices.at[mine], land_slices.at[mine]))
    first.append(cp.local(whole, land_whole.at[mine]))
    for k in range(1, 8):
        first.append(cp.send(slices.at[(mine + k) % 8], land_slices.at[mine], place.to_ep(k)))
        first.append(cp.send(whole, land_whole.at[mine], place.to_ep(k)))
    tok_stream = gather_ep(cp, place, tok, tok_all, tok.shape[1])
    next(tok_stream)
    down_stream = gather_rep(cp, place, down, w_down, down.shape[1], True)
    next(down_stream)
    for copy in first:
        cp.arrived(copy)
    used = pack_slices.shape[0] // 8
    spread = spread_matrix(8 * used, 8, used).astype(BF)
    for land, pack in ((land_slices, pack_slices), (land_whole, pack_whole)):
        columns = land.shape[2]
        step = 128
        for c in range(0, columns, step):
            block = land[:, :, c : c + step].reshape(8 * ROW_PAD, step)
            pack[:, c : c + step] = dot(spread, block).astype(BF)
    slice_stream = gather_rep(cp, place, pack_slices, w_slices, slices.shape[2], False)
    next(slice_stream)
    whole_stream = gather_rep(cp, place, pack_whole, w_whole, whole.shape[1], True)
    next(whole_stream)
    cot_stream = gather_ep(cp, place, cot, cot_all, cot.shape[1])
    run_streams(tok_stream, slice_stream, whole_stream, cot_stream, down_stream)
    cp.finish()


def call_a(slices, whole, down, tok, cot, used):
    anyspace = pl.BlockSpec(memory_space=pl.ANY)
    copies = 160
    return pl.pallas_call(
        kernel_a,
        out_shape=(
            jax.ShapeDtypeStruct((8,) + tok.shape, BF),
            jax.ShapeDtypeStruct((8,) + cot.shape, BF),
            jax.ShapeDtypeStruct((16, 8 * used, slices.shape[2]), BF),
            jax.ShapeDtypeStruct((16, 8 * used, whole.shape[1]), BF),
            jax.ShapeDtypeStruct((16,) + down.shape, BF),
        ),
        in_specs=[anyspace] * 5,
        out_specs=(anyspace,) * 5,
        scratch_shapes=[
            pltpu.VMEM((8, ROW_PAD, slices.shape[2]), BF),
            pltpu.VMEM((8, ROW_PAD, whole.shape[1]), BF),
            pltpu.VMEM((8 * used, slices.shape[2]), BF),
            pltpu.VMEM((8 * used, whole.shape[1]), BF),
            pltpu.SemaphoreType.DMA((copies,)),
            pltpu.SemaphoreType.DMA((copies,)),
        ],
        compiler_params=pltpu.CompilerParams(
            collective_id=0, has_side_effects=True, vmem_limit_bytes=VMEM_LIMIT
        ),
        name="gather_inputs",
    )(slices, whole, down, tok, cot)


def kernel_b(
    heads, tok, live, w_out, gain,
    residual, attended, hidden_all,
    land, hidden, send_sem, recv_sem,
):
    place = Place()
    cp = Copies(send_sem, recv_sem)
    greet(ep_peers(place))
    rows, width = tok.shape
    mine = place.ep
    span = heads.shape[2]
    column = pl.ds(pl.multiple_of(mine * span, 128), span)
    first = [cp.local(heads.at[mine], land.at[:, column])]
    for k in range(1, 8):
        first.append(cp.send(heads.at[(mine + k) % 8], land.at[:, column], place.to_ep(k)))
    for copy in first:
        cp.arrived(copy)
    low = land[:, :width]
    attended[...] = low
    step = 256
    squares = jnp.zeros((rows, 1), F32)
    for c in range(0, width, step):
        part = tok[:, c : c + step].astype(F32) + live[...] * dot(low, w_out[:, c : c + step])
        residual[:, c : c + step] = part
        squares += jnp.sum(part * part, axis=1, keepdims=True)
    scale = lax.rsqrt(squares / width + EPS)
    hidden[...] = (residual[...] * scale * gain[...]).astype(BF)
    run_streams(gather_ep(cp, place, hidden, hidden_all, width))
    cp.finish()


def call_b(heads, tok, live, w_out, gain):
    anyspace = pl.BlockSpec(memory_space=pl.ANY)
    vmem = pl.BlockSpec(memory_space=pltpu.VMEM)
    rows, width = tok.shape
    return pl.pallas_call(
        kernel_b,
        out_shape=(
            jax.ShapeDtypeStruct((rows, width), F32),
            jax.ShapeDtypeStruct((rows, width), BF),
            jax.ShapeDtypeStruct((8, rows, width), BF),
        ),
        in_specs=[anyspace, vmem, vmem, vmem, vmem],
        out_specs=(vmem, vmem, anyspace),
        scratch_shapes=[
            pltpu.VMEM((rows, 8 * heads.shape[2]), BF),
            pltpu.VMEM((rows, width), BF),
            pltpu.SemaphoreType.DMA((32,)),
            pltpu.SemaphoreType.DMA((32,)),
        ],
        compiler_params=pltpu.CompilerParams(
            collective_id=1, has_side_effects=True, vmem_limit_bytes=VMEM_LIMIT
        ),
        name="attention_out",
    )(heads, tok, live, w_out, gain)


def add_into(out, first, others):
    lead = out.shape[:-2]
    rows = out.shape[-2]

    for index in itertools.product(*(range(n) for n in lead)):

        @pl.loop(0, rows // ROW_PAD)
        def _(i):
            at = index + (pl.ds(pl.multiple_of(i * ROW_PAD, ROW_PAD), ROW_PAD),)
            total = first[at].astype(F32)
            for other in others:
                total += other[at].astype(F32)
            out[at] = total.astype(out.dtype)


def sum_ring_y(cp, place, mine, work, near_lo, near_hi, last_up, last_down, chunk, lo, hi):
    y = place.y
    up, down = place.to_y(1), place.to_y(-1)
    a = cp.send(lo(chunk(mine, y + 2)), near_lo, up)
    b = cp.send(hi(chunk(mine, y + 2)), near_hi, down)
    c = cp.send(hi(chunk(mine, y + 1)), hi(last_up), up)
    d = cp.send(lo(chunk(mine, y - 1)), lo(last_down), down)
    yield
    cp.arrived(a)
    add_into(lo(chunk(work, y + 1)), lo(chunk(mine, y + 1)), [near_lo])
    e = cp.send(lo(chunk(work, y + 1)), lo(last_up), up)
    cp.arrived(b)
    add_into(hi(chunk(work, y - 1)), hi(chunk(mine, y - 1)), [near_hi])
    f = cp.send(hi(chunk(work, y - 1)), hi(last_down), down)
    yield
    for copy in (c, d, e, f):
        cp.arrived(copy)


def sum_rep_yz(cp, place, mine, bufs, out):
    work, near_lo, near_hi, last_up, last_down, half, over = bufs
    ring = sum_ring_y(
        cp, place, mine, work, near_lo, near_hi, last_up, last_down,
        lambda ref, y: ref.at[y % 4],
        lambda ref: ref.at[0],
        lambda ref: ref.at[1],
    )
    yield from ring
    other = 1 - place.zl
    chunk = mine.at[place.y]
    add_into(half, chunk.at[other], [last_up.at[other], last_down.at[other]])
    copy = cp.send(half, over, place.to_zl())
    yield
    cp.arrived(copy)
    add_into(
        out, chunk.at[place.zl], [last_up.at[place.zl], last_down.at[place.zl], over]
    )


def sum_bufs(rows, columns):
    return [
        pltpu.VMEM((4, 2, rows, columns), BF),
        pltpu.VMEM((rows, columns), BF),
        pltpu.VMEM((rows, columns), BF),
        pltpu.VMEM((2, rows, columns), BF),
        pltpu.VMEM((2, rows, columns), BF),
        pltpu.VMEM((rows, columns), BF),
        pltpu.VMEM((rows, columns), BF),
    ]


def kernel_c(
    grads, outs, g_gate, g_up, g_down,
    residual, cot, live, probs, w_out, w_router, gain,
    out, g_residual, g_branch, g_logits, d_gain, g_heads, s_gate, s_up, s_down,
    land_grads, land_outs, g_att, pair, bufs, send_sem, recv_sem,
):
    place = Place()
    cp = Copies(send_sem, recv_sem)
    greet(ep_peers(place) + rep_peers(place))
    rows, width = residual.shape
    mine = place.ep
    summed = ((g_gate, s_gate), (g_up, s_up), (g_down, s_down))
    core = place.core
    own_half, mate_half = [], []
    for (grad, _), (own, got) in zip(summed, pair):
        own_half.append(cp.local(grad.at[core], own))
        mate_half.append(cp.send(grad.at[1 - core], got, place.to_core()))
    first = [cp.local(grads.at[mine], land_grads.at[mine])]
    second = [cp.local(outs.at[mine], land_outs.at[mine])]
    for k in range(1, 8):
        first.append(cp.send(grads.at[(mine + k) % 8], land_grads.at[mine], place.to_ep(k)))
    for k in range(1, 8):
        second.append(cp.send(outs.at[(mine + k) % 8], land_outs.at[mine], place.to_ep(k)))
    streams = []
    for ((_, total), (own, got), buf, a, b) in zip(summed, pair, bufs, own_half, mate_half):
        cp.arrived(a)
        cp.arrived(b)
        add_into(own, own, [got])
        streams.append(sum_rep_yz(cp, place, own, buf, total))
        next(streams[-1])
    for copy in first:
        cp.arrived(copy)

    def total_of(land, c, n):
        total = land[0, :, c : c + n].astype(F32)
        for i in range(1, 8):
            total += land[i, :, c : c + n].astype(F32)
        return total

    alive = live[...]
    router_grad = total_of(land_grads, width, EXTRA) * alive
    prob = probs[...]
    logit_grad = prob * (router_grad - jnp.sum(prob * router_grad, axis=1, keepdims=True))
    g_logits[...] = logit_grad
    step = 256
    squares = jnp.zeros((rows, 1), F32)
    mean_k = jnp.zeros((rows, 1), F32)
    for c in range(0, width, step):
        part = residual[:, c : c + step]
        squares += jnp.sum(part * part, axis=1, keepdims=True)
    scale = lax.rsqrt(squares / width + EPS)
    for c in range(0, width, step):
        k = total_of(land_grads, c, step) + lax.dot_general(
            logit_grad, w_router[c : c + step, :].astype(F32), (((1,), (1,)), ((), ())),
            preferred_element_type=F32, precision=HIGH,
        )
        normed = residual[:, c : c + step] * scale
        d_gain[:, c : c + step] = jnp.sum(k * normed, axis=0, keepdims=True)
        k = k * gain[:, c : c + step]
        mean_k += jnp.sum(k * normed, axis=1, keepdims=True)
        g_residual[:, c : c + step] = k
    mean_k = mean_k / width
    for c in range(0, width, step):
        normed = residual[:, c : c + step] * scale
        grad = cot[:, c : c + step].astype(F32) + scale * (
            g_residual[:, c : c + step] - normed * mean_k
        )
        g_residual[:, c : c + step] = grad
        g_branch[:, c : c + step] = (alive * grad).astype(BF)
    g_att[...] = jnp.zeros_like(g_att)
    low = g_branch[...]
    for c in range(0, width, step):
        g_att[c // step] = dot_nt(low, w_out[c : c + step, :]).astype(BF)
    third = [cp.local(g_att.at[mine], g_heads.at[mine])]
    for k in range(1, 8):
        third.append(cp.send(g_att.at[(mine + k) % 8], g_heads.at[mine], place.to_ep(k)))
    run_streams(*streams)
    for copy in second:
        cp.arrived(copy)
    for c in range(0, width, step):
        out[:, c : c + step] = (
            residual[:, c : c + step] + total_of(land_outs, c, step)
        ).astype(BF)
    cp.finish()


def call_c(grads, outs, g_gate, g_up, g_down, residual, cot, live, probs, w_out, w_router, gain):
    anyspace = pl.BlockSpec(memory_space=pl.ANY)
    vmem = pl.BlockSpec(memory_space=pltpu.VMEM)
    rows, width = residual.shape
    summed = [g.shape for g in (g_gate, g_up, g_down)]
    small = [s[3:] for s in summed]
    return pl.pallas_call(
        kernel_c,
        out_shape=(
            jax.ShapeDtypeStruct((rows, width), BF),
            jax.ShapeDtypeStruct((rows, width), F32),
            jax.ShapeDtypeStruct((rows, width), BF),
            jax.ShapeDtypeStruct((rows, EXTRA), F32),
            jax.ShapeDtypeStruct((1, width), F32),
            jax.ShapeDtypeStruct((8, rows, HEADS_DEV * HD), BF),
        )
        + tuple(jax.ShapeDtypeStruct(s, BF) for s in small),
        in_specs=[anyspace] * 5 + [vmem] * 7,
        out_specs=(vmem,) * 5 + (anyspace,) + (vmem,) * 3,
        scratch_shapes=[
            pltpu.VMEM((8, rows, grads.shape[2]), BF),
            pltpu.VMEM((8, rows, width), BF),
            pltpu.VMEM((8, rows, HEADS_DEV * HD), BF),
            [[pltpu.VMEM(s[1:], BF)] * 2 for s in summed],
            [sum_bufs(*s) for s in small],
            pltpu.SemaphoreType.DMA((80,)),
            pltpu.SemaphoreType.DMA((80,)),
        ],
        compiler_params=pltpu.CompilerParams(
            collective_id=2, has_side_effects=True, vmem_limit_bytes=VMEM_LIMIT
        ),
        name="sum_hidden_two",
    )(grads, outs, g_gate, g_up, g_down, residual, cot, live, probs, w_out, w_router, gain)


def gather_expert(cp, place, src, dst):
    core, y, zl = place.core, place.y, place.zl
    columns = src.shape[1]
    cut = half_columns(columns)
    lo, hi = pl.ds(0, cut), pl.ds(cut, columns - cut)
    at = lambda k, z: dst.at[core, (y + k) % 4, z]
    own = cp.local(src, at(0, zl))
    over = cp.send(src, at(0, zl), place.to_zl())
    ups = {zl_: None for zl_ in (0, 1)}
    cp.send(src, at(0, zl), place.to_core())
    first = (
        cp.send(src, at(0, zl), place.to_y(1)),
        cp.send(src, at(0, zl), place.to_y(-1)),
    )
    yield
    cp.arrived(over)
    other = 1 - zl
    second = (
        cp.send(at(0, other), at(0, other), place.to_y(1)),
        cp.send(at(0, other), at(0, other), place.to_y(-1)),
    )
    cp.send(at(0, other), at(0, other), place.to_core())
    yield
    halves = []
    for (up, down), z in ((first, zl), (second, other)):
        cp.arrived(up)
        a = cp.send(at(-1, z).at[:, lo], at(-1, z).at[:, lo], place.to_y(1))
        cp.send(at(-1, z), at(-1, z), place.to_core())
        cp.arrived(down)
        b = cp.send(at(1, z).at[:, hi], at(1, z).at[:, hi], place.to_y(-1))
        cp.send(at(1, z), at(1, z), place.to_core())
        halves.append((a, b))
        yield
    for (a, b), z in zip(halves, (zl, other)):
        cp.arrived(a)
        cp.arrived(b)
        cp.send(at(2, z), at(2, z), place.to_core())
        yield
    cp.arrived(own)


def sum_rep_dense(cp, place, mine, mate, bufs, out):
    add_into(mine, mine, [mate])
    yield from sum_rep_yz(cp, place, mine, bufs, out)


def kernel_d(
    grads, s_gate, s_up, s_down, d_slices, d_whole, d_down,
    g_hidden, e_gate, e_up, e_down, o_slices, o_whole, o_down,
    land, pair, bufs, totals, wide, send_sem, recv_sem,
):
    place = Place()
    cp = Copies(send_sem, recv_sem)
    greet(ep_peers(place) + rep_peers(place))
    mine = place.ep
    core = place.core
    first = [cp.local(grads.at[mine], land.at[mine])]
    for k in range(1, 8):
        first.append(cp.send(grads.at[(mine + k) % 8], land.at[mine], place.to_ep(k)))
    streams = []
    parts = (d_slices, d_whole, d_down)
    started = []
    for grad, (own, got) in zip(parts, pair):
        started.append(
            (
                cp.local(grad.at[:, :, core], own),
                cp.send(grad.at[:, :, 1 - core], got, place.to_core()),
            )
        )
    for (own, got), (a, b), buf, total in zip(pair, started, bufs, totals):
        cp.arrived(a)
        cp.arrived(b)
        streams.append(sum_rep_dense(cp, place, own, got, buf, total))
        next(streams[-1])
    experts = [
        gather_expert(cp, place, s, e)
        for s, e in ((s_gate, e_gate), (s_up, e_up), (s_down, e_down))
    ]
    for stream in experts:
        next(stream)
    run_streams(*streams, *experts)
    used = totals[0].shape[0] // 8
    spread = spread_matrix(8 * used, 8, used).astype(BF)
    for total, padded in zip(totals, wide):
        columns = total.shape[1]
        for c in range(0, columns, 128):
            padded[:, :, c : c + 128] = (
                dot_tn(spread, total[:, c : c + 128]).astype(BF).reshape(8, ROW_PAD, 128)
            )
    for padded, result in zip(wide, (o_slices, o_whole)):
        cp.local(padded.at[mine], result.at[mine])
        for k in range(1, 8):
            cp.send(padded.at[(mine + k) % 8], result.at[mine], place.to_ep(k))
    o_down[...] = totals[2][...]
    for copy in first:
        cp.arrived(copy)
    width = g_hidden.shape[1]
    for c in range(0, width, 256):
        total = land[0, :, c : c + 256].astype(F32)
        for i in range(1, 8):
            total += land[i, :, c : c + 256].astype(F32)
        g_hidden[:, c : c + 256] = total
    cp.finish()


def call_d(grads, s_gate, s_up, s_down, d_slices, d_whole, d_down):
    anyspace = pl.BlockSpec(memory_space=pl.ANY)
    vmem = pl.BlockSpec(memory_space=pltpu.VMEM)
    _, rows, width = grads.shape
    parts = [g.shape for g in (d_slices, d_whole, d_down)]
    small = [s[3:] for s in parts]
    return pl.pallas_call(
        kernel_d,
        out_shape=(jax.ShapeDtypeStruct((rows, width), F32),)
        + tuple(jax.ShapeDtypeStruct((2, 4, 2) + s.shape, BF) for s in (s_gate, s_up, s_down))
        + tuple(jax.ShapeDtypeStruct((8, ROW_PAD, s[1]), BF) for s in small[:2])
        + (jax.ShapeDtypeStruct(small[2], BF),),
        in_specs=[anyspace] * 7,
        out_specs=(vmem,) + (anyspace,) * 5 + (vmem,),
        scratch_shapes=[
            pltpu.VMEM((8, rows, width), BF),
            [[pltpu.VMEM((4, 2) + s, BF)] * 2 for s in small],
            [sum_bufs(*s) for s in small],
            [pltpu.VMEM(s, BF) for s in small],
            [pltpu.VMEM((8, ROW_PAD, s[1]), BF) for s in small[:2]],
            pltpu.SemaphoreType.DMA((140,)),
            pltpu.SemaphoreType.DMA((140,)),
        ],
        compiler_params=pltpu.CompilerParams(
            collective_id=3, has_side_effects=True, vmem_limit_bytes=VMEM_LIMIT
        ),
        name="sum_hidden_one",
    )(grads, s_gate, s_up, s_down, d_slices, d_whole, d_down)


def rotate(values, cosine, sine):
    half = values.shape[-1] // 2
    front, back = values[..., :half], values[..., half:]
    cos, sin = cosine[:, None, :], sine[:, None, :]
    return jnp.concatenate([front * cos - back * sin, back * cos + front * sin], axis=-1)


def norm_parts(values):
    scale = lax.rsqrt(jnp.mean(values * values, axis=-1, keepdims=True) + EPS)
    return scale, values * scale


def pad_rows(values, rows):
    return jnp.pad(values, ((0, rows - values.shape[0]),) + ((0, 0),) * (values.ndim - 1))


def body(
    tokens, cotangent, lengths, token_mask, routes,
    w_query, w_key, w_value, w_output, w_router,
    shared_gate, shared_up, shared_down, norm_attn, norm_ffn,
    expert_gate, expert_up, expert_down,
):
    rows, width = tokens.shape
    top = routes.shape[1]
    used = w_query.shape[0]
    hidden = expert_gate.shape[2]
    experts = w_router.shape[1]
    exp_dev = expert_gate.shape[0]
    ep = lax.axis_index("ep")
    group = rows * 8
    span = HEADS_DEV * HD
    owners = width // span
    down_used = shared_down.shape[0]
    shared_cols = 16 * down_used

    def by_owner(w):
        return jnp.pad(w.reshape(used, owners, span), ((0, 0), (0, 8 - owners), (0, 0)))

    def by_shared(w):
        w = w.reshape(used, 16, 8, down_used).transpose(0, 2, 1, 3).reshape(used, 8, shared_cols)
        return jnp.pad(w, ((0, 0), (0, 0), (0, 128 - shared_cols)))

    slices = jnp.concatenate(
        [by_owner(w_query), by_owner(w_key), by_owner(w_value), by_shared(shared_gate), by_shared(shared_up)],
        axis=2,
    ).transpose(1, 0, 2)
    slices = jnp.pad(slices, ((0, 0), (0, ROW_PAD - used), (0, 0)))
    whole = jnp.concatenate(
        [w_output, w_router, norm_attn[:, None], norm_ffn[:, None]], axis=1
    )
    whole = jnp.pad(whole, ((0, ROW_PAD - used), (0, width + EXTRA - whole.shape[1])))
    down = pad_rows(shared_down, ROW_PAD)
    position = ep * rows + jnp.arange(rows, dtype=jnp.int32)
    live_own = ((position < lengths[0]) & (token_mask == 1)).astype(F32)
    tok_wide = jnp.concatenate(
        [
            tokens,
            jnp.pad(
                jnp.concatenate([routes.astype(BF), live_own[:, None].astype(BF)], axis=1),
                ((0, 0), (0, EXTRA - top - 1)),
            ),
        ],
        axis=1,
    )
    tok_all, cot_all, w_slices, w_whole, w_down = call_a(
        slices, whole, down, tok_wide, cotangent, used
    )
    tok_all = tok_all.reshape(group, width + EXTRA)
    cot_all = cot_all.reshape(group, width)
    w_slices = w_slices.reshape(width, -1)
    w_whole = w_whole.reshape(width, -1)
    w_down = jnp.pad(
        w_down[:, :down_used].reshape(shared_cols, width), ((0, 128 - shared_cols), (0, 0))
    )
    live = tok_all[:, width + top].astype(F32)
    routes_all = tok_all[:, width : width + top].astype(jnp.int32)
    gain_one = w_whole[:, width + experts].astype(F32)
    gain_two = w_whole[:, width + experts + 1].astype(F32)
    router = w_whole[:, width : width + experts]
    w_out = w_whole[:, :width]
    w_qkv = w_slices[:, : 3 * span]
    w_gate = w_slices[:, 3 * span : 3 * span + 128]
    w_up = w_slices[:, 3 * span + 128 :]

    pos = jnp.arange(group, dtype=jnp.int32)
    frequency = 10000.0 ** (-(jnp.arange(HD // 2, dtype=F32) * 2.0 / HD))
    angles = pos.astype(F32)[:, None] * frequency[None, :]
    cosine, sine = jnp.cos(angles), jnp.sin(angles)
    inputs_all = tok_all[:, :width].astype(F32)
    _, normed_one = norm_parts(inputs_all)
    hidden_one = (normed_one * gain_one).astype(BF)
    qkv = dot(hidden_one, w_qkv)
    query = rotate(qkv[:, :span].reshape(group, HEADS_DEV, HD), cosine, sine).astype(BF)
    key = rotate(qkv[:, span : 2 * span].reshape(group, HEADS_DEV, HD), cosine, sine).astype(BF)
    value = qkv[:, 2 * span :].astype(BF).reshape(group, HEADS_DEV, HD)
    allowed = (pos[None, :] <= pos[:, None]) & (
        (live[None, :] > 0.5) | (pos[None, :] == pos[:, None])
    )
    scale = HD**-0.5
    scores = jnp.einsum("qhd,khd->hqk", query, key, preferred_element_type=F32) * scale
    scores = jnp.where(allowed[None], scores, -1e30)
    top_score = jnp.max(scores, axis=-1, keepdims=True)
    exponent = jnp.exp(scores - top_score)
    probs = exponent / jnp.sum(exponent, axis=-1, keepdims=True)
    attend = jnp.einsum("hqk,khd->qhd", probs.astype(BF), value, preferred_element_type=F32)
    heads = attend.reshape(8, rows, span).astype(BF)

    live_col = live_own[:, None]
    residual, attended, hidden_all = call_b(heads, tokens, live_col, w_out, gain_two[None])
    hidden_all = hidden_all.reshape(group, width)

    logits = dot(hidden_all, router)
    router_probs = jax.nn.softmax(logits, axis=-1)
    named = jnp.any(
        routes_all[:, :, None] == jnp.arange(experts, dtype=jnp.int32)[None, None, :], axis=1
    )
    gates = jnp.where(named, router_probs, 0.0) * live[:, None]
    expert_ids = ep * exp_dev + jnp.arange(exp_dev)
    pick = (expert_ids[:, None] == jnp.arange(experts)[None, :]).astype(F32)
    weight = jnp.sum(gates[:, None, :] * pick[None], axis=2)
    routed_here = jnp.sum(named.astype(F32)[:, None, :] * pick[None], axis=2)

    def pair_back(gate, up, grad):
        sig = jax.nn.sigmoid(gate)
        silu = gate * sig
        return grad * up * (sig + silu * (1.0 - sig)), grad * silu

    gate_val = jnp.einsum("td,edf->etf", hidden_all, expert_gate, preferred_element_type=F32)
    up_val = jnp.einsum("td,edf->etf", hidden_all, expert_up, preferred_element_type=F32)
    act = jax.nn.silu(gate_val) * up_val
    raw = jnp.einsum("td,efd->etf", cot_all, expert_down, preferred_element_type=F32)
    weight_t = weight.T[:, :, None]
    wact = (act * weight_t).astype(BF)
    q_here = jnp.sum(act * raw, axis=2).T * routed_here
    g_a, g_b = pair_back(gate_val, up_val, raw * weight_t)
    g_a, g_b = g_a.astype(BF), g_b.astype(BF)
    d_eg = jnp.einsum("td,etf->edf", hidden_all, g_a, preferred_element_type=F32).astype(BF)
    d_eu = jnp.einsum("td,etf->edf", hidden_all, g_b, preferred_element_type=F32).astype(BF)
    d_ed = jnp.einsum("etf,td->efd", wact, cot_all, preferred_element_type=F32).astype(BF)

    s_gate = dot(hidden_all, w_gate)
    s_up = dot(hidden_all, w_up)
    s_act = (jax.nn.silu(s_gate) * s_up * live[:, None]).astype(BF)
    s_raw = dot_nt(cot_all, w_down) * live[:, None]
    sg_a, sg_b = pair_back(s_gate, s_up, s_raw)
    sg_a, sg_b = sg_a.astype(BF), sg_b.astype(BF)
    d_sg, d_su = dot_tn(hidden_all, sg_a), dot_tn(hidden_all, sg_b)
    d_sd = dot_tn(s_act, cot_all)

    out_part = jnp.einsum("etf,efd->td", wact, expert_down, preferred_element_type=F32) + dot(
        s_act, w_down
    )
    grad_part = (
        jnp.einsum("etf,edf->td", g_a, expert_gate, preferred_element_type=F32)
        + jnp.einsum("etf,edf->td", g_b, expert_up, preferred_element_type=F32)
        + dot_nt(sg_a, w_gate)
        + dot_nt(sg_b, w_up)
    )
    q_wide = jnp.sum(q_here[:, :, None] * pick[None], axis=1)
    grad_wide = jnp.concatenate(
        [grad_part.astype(BF), jnp.pad(q_wide.astype(BF), ((0, 0), (0, EXTRA - experts)))], axis=1
    )
    own = lambda a: lax.dynamic_slice_in_dim(a, ep * rows, rows, axis=0)
    probs_own = jnp.pad(own(router_probs), ((0, 0), (0, EXTRA - experts)))
    router_wide = jnp.pad(router, ((0, 0), (0, EXTRA - experts)))
    out, g_residual, g_branch, g_logits, d_gain_two, g_heads, sum_gate, sum_up, sum_down = call_c(
        grad_wide.reshape(8, rows, width + EXTRA),
        out_part.astype(BF).reshape(8, rows, width),
        d_eg.reshape(exp_dev, 4, 2, width // 8, hidden),
        d_eu.reshape(exp_dev, 4, 2, width // 8, hidden),
        d_ed.reshape(exp_dev, 4, 2, hidden // 8, width),
        residual, cotangent, live_col, probs_own, w_out, router_wide, gain_two[None],
    )

    g_att = g_heads.reshape(group, HEADS_DEV, HD)
    g_values = jnp.einsum("hqk,qhd->khd", probs.astype(BF), g_att, preferred_element_type=F32)
    g_probs = jnp.einsum("qhd,khd->hqk", g_att, value, preferred_element_type=F32)
    delta = jnp.sum(probs * g_probs, axis=-1, keepdims=True)
    g_scores = (probs * (g_probs - delta)).astype(BF)
    g_query = jnp.einsum("hqk,khd->qhd", g_scores, key, preferred_element_type=F32) * scale
    g_key = jnp.einsum("hqk,qhd->khd", g_scores, query, preferred_element_type=F32) * scale
    g_qkv = jnp.concatenate(
        [
            rotate(g_query, cosine, -sine).reshape(group, span),
            rotate(g_key, cosine, -sine).reshape(group, span),
            g_values.reshape(group, span),
        ],
        axis=1,
    ).astype(BF)
    d_qkv = dot_tn(hidden_one, g_qkv)
    g_hidden_part = dot_nt(g_qkv, w_qkv)
    d_gain_one = jnp.sum(g_hidden_part * normed_one, axis=0)
    hidden_own = own(hidden_all)
    d_router = lax.dot_general(
        hidden_own.astype(F32), g_logits, (((0,), (0,)), ((), ())),
        preferred_element_type=F32, precision=HIGH,
    )[:, :experts]
    d_out = dot_tn(attended, g_branch)
    d_slices = jnp.concatenate([d_qkv, d_sg, d_su], axis=1).astype(BF)
    d_whole = jnp.concatenate(
        [
            d_out,
            d_router,
            d_gain_one[:, None],
            d_gain_two.reshape(width, 1),
            jnp.zeros((width, EXTRA - experts - 2), F32),
        ],
        axis=1,
    ).astype(BF)
    d_down = jnp.pad(
        d_sd[:shared_cols].reshape(16, down_used, width), ((0, 0), (0, ROW_PAD - down_used), (0, 0))
    ).astype(BF)
    split = lambda a: a.reshape((4, 2, 2, -1, a.shape[-1]))
    g_hidden, e_gate, e_up, e_down, o_slices, o_whole, o_down = call_d(
        g_hidden_part.astype(BF).reshape(8, rows, width),
        sum_gate, sum_up, sum_down,
        split(d_slices), split(d_whole), split(d_down),
    )
    inputs = tokens.astype(F32)
    scale_one, normed_own = norm_parts(inputs)
    k = g_hidden * gain_one
    d_tokens = g_residual + scale_one * (
        k - normed_own * jnp.mean(k * normed_own, axis=-1, keepdims=True)
    )
    o_slices = o_slices[:, :used].astype(F32)
    o_whole = jnp.sum(o_whole[:, :used].astype(F32), axis=0)

    def from_owner(i):
        return o_slices[:owners, :, i * span : (i + 1) * span].transpose(1, 0, 2).reshape(used, width)

    def from_shared(i):
        at = 3 * span + 128 * i
        return (
            o_slices[:, :, at : at + shared_cols]
            .reshape(8, used, 16, down_used)
            .transpose(1, 2, 0, 3)
            .reshape(used, hidden)
        )

    return (
        out,
        d_tokens,
        from_owner(0),
        from_owner(1),
        from_owner(2),
        o_whole[:, :width],
        o_whole[:, width : width + experts],
        from_shared(0),
        from_shared(1),
        o_down[:down_used].astype(F32),
        o_whole[:, width + experts],
        o_whole[:, width + experts + 1],
        e_gate.reshape(exp_dev, width, hidden).astype(F32),
        e_up.reshape(exp_dev, width, hidden).astype(F32),
        e_down.reshape(exp_dev, hidden, width).astype(F32),
    )


def solution(mesh):
    both = ("rep", "ep")
    row = P(both, None)
    expert = P("ep", None, None)
    in_specs = (
        row, row, P("rep"), P(both), row, row, row, row, row, row, row, row, row,
        P(both), P(both), expert, expert, expert,
    )
    out_specs = (
        row, row, row, row, row, row, row, row, row, row, P(both), P(both),
        expert, expert, expert,
    )
    return jax.shard_map(body, mesh=mesh, in_specs=in_specs, out_specs=out_specs, check_vma=False)
```

time: 3520 us -> 594 us (0.17)
  waiting for transfers between devices: 2070 us -> 0 us
  blocking collectives: 915 us -> 0 us
  Pallas kernels: 0 us -> 313 us
  local copies, waits for them, and re-layouts: 161 us -> 74.9 us
  starting transfers between devices: 78.2 us -> 0 us
  other arithmetic: 90.8 us -> 46.3 us
    all_gather x9 -> x0, waiting for transfers between devices: 1820 us -> none  [the longest x1 319 us: body(): lax.all_gather(shared_down, ('rep', 'ep'), axis=0, tiled=True)]
    unnamed x3 -> x0, blocking collectives: 555 us -> none
    all_gather x2 -> x0, blocking collectives: 360 us -> none  [the longest x1 340 us: body(): lax.all_gather(w_router, ('rep', 'ep'), axis=0, tiled=True)]
    pallas_call x0 -> x4, Pallas kernels: none -> 313 us  [the longest x1 109 us: call_d(): pl.pallas_call(kernel_d, out_shape=(jax.ShapeDtypeStruct((rows, width), F...]
    unnamed x30 -> x0, waiting for transfers between devices: 115 us -> none
    unnamed x172 -> x140, local copies, waits for them, and re-layouts: 93 us -> 11 us
    reshape x1 -> x0, waiting for transfers between devices: 68.2 us -> none  [body(): grad_value_local.astype(jnp.bfloat16).reshape(tok_dev, model_width)]
    unnamed x17 -> x0, starting transfers between devices: 58.8 us -> none
  transfers between devices with their start and end apart: 33 -> 0, of which waited for: 15 -> 0; matrix products, arithmetic and copies ran while one was open for 21% -> 0% of each run, Pallas kernels for 0% -> 0%
where the time goes in v1:
time: 594 us; the launch traced here: 585 us
  Pallas kernels  313 us (53%)
  matrix products  148 us (25%)
  local copies, waits for them, and re-layouts  74.9 us (13%)
  other arithmetic  46.3 us (8%)
    pallas_call x1, Pallas kernels, call_d(): pl.pallas_call(kernel_d, out_shape=(jax.ShapeDtypeStruct((rows, width), F...  109 us
    pallas_call x1, Pallas kernels, call_c(): pl.pallas_call(kernel_c, out_shape=(jax.ShapeDtypeStruct((rows, width), B...  102 us
    pallas_call x1, Pallas kernels, call_a(): pl.pallas_call(kernel_a, out_shape=(jax.ShapeDtypeStruct((8,) + tok.shape...  66.5 us
    pallas_call x1, Pallas kernels, call_b(): pl.pallas_call(kernel_b, out_shape=(jax.ShapeDtypeStruct((rows, width), F...  36 us
    dot_general x1, matrix products, body(): jnp.einsum('td,edf->etf', hidden_all, expert_up, preferred_element_type=F32)  15.1 us
    dot_general x4, matrix products, dot_nt(): lax.dot_general(a, b, (((1,), (1,)), ((), ())), preferred_element_type=F32)  13.8 us
    dot_general x5, matrix products, dot(): return jnp.dot(a, b, preferred_element_type=F32)  13.3 us

profile of v1, /device:TPU:1, one launch (start us, length us, event | category | flops | bytes accessed | tf_op | source)
XLA Modules:
  0.0 584.9 jit_solution(9794387933724489606)
XLA Ops:
  10.8 66.5 %gather_inputs.1 = (bf16[8,128,1408]{2,1,0:T(8,128)(2,1)}, bf16[8,128,1280]{2,1,0:T(8,128)(2,1)}, bf16[16,80,1024]{2,1,0:T(8,128)(2,1)}, bf16[16,80,1408]{2,1,0:T(8,128)(2,1)}, bf16[16,16,1280]{2,1,0:T(8,128)(2,1)}) custom-call(bf16[8,16,1024]{2,1,0:T(8,128)(2,1)} %pad.59.slices, bf16[16,1408]{1,0:T(8,128)(2,1)} %pad.60.whole, bf16[16,1280]{1,0:T(8,128)(2,1)} %pad.61.down, ...), custom_call_target="tpu_custom_call" | custom-call | tf_op jit(solution)/shard_map/gather_inputs/pallas_call | solution.py:301
  84.1 3.9 fusion.32
  92.6 3.3 fusion.73
  101.8 3.2 subtract_convert_fusion.3
  105.0 8.9 %fusion.88 = (f32[2,1024]{1,0:T(2,128)S(1)}, f32[2,1024,1024]{1,2,0:T(8,128)}) fusion(pred[1024,1024]{0,1:T(8,128)(4,1)} %fusion.20, bf16[1024,2,64]{2,0,1:T(8,128)(2,1)} %get-tuple-element.94, bf16[1024,2,64]{2,0,1:T(8,128)(2,1)} %get-tuple-element.95, bf16[1024,2,64]{2,0,1:T(8,128)(2,1)} %get-tuple-element.80, bf16[1024,2,64]{2,0,1:T(8,128)(2,1)S(1)} %get-tuple-element.79), kind=kOutput, calls=%fused_computation.175 | convolution fusion | flops 547357696 | bytes 10493952 | tf_op jit(solution)/shard_map/sub | solution.py:808
  114.0 4.1 fusion.36
  120.1 3.8 slice.159.w_out
  124.5 36.0 %attention_out.1 = (f32[128,1280]{1,0:T(8,128)}, bf16[128,1280]{1,0:T(8,128)(2,1)}, bf16[8,128,1280]{2,1,0:T(8,128)(2,1)}) custom-call(bf16[8,128,256]{2,1,0:T(8,128)(2,1)} %copy.294.heads, bf16[128,1280]{1,0:T(8,128)(2,1)} %tok.1, f32[128,1]{1,0:T(8,128)} %copy.239.live, bf16[1280,1280]{1,0:T(8,128)(2,1)} %slice.159.w_out, f32[1,1280]{1,0:T(1,128)} %reshape.412.gain), custom_call_target="tpu_custom_call" | custom-call | tf_op jit(solution)/shard_map/attention_out/pallas_call | solution.py:362
  165.2 11.5 %fusion.90 = f32[1024,2,896]{0,2,1:T(8,128)} fusion(bf16[1024,1280,1]{1,0,2:T(8,128)(2,1)} %bitcast.213, bf16[2,896,1280]{2,1,0:T(8,128)(2,1)} %param.35), kind=kOutput, calls=%fused_computation.177 | convolution fusion | flops 4697620480 | bytes 14548992 | tf_op jit(solution)/shard_map/td,efd->etf/dot_general | solution.py:836
  176.7 9.4 %fusion.91 = f32[1024,2,896]{0,2,1:T(8,128)} fusion(bf16[1024,1280,1]{1,0,2:T(8,128)(2,1)S(1)} %bitcast.203, bf16[2,1280,896]{2,1,0:T(8,128)(2,1)} %param.33), kind=kOutput, calls=%fused_computation.178 | convolution fusion | flops 4697620480 | bytes 14548992 | tf_op jit(solution)/shard_map/td,edf->etf/dot_general | solution.py:833
  186.1 15.1 %fusion.5 = (bf16[2,1024,896]{1,2,0:T(8,128)(2,1)}, f32[2,1024]{1,0:T(2,128)S(1)}, bf16[2,1024,896]{1,2,0:T(8,128)(2,1)}, bf16[2,1024,896]{1,2,0:T(8,128)(2,1)}) fusion(f32[1024,2,896]{0,2,1:T(8,128)} %fusion.90, f32[1024,2,896]{0,2,1:T(8,128)} %fusion.91, f32[2,1024]{1,0:T(2,128)S(1)} %bitcast.271, bf16[1024,1280,1]{1,0,2:T(8,128)(2,1)S(1)} %bitcast.204, ...), kind=kOutput, calls=%fused_computation.14 | convolution fusion | flops 4730648576 | bytes 32915456 | tf_op jit(solution)/shard_map/td,edf->etf/dot_general | solution.py:834
  212.7 7.2 %fusion.93 = f32[1024,1280,1]{1,0,2:T(8,128)S(1)} fusion(bf16[2,1024,896]{1,2,0:T(8,128)(2,1)} %get-tuple-element.76, bf16[2,1280,896]{2,1,0:T(8,128)(2,1)S(1)} %bitcast.278), kind=kOutput, calls=%fused_computation.180 | convolution fusion | flops 4697620480 | bytes 13500416 | tf_op jit(solution)/shard_map/etf,edf->td/dot_general | solution.py:860
  220.0 7.3 %fusion.92 = f32[1024,1280,1]{1,0,2:T(8,128)S(1)} fusion(bf16[2,1024,896]{1,2,0:T(8,128)(2,1)} %get-tuple-element.73, bf16[2,1280,896]{2,1,0:T(8,128)(2,1)S(1)} %bitcast.280), kind=kOutput, calls=%fused_computation.179 | convolution fusion | flops 4697620480 | bytes 13500416 | tf_op jit(solution)/shard_map/etf,edf->td/dot_general | solution.py:859
  232.3 5.4 fusion.94
  240.3 6.5 %fusion.23 = bf16[2,1280,896]{1,2,0:T(8,128)(2,1)} fusion(bf16[2,1024,896]{1,2,0:T(8,128)(2,1)S(1)} %copy-done.46, bf16[1024,1280,1]{1,0,2:T(8,128)(2,1)S(1)} %bitcast.207), kind=kOutput, calls=%fused_computation.50 | convolution fusion | flops 4699914240 | bytes 10878976 | tf_op jit(solution)/shard_map/td,etf->edf/dot_general | solution.py:842
  246.8 7.3 %copy.250 = bf16[2,1280,896]{2,1,0:T(8,128)(2,1)} copy(bf16[2,1280,896]{1,2,0:T(8,128)(2,1)} %fusion.23) | data formatting | bytes 9175040 | tf_op jit(solution)/shard_map/convert_element_type | solution.py:842
  254.1 9.5 %fusion.24 = bf16[2,1280,896]{1,2,0:T(8,128)(2,1)} fusion(bf16[2,1024,896]{1,2,0:T(8,128)(2,1)} %get-tuple-element.76, bf16[1024,1280,1]{1,0,2:T(8,128)(2,1)S(1)} %bitcast.208), kind=kOutput, calls=%fused_computation.51 | convolution fusion | flops 4699914240 | bytes 10878976 | tf_op jit(solution)/shard_map/td,etf->edf/dot_general | solution.py:843
  263.6 7.5 %copy.251 = bf16[2,1280,896]{2,1,0:T(8,128)(2,1)} copy(bf16[2,1280,896]{1,2,0:T(8,128)(2,1)} %fusion.24) | data formatting | bytes 9175040 | tf_op jit(solution)/shard_map/convert_element_type | solution.py:843
  271.1 9.9 %convolution_convert_fusion.1 = bf16[2,896,1280]{2,1,0:T(8,128)(2,1)} fusion(bf16[2,1024,896]{1,2,0:T(8,128)(2,1)} %get-tuple-element.75, bf16[1024,1280,1]{1,0,2:T(8,128)(2,1)} %bitcast.215), kind=kOutput, calls=%fused_computation.36 | convolution fusion | flops 4699914240 | bytes 10878976 | tf_op jit(solution)/shard_map/etf,td->efd/dot_general | solution.py:844
  284.3 101.5 %sum_hidden_two.1 = (bf16[128,1280]{1,0:T(8,128)(2,1)}, f32[128,1280]{1,0:T(8,128)}, bf16[128,1280]{1,0:T(8,128)(2,1)}, f32[128,128]{1,0:T(8,128)}, f32[1,1280]{...) custom-call(bf16[8,128,1408]{2,1,0:T(8,128)(2,1)} %bitcast.220, ...), custom_call_target="tpu_custom_call" | custom-call | tf_op jit(solution)/shard_map/sum_hidden_two/pallas_call | solution.py:542
  388.1 6.0 %fusion.39 = bf16[2,128,1024]{2,1,0:T(8,128)(2,1)} fusion(bf16[1024,2,128]{0,2,1:T(8,128)(2,1)} %copy.263, f32[2,1024,1024]{1,2,0:T(8,128)} %get-tuple-element.109, f32[2,1024]{1,0:T(2,128)S(1)} %get-tuple-element.108), kind=kOutput, calls=%fused_computation.69 | convolution fusion | flops 541327360 | bytes 9445376 | tf_op jit(solution)/shard_map/hqk,qhd->khd/dot_general | solution.py:881
  394.1 4.9 multiply_reduce_fusion
  399.9 2.9 multiply_convert_fusion
  411.4 7.1 %fusion.12 = (bf16[1280]{0:T(1024)(128)(2,1)S(1)}, bf16[1024,1280]{1,0:T(8,128)(2,1)}) fusion(f32[1024]{0:T(1024)S(1)} %copy-done.40, bf16[1024,1408]{1,0:T(8,128)(2,1)} %bitcast.238, bf16[1280,1024]{1,0:T(8,128)(2,1)} %bitcast.267, bf16[1024,256]{0,1:T(8,128)(2,1)} %bitcast.283, bf16[1024,256]{0,1:T(8,128)(2,1)} %bitcast.253, bf16[1024,256]{0,1:T(8,128)(2,1)} %bitcast.255), kind=kOutput, calls=%fused_computation.28 | convolution fusion | flops 2024536832 | bytes 8788480 | tf_op jit(solution)/shard_map/dot_general | solution.py:28
  418.5 2.8 copy.265
  421.3 2.7 convolution_convert_fusion.5
  431.1 2.7 convolution_convert_fusion
  437.2 6.8 %concatenate.71.d_whole = bf16[4,2,2,80,1408]{4,3,2,1,0:T(8,128)(2,1)} concatenate(bf16[4,2,2,80,1280]{4,3,2,1,0:T(8,128)(2,1)} %bitcast.219, bf16[4,2,2,80,16]{4,3,2,1,0:T(8,128)(2,1)S(1)} %bitcast.248, bf16[4,2,2,80,1]{4,3,2,1,0:T(8,128)(2,1)} %concatenate.72, bf16[4,2,2,80,1]{4,3,2,1,0:T(8,128)(2,1)} %concatenate.73, bf16[4,2,2,80,110]{4,3,2,1,0:T(8,128)(2,1)S(1)} %broadcast_in_dim.29), dimensions={4} | concatenate | bytes 7208960 | tf_op jit(solution)/shard_map/concatenate | solution.py:905
  445.7 109.2 %sum_hidden_one.1 = (f32[128,1280]{1,0:T(8,128)}, bf16[2,4,2,160,896]{4,3,2,1,0:T(8,128)(2,1)}, bf16[2,4,2,160,896]{4,3,2,1,0:T(8,128)(2,1)}, bf16[2,4,2,112,128...) custom-call(bf16[8,128,1280]{2,1,0:T(8,128)(2,1)} %bitcast.245, ...), custom_call_target="tpu_custom_call" | custom-call | tf_op jit(solution)/shard_map/sum_hidden_one/pallas_call | solution.py:682
  567.7 7.0 %bitcast_convert_fusion.2 = f32[2,1280,896]{2,1,0:T(8,128)} fusion(bf16[2,4,2,160,896]{4,3,2,1,0:T(8,128)(2,1)} %get-tuple-element.60), kind=kLoop, calls=%fused_computation.41 | loop fusion | flops 2293760 | bytes 13762560 | tf_op jit(solution)/shard_map/convert_element_type | solution.py:958
  574.7 4.6 bitcast_convert_fusion.1
  579.3 4.7 bitcast_convert_fusion
  (260 shorter events, 93.0 us)
Async XLA Ops:
  0.6 7.1 %copy-start.33 = (bf16[10,1280]{1,0:T(8,128)(2,1)S(1)}, bf16[10,1280]{1,0:T(8,128)(2,1)}, u32[]{:S(2)}) copy-start(bf16[10,1280]{1,0:T(8,128)(2,1)} %param.26) | copy-start | bytes 76804
  0.7 7.1 %copy-start.37 = (bf16[10,16]{1,0:T(8,128)(2,1)S(1)}, bf16[10,16]{1,0:T(8,128)(2,1)}, u32[]{:S(2)}) copy-start(bf16[10,16]{1,0:T(8,128)(2,1)} %param.27) | copy-start | bytes 964
  0.7 6.9 %copy-start.41 = (bf16[10]{0:T(256)(128)(2,1)S(1)}, bf16[10]{0:T(256)(128)(2,1)}, u32[]{:S(2)}) copy-start(bf16[10]{0:T(256)(128)(2,1)} %param.31) | copy-start | bytes 64
  0.7 7.0 %copy-start.42 = (bf16[10]{0:T(256)(128)(2,1)S(1)}, bf16[10]{0:T(256)(128)(2,1)}, u32[]{:S(2)}) copy-start(bf16[10]{0:T(256)(128)(2,1)} %param.32) | copy-start | bytes 64
  0.7 7.9 %copy-start.34 = (bf16[7,1280]{1,0:T(8,128)(2,1)S(1)}, bf16[7,1280]{1,0:T(8,128)(2,1)}, u32[]{:S(2)}) copy-start(bf16[7,1280]{1,0:T(8,128)(2,1)} %param.30) | copy-start | bytes 53764
  0.7 9.1 %copy-start.43 = (s32[128]{0:T(128)S(1)}, s32[128]{0:T(128)}, u32[]{:S(2)}) copy-start(s32[128]{0:T(128)} %param.21) | copy-start | bytes 1540
  0.7 9.2 %copy-start.38 = (s32[128,7]{0,1:T(8,128)S(1)}, s32[128,7]{0,1:T(8,128)}, u32[]{:S(2)}) copy-start(s32[128,7]{0,1:T(8,128)} %param.22) | copy-start | bytes 10756
  0.7 9.3 %copy-start.2 = (bf16[128,1280]{1,0:T(8,128)(2,1)S(1)}, bf16[128,1280]{1,0:T(8,128)(2,1)}, u32[]{:S(2)}) copy-start(bf16[128,1280]{1,0:T(8,128)(2,1)} %tok.1) | copy-start | bytes 983044
  77.3 6.8 %copy-start.6 = (bf16[8,128,1408]{2,1,0:T(8,128)(2,1)S(1)}, bf16[8,128,1408]{2,1,0:T(8,128)(2,1)}, u32[]{:S(2)}) copy-start(bf16[8,128,1408]{2,1,0:T(8,128)(2,1)} %get-tuple-element.40) | copy-start | bytes 8650756
  95.9 9.1 %copy-start.4 = (f32[1024,64]{1,0:T(8,128)}, f32[1024,64]{1,0:T(8,128)S(1)}, u32[]{:S(2)}) copy-start(f32[1024,64]{1,0:T(8,128)S(1)} %get-tuple-element.107) | copy-start | bytes 786436
  105.0 8.9 %copy-start.8 = (bf16[1024,2,64]{2,0,1:T(8,128)(2,1)}, bf16[1024,2,64]{2,0,1:T(8,128)(2,1)S(1)}, u32[]{:S(2)}) copy-start(bf16[1024,2,64]{2,0,1:T(8,128)(2,1)S(1)} %get-tuple-element.79) | copy-start | bytes 786436
  105.0 8.9 %copy-start.21 = (bf16[1024,256]{0,1:T(8,128)(2,1)S(1)}, bf16[1024,256]{0,1:T(8,128)(2,1)}, u32[]{:S(2)}) copy-start(bf16[1024,256]{0,1:T(8,128)(2,1)} %slice.221) | copy-start | bytes 1572868
  165.2 11.5 %copy-start = (bf16[8,128,1280]{2,1,0:T(8,128)(2,1)S(1)}, bf16[8,128,1280]{2,1,0:T(8,128)(2,1)}, u32[]{:S(2)}) copy-start(bf16[8,128,1280]{2,1,0:T(8,128)(2,1)} %get-tuple-element.43) | copy-start | bytes 7864324
  165.2 20.9 %slice-start.6 = ((s8[4587520]{0:T(1024)(128)(4,1)}), s8[4194304]{0:T(1024)(128)(4,1)S(1)}, s32[]{:S(2)}) async-start(s8[4587520]{0:T(1024)(128)(4,1)} %bitcast.275), calls=%async_computation.6 | async-start | bytes 8388608
  176.7 9.4 %slice-start.7 = ((s8[4587520]{0:T(1024)(128)(4,1)}), s8[393216]{0:T(1024)(128)(4,1)S(1)}, s32[]{:S(2)}) async-start(s8[4587520]{0:T(1024)(128)(4,1)} %bitcast.275), calls=%async_computation.7 | async-start | bytes 786432
  205.9 6.8 %slice-start.8 = ((s8[4587520]{0:T(1024)(128)(4,1)}), s8[4194304]{0:T(1024)(128)(4,1)S(1)}, s32[]{:S(2)}) async-start(s8[4587520]{0:T(1024)(128)(4,1)} %bitcast.277), calls=%async_computation.8 | async-start | bytes 8388608
  210.6 9.3 %copy-start.17 = (bf16[1024,128]{1,0:T(8,128)(2,1)}, bf16[1024,128]{1,0:T(8,128)(2,1)S(1)}, u32[]{:S(2)}) copy-start(bf16[1024,128]{1,0:T(8,128)(2,1)S(1)} %get-tuple-element.92) | copy-start | bytes 786436
  210.6 27.1 %copy-start.15 = (bf16[1024,128]{1,0:T(8,128)(2,1)}, bf16[1024,128]{1,0:T(8,128)(2,1)S(1)}, u32[]{:S(2)}) copy-start(bf16[1024,128]{1,0:T(8,128)(2,1)S(1)} %get-tuple-element.91) | copy-start | bytes 786436
  210.6 9.3 %slice-start.10 = ((s8[4587520]{0:T(1024)(128)(4,1)}), s8[4194304]{0:T(1024)(128)(4,1)S(1)}, s32[]{:S(2)}) async-start(s8[4587520]{0:T(1024)(128)(4,1)} %bitcast.279), calls=%async_computation.10 | async-start | bytes 8388608
  212.7 7.3 %slice-start.11 = ((s8[4587520]{0:T(1024)(128)(4,1)}), s8[393216]{0:T(1024)(128)(4,1)S(1)}, s32[]{:S(2)}) async-start(s8[4587520]{0:T(1024)(128)(4,1)} %bitcast.279), calls=%async_computation.11 | async-start | bytes 786432
  212.7 18.3 %slice-start.12 = ((s8[4587520]{0:T(1024)(128)(4,1)}), s8[4194304]{0:T(1024)(128)(4,1)S(1)}, s32[]{:S(2)}) async-start(s8[4587520]{0:T(1024)(128)(4,1)} %bitcast.281), calls=%async_computation.12 | async-start | bytes 8388608
  220.0 11.0 %slice-start.13 = ((s8[4587520]{0:T(1024)(128)(4,1)}), s8[393216]{0:T(1024)(128)(4,1)S(1)}, s32[]{:S(2)}) async-start(s8[4587520]{0:T(1024)(128)(4,1)} %bitcast.281), calls=%async_computation.13 | async-start | bytes 786432
  429.2 6.6 %copy-start.36 = (f32[1,1280]{1,0:T(1,128)S(1)}, f32[1,1280]{1,0:T(1,128)}, u32[]{:S(2)}) copy-start(f32[1,1280]{1,0:T(1,128)} %get-tuple-element.55) | copy-start | bytes 15364
  437.2 6.9 %copy-start.1 = (bf16[8,128,1280]{2,1,0:T(8,128)(2,1)S(1)}, bf16[8,128,1280]{2,1,0:T(8,128)(2,1)}, u32[]{:S(2)}) copy-start(bf16[8,128,1280]{2,1,0:T(8,128)(2,1)} %get-tuple-element.39) | copy-start | bytes 7864324
  437.2 6.9 %copy-start.16 = (bf16[1024,128]{1,0:T(8,128)(2,1)S(1)}, bf16[1024,128]{1,0:T(8,128)(2,1)}, u32[]{:S(2)}) copy-start(bf16[1024,128]{1,0:T(8,128)(2,1)} %copy-done.15) | copy-start | bytes 786436
  445.7 109.2 %copy-start.3 = (bf16[128,1280]{1,0:T(8,128)(2,1)S(1)}, bf16[128,1280]{1,0:T(8,128)(2,1)}, u32[]{:S(2)}) copy-start(bf16[128,1280]{1,0:T(8,128)(2,1)} %tok.1) | copy-start | bytes 983044
  445.7 110.7 %copy-start.20 = (f32[128,1280]{1,0:T(8,128)S(1)}, f32[128,1280]{1,0:T(8,128)}, u32[]{:S(2)}) copy-start(f32[128,1280]{1,0:T(8,128)} %get-tuple-element.47) | copy-start | bytes 1966084
  554.9 6.9 %copy-start.26 = (bf16[8,16,1408]{2,1,0:T(8,128)(2,1)S(1)}, bf16[8,16,1408]{2,1,0:T(8,128)(2,1)}, u32[]{:S(2)}) copy-start(bf16[8,16,1408]{2,1,0:T(8,128)(2,1)} %get-tuple-element.58) | copy-start | bytes 1081348
  559.6 6.7 %copy-start.35 = (bf16[16,1280]{1,0:T(8,128)(2,1)S(1)}, bf16[16,1280]{1,0:T(8,128)(2,1)}, u32[]{:S(2)}) copy-start(bf16[16,1280]{1,0:T(8,128)(2,1)} %get-tuple-element.59) | copy-start | bytes 122884
  565.3 9.4 %slice-start.4 = ((s8[4587520]{0:T(1024)(128)(4,1)}), s8[393216]{0:T(1024)(128)(4,1)S(1)}, s32[]{:S(2)}) async-start(s8[4587520]{0:T(1024)(128)(4,1)} %bitcast.231), calls=%async_computation.4 | async-start | bytes 786432
  567.7 7.0 %slice-start.5 = ((s8[4587520]{0:T(1024)(128)(4,1)}), s8[4194304]{0:T(1024)(128)(4,1)S(1)}, s32[]{:S(2)}) async-start(s8[4587520]{0:T(1024)(128)(4,1)} %bitcast.231), calls=%async_computation.5 | async-start | bytes 8388608
  567.7 11.7 %slice-start.2 = ((s8[4587520]{0:T(1024)(128)(4,1)}), s8[4194304]{0:T(1024)(128)(4,1)S(1)}, s32[]{:S(2)}) async-start(s8[4587520]{0:T(1024)(128)(4,1)} %bitcast.229), calls=%async_computation.2 | async-start | bytes 8388608
  (29 other events, 114.5 us)

commit v2 on v1

v2 whole, which is shorter than its diff:
```python
import functools
import itertools

import jax
import jax.numpy as jnp
import numpy as np
from jax import lax
from jax.experimental import pallas as pl
from jax.experimental.pallas import tpu as pltpu
from jax.sharding import PartitionSpec as P

HD = 128
EPS = 1e-6
BF = jnp.bfloat16
F32 = jnp.float32
MESH = pl.DeviceIdType.MESH
HIGH = lax.Precision.HIGHEST
HEADS_DEV = 2
EXTRA = 128
ROW_PAD = 16
VMEM_LIMIT = 60 << 20


def dot(a, b):
    return jnp.dot(a, b, preferred_element_type=F32)


def dot_nt(a, b):
    return lax.dot_general(a, b, (((1,), (1,)), ((), ())), preferred_element_type=F32)


def dot_tn(a, b):
    return lax.dot_general(a, b, (((0,), (0,)), ((), ())), preferred_element_type=F32)


class Place:
    def __init__(self):
        self.rep = lax.axis_index("rep")
        self.ep = lax.axis_index("ep")
        self.y = self.rep // 4
        self.zl = (self.rep // 2) % 2
        self.core = self.rep % 2
        self.x = self.ep // 2
        self.zh = self.ep % 2

    def rep_at(self, y, zl, core):
        return (y % 4) * 4 + zl * 2 + core

    def ep_at(self, x, zh):
        return (x % 4) * 2 + zh

    def to_x(self, step):
        return (self.rep, self.ep_at(self.x + step, self.zh))

    def to_zh(self):
        return (self.rep, self.ep_at(self.x, 1 - self.zh))

    def to_ep(self, shift):
        return (self.rep, (self.ep + shift) % 8)

    def to_y(self, step):
        return (self.rep_at(self.y + step, self.zl, self.core), self.ep)

    def to_zl(self):
        return (self.rep_at(self.y, 1 - self.zl, self.core), self.ep)

    def to_core(self):
        return (self.rep_at(self.y, self.zl, 1 - self.core), self.ep)


class Copies:
    def __init__(self, send_sem, recv_sem):
        self.send_sem, self.recv_sem = send_sem, recv_sem
        self.number = itertools.count()
        self.sent, self.open = [], []

    def send(self, src, dst, device):
        i = next(self.number)
        copy = pltpu.make_async_remote_copy(
            src_ref=src,
            dst_ref=dst,
            send_sem=self.send_sem.at[i],
            recv_sem=self.recv_sem.at[i],
            device_id=device,
            device_id_type=MESH,
        )
        copy.start()
        self.sent.append(copy)
        self.open.append(copy)
        return copy

    def local(self, src, dst):
        i = next(self.number)
        copy = pltpu.make_async_copy(src, dst, self.recv_sem.at[i])
        copy.start()
        self.open.append(copy)
        return copy

    def arrived(self, copy):
        if any(copy is c for c in self.sent):
            copy.wait_recv()
        else:
            copy.wait()
        self.open = [c for c in self.open if c is not copy]

    def sent_off(self, copy):
        copy.wait_send()
        self.sent = [c for c in self.sent if c is not copy]

    def finish(self):
        for copy in list(self.open):
            self.arrived(copy)
        for copy in self.sent:
            copy.wait_send()


def greet(devices):
    barrier = pltpu.get_barrier_semaphore()
    for device in devices:
        pl.semaphore_signal(barrier, inc=1, device_id=device, device_id_type=MESH)
    pl.semaphore_wait(barrier, len(devices))


def run_streams(*streams):
    live = list(streams)
    while live:
        for stream in list(live):
            try:
                next(stream)
            except StopIteration:
                live.remove(stream)


def half_columns(columns):
    return (columns // 128 + 1) // 2 * 128


def ep_peers(place):
    return [place.to_ep(k) for k in range(1, 8)]


def rep_peers(place):
    return [place.to_y(1), place.to_y(-1), place.to_zl(), place.to_core()]


def gather_ep(cp, place, src, dst, columns):
    cut = half_columns(columns)
    lo, hi = pl.ds(0, cut), pl.ds(cut, columns - cut)
    mine = place.ep
    own = cp.local(src, dst.at[mine])
    right = cp.send(src, dst.at[mine], place.to_x(1))
    left = cp.send(src, dst.at[mine], place.to_x(-1))
    over = cp.send(src, dst.at[mine], place.to_zh())
    yield
    from_left = place.ep_at(place.x - 1, place.zh)
    from_right = place.ep_at(place.x + 1, place.zh)
    from_over = place.ep_at(place.x, 1 - place.zh)
    far = place.ep_at(place.x + 2, place.zh)
    cp.arrived(right)
    half_a = cp.send(dst.at[from_left, :, lo], dst.at[from_left, :, lo], place.to_x(1))
    cp.arrived(left)
    half_b = cp.send(dst.at[from_right, :, hi], dst.at[from_right, :, hi], place.to_x(-1))
    yield
    cp.arrived(over)
    cp.send(dst.at[from_over], dst.at[from_over], place.to_x(1))
    cp.send(dst.at[from_over], dst.at[from_over], place.to_x(-1))
    yield
    cp.arrived(half_a)
    cp.arrived(half_b)
    cp.send(dst.at[far], dst.at[far], place.to_zh())
    yield
    cp.arrived(own)


def gather_ring_y(cp, place, src, dst, columns, slot):
    cut = half_columns(columns)
    lo, hi = pl.ds(0, cut), pl.ds(cut, columns - cut)
    up = cp.send(src, dst.at[slot(place.y)], place.to_y(1))
    down = cp.send(src, dst.at[slot(place.y)], place.to_y(-1))
    yield
    cp.arrived(up)
    below = slot(place.y - 1)
    half_a = cp.send(dst.at[below, :, lo], dst.at[below, :, lo], place.to_y(1))
    cp.arrived(down)
    above = slot(place.y + 1)
    half_b = cp.send(dst.at[above, :, hi], dst.at[above, :, hi], place.to_y(-1))
    yield
    cp.arrived(half_a)
    cp.arrived(half_b)


def gather_rep(cp, place, src, dst, columns, z_first):
    mine = place.rep
    own = cp.local(src, dst.at[mine])
    cp.send(src, dst.at[mine], place.to_core())

    def slot(zl):
        return lambda y: place.rep_at(y, zl, place.core)

    def pass_core(index):
        cp.send(dst.at[index], dst.at[index], place.to_core())

    here, there = slot(place.zl), slot(1 - place.zl)
    if z_first:
        over = cp.send(src, dst.at[mine], place.to_zl())
        first = gather_ring_y(cp, place, src, dst, columns, here)
        next(first)
        yield
        cp.arrived(over)
        second = gather_ring_y(
            cp, place, dst.at[there(place.y)], dst, columns, there
        )
        next(second)
        pass_core(there(place.y))
        yield
        next(first)
        for k in (-1, 1):
            pass_core(here(place.y + k))
        yield
        next(second)
        for k in (-1, 1):
            pass_core(there(place.y + k))
        yield
        next(first, None)
        pass_core(here(place.y + 2))
        yield
        next(second, None)
        pass_core(there(place.y + 2))
    else:
        over = [cp.send(src, dst.at[mine], place.to_zl())]
        ring = gather_ring_y(cp, place, src, dst, columns, here)
        next(ring)
        yield
        next(ring)
        for k in (-1, 1):
            block = dst.at[here(place.y + k)]
            over.append(cp.send(block, block, place.to_zl()))
            pass_core(here(place.y + k))
        yield
        next(ring, None)
        block = dst.at[here(place.y + 2)]
        over.append(cp.send(block, block, place.to_zl()))
        pass_core(here(place.y + 2))
        yield
        for copy, k in zip(over, (0, -1, 1, 2)):
            cp.arrived(copy)
            pass_core(there(place.y + k))
            yield
    cp.arrived(own)


def spread_matrix(rows, blocks, used):
    shape = (rows, blocks * ROW_PAD)
    to = lax.broadcasted_iota(jnp.int32, shape, 0)
    at = lax.broadcasted_iota(jnp.int32, shape, 1)
    return jnp.where((at // ROW_PAD) * used + at % ROW_PAD == to, 1.0, 0.0) * jnp.where(
        at % ROW_PAD < used, 1.0, 0.0
    )


def kernel_a(
    slices, whole, down, tok, cot,
    tok_all, cot_all, w_slices, w_whole, w_down,
    land_slices, land_whole, pack_slices, pack_whole, send_sem, recv_sem,
):
    place = Place()
    cp = Copies(send_sem, recv_sem)
    greet(ep_peers(place) + rep_peers(place))
    first = []
    mine = place.ep
    first.append(cp.local(slices.at[mine], land_slices.at[mine]))
    first.append(cp.local(whole, land_whole.at[mine]))
    for k in range(1, 8):
        first.append(cp.send(slices.at[(mine + k) % 8], land_slices.at[mine], place.to_ep(k)))
        first.append(cp.send(whole, land_whole.at[mine], place.to_ep(k)))
    tok_stream = gather_ep(cp, place, tok, tok_all, tok.shape[1])
    next(tok_stream)
    down_stream = gather_rep(cp, place, down, w_down, down.shape[1], True)
    next(down_stream)
    for copy in first:
        cp.arrived(copy)
    used = pack_slices.shape[0] // 8
    spread = spread_matrix(8 * used, 8, used).astype(BF)
    for land, pack in ((land_slices, pack_slices), (land_whole, pack_whole)):
        columns = land.shape[2]
        step = 128
        for c in range(0, columns, step):
            block = land[:, :, c : c + step].reshape(8 * ROW_PAD, step)
            pack[:, c : c + step] = dot(spread, block).astype(BF)
    slice_stream = gather_rep(cp, place, pack_slices, w_slices, slices.shape[2], False)
    next(slice_stream)
    whole_stream = gather_rep(cp, place, pack_whole, w_whole, whole.shape[1], True)
    next(whole_stream)
    cot_stream = gather_ep(cp, place, cot, cot_all, cot.shape[1])
    run_streams(tok_stream, slice_stream, whole_stream, cot_stream, down_stream)
    cp.finish()


def call_a(slices, whole, down, tok, cot, used):
    anyspace = pl.BlockSpec(memory_space=pl.ANY)
    copies = 160
    return pl.pallas_call(
        kernel_a,
        out_shape=(
            jax.ShapeDtypeStruct((8,) + tok.shape, BF),
            jax.ShapeDtypeStruct((8,) + cot.shape, BF),
            jax.ShapeDtypeStruct((16, 8 * used, slices.shape[2]), BF),
            jax.ShapeDtypeStruct((16, 8 * used, whole.shape[1]), BF),
            jax.ShapeDtypeStruct((16,) + down.shape, BF),
        ),
        in_specs=[anyspace] * 5,
        out_specs=(anyspace,) * 5,
        scratch_shapes=[
            pltpu.VMEM((8, ROW_PAD, slices.shape[2]), BF),
            pltpu.VMEM((8, ROW_PAD, whole.shape[1]), BF),
            pltpu.VMEM((8 * used, slices.shape[2]), BF),
            pltpu.VMEM((8 * used, whole.shape[1]), BF),
            pltpu.SemaphoreType.DMA((copies,)),
            pltpu.SemaphoreType.DMA((copies,)),
        ],
        compiler_params=pltpu.CompilerParams(
            collective_id=0, has_side_effects=True, vmem_limit_bytes=VMEM_LIMIT
        ),
        name="gather_inputs",
    )(slices, whole, down, tok, cot)


def kernel_b(
    heads, tok, live, w_out, gain,
    residual, attended, hidden_all,
    land, hidden, send_sem, recv_sem,
):
    place = Place()
    cp = Copies(send_sem, recv_sem)
    greet(ep_peers(place))
    rows, width = tok.shape
    mine = place.ep
    span = heads.shape[2]
    column = pl.ds(pl.multiple_of(mine * span, 128), span)
    first = [cp.local(heads.at[mine], land.at[:, column])]
    for k in range(1, 8):
        first.append(cp.send(heads.at[(mine + k) % 8], land.at[:, column], place.to_ep(k)))
    for copy in first:
        cp.arrived(copy)
    low = land[:, :width]
    attended[...] = low
    step = 256
    squares = jnp.zeros((rows, 1), F32)
    for c in range(0, width, step):
        part = tok[:, c : c + step].astype(F32) + live[...] * dot(low, w_out[:, c : c + step])
        residual[:, c : c + step] = part
        squares += jnp.sum(part * part, axis=1, keepdims=True)
    scale = lax.rsqrt(squares / width + EPS)
    hidden[...] = (residual[...] * scale * gain[...]).astype(BF)
    run_streams(gather_ep(cp, place, hidden, hidden_all, width))
    cp.finish()


def call_b(heads, tok, live, w_out, gain):
    anyspace = pl.BlockSpec(memory_space=pl.ANY)
    vmem = pl.BlockSpec(memory_space=pltpu.VMEM)
    rows, width = tok.shape
    return pl.pallas_call(
        kernel_b,
        out_shape=(
            jax.ShapeDtypeStruct((rows, width), F32),
            jax.ShapeDtypeStruct((rows, width), BF),
            jax.ShapeDtypeStruct((8, rows, width), BF),
        ),
        in_specs=[anyspace, vmem, vmem, vmem, vmem],
        out_specs=(vmem, vmem, anyspace),
        scratch_shapes=[
            pltpu.VMEM((rows, 8 * heads.shape[2]), BF),
            pltpu.VMEM((rows, width), BF),
            pltpu.SemaphoreType.DMA((32,)),
            pltpu.SemaphoreType.DMA((32,)),
        ],
        compiler_params=pltpu.CompilerParams(
            collective_id=1, has_side_effects=True, vmem_limit_bytes=VMEM_LIMIT
        ),
        name="attention_out",
    )(heads, tok, live, w_out, gain)


def add_into(out, terms):
    lead = out.shape[:-2]
    rows = out.shape[-2]

    for index in itertools.product(*(range(n) for n in lead)):

        @pl.loop(0, rows // ROW_PAD)
        def _(i):
            at = index + (pl.ds(pl.multiple_of(i * ROW_PAD, ROW_PAD), ROW_PAD),)
            total = terms[0][at].astype(F32)
            for term in terms[1:]:
                total += term[at].astype(F32)
            out[at] = total.astype(out.dtype)


class Grid:
    def __init__(self, ring, pair, up, down, over):
        self.here, self.up_at, self.down_at, self.far = ring, (ring + 1) % 4, (ring + 3) % 4, (ring + 2) % 4
        self.pair, self.other = pair, 1 - pair
        self.up, self.down, self.over = up, down, over


def grid_rep(place):
    return Grid(place.y, place.zl, place.to_y(1), place.to_y(-1), place.to_zl())


def grid_ep(place):
    return Grid(place.x, place.zh, place.to_x(1), place.to_x(-1), place.to_zh())


def ring_pair_bufs(rows, columns):
    return [pltpu.VMEM((8, rows, columns), BF)]


def sum_ring_pair(cp, g, source, mine, bufs, out):
    (buf,) = bufs
    near, last, half, over = (0, 1), ((2, 3), (4, 5)), 6, 7
    b = lambda i: buf.at[i]
    s1 = cp.send(source.at[g.far, 0], b(near[0]), g.up)
    s2 = cp.send(source.at[g.far, 1], b(near[1]), g.down)
    s3 = cp.send(source.at[g.up_at, 1], b(last[0][1]), g.up)
    s4 = cp.send(source.at[g.down_at, 0], b(last[1][0]), g.down)
    yield
    cp.arrived(s1)
    add_into(mine.at[g.up_at, 0], [mine.at[g.up_at, 0], b(near[0])])
    s5 = cp.send(mine.at[g.up_at, 0], b(last[0][0]), g.up)
    cp.arrived(s2)
    add_into(mine.at[g.down_at, 1], [mine.at[g.down_at, 1], b(near[1])])
    s6 = cp.send(mine.at[g.down_at, 1], b(last[1][1]), g.down)
    yield
    for copy in (s3, s4, s5, s6):
        cp.arrived(copy)
    add_into(
        b(half),
        [mine.at[g.here, g.other], buf.at[2 + g.other], buf.at[4 + g.other]],
    )
    s7 = cp.send(b(half), b(over), g.over)
    yield
    cp.arrived(s7)
    add_into(
        out, [mine.at[g.here, g.pair], buf.at[2 + g.pair], buf.at[4 + g.pair], b(over)]
    )
    for copy in (s1, s2, s3, s4, s5, s6, s7):
        cp.sent_off(copy)


def pair_ring_bufs(rows, columns):
    cut = half_columns(columns)
    return [
        pltpu.VMEM((4, rows, columns), BF),
        pltpu.VMEM((2, rows, columns), BF),
        pltpu.VMEM((rows, cut), BF),
        pltpu.VMEM((rows, columns - cut), BF),
    ]


def sum_pair_ring(cp, g, source, mine, bufs, out):
    acc, last, near_lo, near_hi = bufs
    columns = acc.shape[2]
    cut = half_columns(columns)
    lo, hi = pl.ds(0, cut), pl.ds(cut, columns - cut)
    s0 = cp.send(source.at[:, g.other], acc, g.over)
    yield
    cp.arrived(s0)
    for k in range(4):
        add_into(acc.at[k], [acc.at[k], mine.at[k, g.pair]])
    s1 = cp.send(acc.at[g.far, :, lo], near_lo, g.up)
    s2 = cp.send(acc.at[g.far, :, hi], near_hi, g.down)
    s3 = cp.send(acc.at[g.up_at, :, hi], last.at[0, :, hi], g.up)
    s4 = cp.send(acc.at[g.down_at, :, lo], last.at[1, :, lo], g.down)
    yield
    cp.arrived(s1)
    part = acc.at[g.up_at, :, lo]
    add_into(part, [part, near_lo])
    s5 = cp.send(part, last.at[0, :, lo], g.up)
    cp.arrived(s2)
    part = acc.at[g.down_at, :, hi]
    add_into(part, [part, near_hi])
    s6 = cp.send(part, last.at[1, :, hi], g.down)
    yield
    for copy in (s3, s4, s5, s6):
        cp.arrived(copy)
    add_into(out, [acc.at[g.here], last.at[0], last.at[1]])


def gather_expert(cp, place, src, dst, z_first):
    core, y, zl = place.core, place.y, place.zl
    other = 1 - zl
    columns = src.shape[1]
    cut = half_columns(columns)
    lo, hi = pl.ds(0, cut), pl.ds(cut, columns - cut)
    up, down, over, mate = place.to_y(1), place.to_y(-1), place.to_zl(), place.to_core()

    def at(k, z):
        return dst.at[core, (y + k) % 4, z]

    def forward(k, z, to):
        return cp.send(at(k, z), at(k, z), to)

    def ring_halves(z):
        a = cp.send(at(-1, z).at[:, lo], at(-1, z).at[:, lo], up)
        b = cp.send(at(1, z).at[:, hi], at(1, z).at[:, hi], down)
        return a, b

    own = cp.local(src, at(0, zl))
    first = [cp.send(src, at(0, zl), to) for to in (up, down)]
    across = cp.send(src, at(0, zl), over)
    cp.send(src, at(0, zl), mate)
    yield
    if z_first:
        cp.arrived(across)
        second = [forward(0, other, to) for to in (up, down)]
        forward(0, other, mate)
        yield
        halves = []
        for pair, z in ((first, zl), (second, other)):
            for copy in pair:
                cp.arrived(copy)
            halves.append(ring_halves(z))
            forward(-1, z, mate)
            forward(1, z, mate)
            yield
        for pair, z in zip(halves, (zl, other)):
            for copy in pair:
                cp.arrived(copy)
            forward(2, z, mate)
            yield
    else:
        for copy in first:
            cp.arrived(copy)
        halves = ring_halves(zl)
        crossed = [across]
        for k in (-1, 1):
            crossed.append(forward(k, zl, over))
            forward(k, zl, mate)
        yield
        for copy in halves:
            cp.arrived(copy)
        crossed.append(forward(2, zl, over))
        forward(2, zl, mate)
        yield
        for copy, k in zip(crossed, (0, -1, 1, 2)):
            cp.arrived(copy)
            forward(k, other, mate)
            yield
    cp.arrived(own)


def expert_stream(cp, place, grad, tiles, got, bufs, total, dst, ring_first):
    b = cp.send(grad.at[1 - place.core], got, place.to_core())
    places = list(itertools.product(range(4), range(2)))
    load = lambda n: cp.local(grad.at[(place.core,) + places[n]], tiles.at[n % 2])
    yield
    loads = [load(0), load(1)]
    cp.arrived(b)
    for n, at in enumerate(places):
        cp.arrived(loads[n])
        add_into(got.at[at], [got.at[at], tiles.at[n % 2]])
        if n + 2 < len(places):
            loads.append(load(n + 2))
    summed = sum_ring_pair if ring_first else sum_pair_ring
    yield from summed(cp, grid_rep(place), got, got, bufs, total)
    yield from gather_expert(cp, place, total, dst, ring_first)


def dense_stream(cp, place, grad, got, bufs, total, ring_first):
    b = cp.send(grad.at[:, :, 1 - place.core], got, place.to_core())
    yield
    cp.arrived(b)
    own = grad.at[:, :, place.core]
    add_into(got, [got, own])
    summed = sum_ring_pair if ring_first else sum_pair_ring
    yield from summed(cp, grid_rep(place), got, got, bufs, total)


def spread_stream(cp, place, stream, total, padded, result):
    yield from stream
    used = total.shape[0] // 8
    spread = spread_matrix(8 * used, 8, used).astype(BF)
    columns = total.shape[1]
    for c in range(0, columns, 128):
        padded[:, :, c : c + 128] = (
            dot_tn(spread, total[:, c : c + 128]).astype(BF).reshape(8, ROW_PAD, 128)
        )
    cp.local(padded.at[place.ep], result.at[place.ep])
    for k in range(1, 8):
        cp.send(padded.at[(place.ep + k) % 8], result.at[place.ep], place.to_ep(k))


def advance(*streams):
    for stream in streams:
        next(stream, None)


def kernel_back(
    grads, outs, eg, eu, ed, d_shared, d_down, h_probs, h_hidden, h_qkv,
    w_slices, residual, cot, tok, live, probs, attended, w_whole, gain_one, gain_two, cosine, sine,
    out, d_tok, x_gate, x_up, x_down, o_qkv, o_shared, o_whole, o_down,
    m_grads, m_outs, b_grads, b_outs, total_grads, total_hidden,
    e_own, e_got, e_bufs, e_total,
    v_shared, v_whole, v_qkv, v_down, got, bufs, totals, padded,
    g_att, g_heads, g_residual, g_keys, g_values, g_qkv, v_probs, v_hidden, v_qkvs, v_w, g_branch,
    send_sem, recv_sem,
):
    place = Place()
    cp = Copies(send_sem, recv_sem)
    greet(ep_peers(place) + rep_peers(place))
    rows, width = residual.shape
    mine = place.ep
    ge = grid_ep(place)
    wide = width + EXTRA
    cuts = (pl.ds(0, wide // 2 // 128 * 128), pl.ds(wide // 2 // 128 * 128, wide - wide // 2 // 128 * 128))

    def view(ref, c):
        return ref.at[:, :, :, c]

    load = cp.local(grads, m_grads)
    xs = [
        sum_ring_pair(cp, ge, view(grads, c), view(m_grads, c), b, total_grads.at[:, c])
        for c, b in zip(cuts, b_grads)
    ]
    advance(*xs)
    es = [
        expert_stream(cp, place, g, own, got_, b, t, x, first)
        for g, own, got_, b, t, x, first in zip(
            (eg, eu, ed), (e_own[0], e_own[0], e_own[1]), e_got, e_bufs, e_total, (x_gate, x_up, x_down), (True, True, False)
        )
    ]
    advance(*es)
    loads = [
        cp.local(a, b)
        for a, b in (
            (d_shared, v_shared), (d_down, v_down), (h_hidden, v_hidden), (h_qkv, v_qkvs), (h_probs, v_probs),
            (w_slices.at[:, : v_w.shape[1]], v_w),
        )
    ]
    cp.arrived(load)
    advance(es[0], es[1])
    advance(*xs)
    advance(es[2])
    advance(*xs)
    advance(es[0])
    advance(*xs)

    alive = live[...]
    router_grad = total_grads[:, width:] * alive
    prob = probs[...]
    logit_grad = prob * (router_grad - jnp.sum(prob * router_grad, axis=1, keepdims=True))
    step = 256
    squares = jnp.zeros((rows, 1), F32)
    mean_k = jnp.zeros((rows, 1), F32)
    for c in range(0, width, step):
        part = residual[:, c : c + step]
        squares += jnp.sum(part * part, axis=1, keepdims=True)
    scale = lax.rsqrt(squares / width + EPS)
    gain_rows = []
    for c in range(0, width, step):
        k = total_grads[:, c : c + step] + lax.dot_general(
            logit_grad, w_whole[c : c + step, width:].astype(F32), (((1,), (1,)), ((), ())),
            preferred_element_type=F32, precision=HIGH,
        )
        normed = residual[:, c : c + step] * scale
        gain_rows.append(jnp.sum(k * normed, axis=0, keepdims=True))
        k = k * gain_two[:, c : c + step]
        mean_k += jnp.sum(k * normed, axis=1, keepdims=True)
        g_residual[:, c : c + step] = k
    mean_k = mean_k / width
    for c in range(0, width, step):
        normed = residual[:, c : c + step] * scale
        grad = cot[:, c : c + step].astype(F32) + scale * (
            g_residual[:, c : c + step] - normed * mean_k
        )
        g_residual[:, c : c + step] = grad
        g_branch[:, c : c + step] = (alive * grad).astype(BF)
    g_att[...] = jnp.zeros_like(g_att)
    low = g_branch[...]
    for c in range(0, width, step):
        g_att[c // step] = dot_nt(low, w_whole[c : c + step, :width]).astype(BF)
    third = [cp.local(g_att.at[mine], g_heads.at[mine])]
    for k in range(1, 8):
        third.append(cp.send(g_att.at[(mine + k) % 8], g_heads.at[mine], place.to_ep(k)))

    advance(es[1])
    for i in range(2):
        c = slice(i * width // 2, (i + 1) * width // 2)
        v_whole[2 * i : 2 * i + 2, :, :, :, :width] = (
            dot_tn(attended[:, c], low).astype(BF).reshape(2, 2, 2, width // 16, width)
        )
        hid = (residual[:, c] * scale * gain_two[:, c]).astype(BF).astype(F32)
        small = lax.dot_general(
            hid, logit_grad, (((0,), (0,)), ((), ())), preferred_element_type=F32, precision=HIGH
        )
        gain_row = jnp.concatenate(gain_rows, axis=1)[:, c]
        lane = lax.broadcasted_iota(jnp.int32, (width // 2, EXTRA), 1)
        column = jnp.broadcast_to(gain_row, (8, width // 2)).T[:, :1]
        small = jnp.where(lane == EXTRA - 1, column, small)
        v_whole[2 * i : 2 * i + 2, :, :, :, width:] = small.astype(BF).reshape(
            2, 2, 2, width // 16, EXTRA
        )
    for copy in loads:
        cp.arrived(copy)
    dense = [
        dense_stream(cp, place, v, g, b, t, first)
        for v, g, b, t, first in zip(
            (v_whole, v_shared, v_down, v_qkv), got, bufs, totals, (False, True, True, True)
        )
    ]
    ds = [
        spread_stream(cp, place, dense[0], totals[0], padded[0], o_whole),
        spread_stream(cp, place, dense[1], totals[1], padded[1], o_shared),
        dense[2],
        spread_stream(cp, place, dense[3], totals[3], padded[2], o_qkv),
    ]
    advance(*ds[:3])
    load = cp.local(outs, m_outs)
    os = sum_ring_pair(cp, ge, outs, m_outs, b_outs, total_hidden)
    advance(os)
    advance(es[2], es[0])
    for copy in third:
        cp.arrived(copy)

    group = 8 * rows
    span = HEADS_DEV * HD
    for h in range(HEADS_DEV):
        attention_back_head(h, g_heads, v_qkvs, v_probs, cosine, sine, g_keys, g_values, g_qkv)
        if h == 0:
            cp.arrived(load)
        advance(*ds[:3])
        advance(*es)
        advance(os)

    @pl.loop(0, group // BLOCK)
    def _(i):
        at = pl.ds(pl.multiple_of(i * BLOCK, BLOCK), BLOCK)
        part = dot_nt(g_qkv[at, :], v_w[...]).astype(BF)
        m_grads[i, :, :, :width] = part.reshape(2, rows, width)

    half = width // 2 // 128 * 128
    hcuts = (pl.ds(0, half), pl.ds(half, width - half))
    b_hidden = [[b.at[:, :, pl.ds(0, c.size)]] for (b,), c in zip(b_grads, hcuts)]
    advance(os)
    for c in range(0, width, step):
        out[:, c : c + step] = (residual[:, c : c + step] + total_hidden[:, c : c + step]).astype(BF)
    hs = [
        sum_ring_pair(cp, ge, view(m_grads, c), view(m_grads, c), b, total_hidden.at[:, c])
        for c, b in zip(hcuts, b_hidden)
    ]
    advance(*hs)
    for i in range(2):
        c = slice(i * width // 2, (i + 1) * width // 2)
        v_qkv[2 * i : 2 * i + 2] = (
            dot_tn(v_hidden[:, c], g_qkv[...]).astype(BF).reshape(2, 2, 2, width // 16, 3 * span)
        )
    advance(ds[3])
    advance(*es)
    advance(hs[0], ds[3], hs[1], *ds[:3])
    advance(*es)
    advance(hs[0], ds[3], hs[1], *ds[:3])
    advance(*es)
    advance(hs[0], hs[1])
    squares = jnp.zeros((rows, 1), F32)
    mean_k = jnp.zeros((rows, 1), F32)
    for c in range(0, width, step):
        part = tok[:, c : c + step].astype(F32)
        squares += jnp.sum(part * part, axis=1, keepdims=True)
    scale = lax.rsqrt(squares / width + EPS)
    for c in range(0, width, step):
        normed = tok[:, c : c + step].astype(F32) * scale
        k = total_hidden[:, c : c + step] * gain_one[:, c : c + step]
        mean_k += jnp.sum(k * normed, axis=1, keepdims=True)
    mean_k = mean_k / width
    for c in range(0, width, step):
        normed = tok[:, c : c + step].astype(F32) * scale
        k = total_hidden[:, c : c + step] * gain_one[:, c : c + step]
        d_tok[:, c : c + step] = g_residual[:, c : c + step] + scale * (k - normed * mean_k)
    run_streams(ds[3], *ds[:3], *es, os, *hs, *xs)
    o_down[...] = totals[2][...]
    cp.finish()


def call_back(
    grads, outs, eg, eu, ed, d_shared, d_down, h_probs, h_hidden, h_qkv,
    w_slices, residual, cot, tok, live, probs, attended, w_whole, gain_one, gain_two, cosine, sine,
):
    anyspace = pl.BlockSpec(memory_space=pl.ANY)
    vmem = pl.BlockSpec(memory_space=pltpu.VMEM)
    rows, width = residual.shape
    group = rows * 8
    span = HEADS_DEV * HD
    wide = width + EXTRA
    cut = wide // 2 // 128 * 128
    experts = [g.shape[3:] for g in (eg, eu, ed)]
    part = width // 16
    columns = (wide, d_shared.shape[4], width, 3 * span)
    depth = (part, part, ROW_PAD, part)
    orders = (False, True, True, True)
    bufs_of = lambda first, r, c: (ring_pair_bufs if first else pair_ring_bufs)(r, c)
    return pl.pallas_call(
        kernel_back,
        out_shape=(
            jax.ShapeDtypeStruct((rows, width), BF),
            jax.ShapeDtypeStruct((rows, width), F32),
            jax.ShapeDtypeStruct(eg.shape, BF),
            jax.ShapeDtypeStruct(eu.shape, BF),
            jax.ShapeDtypeStruct(ed.shape, BF),
            jax.ShapeDtypeStruct((8, ROW_PAD, 3 * span), BF),
            jax.ShapeDtypeStruct((8, ROW_PAD, columns[1]), BF),
            jax.ShapeDtypeStruct((8, ROW_PAD, wide), BF),
            jax.ShapeDtypeStruct((ROW_PAD, width), BF),
        ),
        in_specs=[anyspace] * 11 + [vmem] * 11,
        out_specs=(vmem, vmem) + (anyspace,) * 6 + (vmem,),
        scratch_shapes=[
            pltpu.VMEM((4, 2, rows, wide), BF),
            pltpu.VMEM((4, 2, rows, width), BF),
            [ring_pair_bufs(rows, c) for c in (cut, wide - cut)],
            ring_pair_bufs(rows, width),
            pltpu.VMEM((rows, wide), F32),
            pltpu.VMEM((rows, width), F32),
            [pltpu.VMEM((2,) + s, BF) for s in experts[1:]],
            [pltpu.VMEM((4, 2) + s, BF) for s in experts],
            [bufs_of(first, *s) for first, s in zip((True, True, False), experts)],
            [pltpu.VMEM(s, BF) for s in experts],
            pltpu.VMEM(d_shared.shape, BF),
            pltpu.VMEM((4, 2, 2, part, wide), BF),
            pltpu.VMEM((4, 2, 2, part, 3 * span), BF),
            pltpu.VMEM(d_down.shape, BF),
            [pltpu.VMEM((4, 2, r, c), BF) for r, c in zip(depth, columns)],
            [bufs_of(first, r, c) for first, r, c in zip(orders, depth, columns)],
            [pltpu.VMEM((r, c), BF) for r, c in zip(depth, columns)],
            [pltpu.VMEM((8, ROW_PAD, columns[i]), BF) for i in (0, 1, 3)],
            pltpu.VMEM((8, rows, span), BF),
            pltpu.VMEM((8, rows, span), BF),
            pltpu.VMEM((rows, width), F32),
            pltpu.VMEM((group, HD), F32),
            pltpu.VMEM((group, HD), F32),
            pltpu.VMEM((group, 3 * span), BF),
            pltpu.VMEM(h_probs.shape, BF),
            pltpu.VMEM(h_hidden.shape, BF),
            pltpu.VMEM(h_qkv.shape, BF),
            pltpu.VMEM((width, 3 * span), BF),
            pltpu.VMEM((rows, width), BF),
            pltpu.SemaphoreType.DMA((320,)),
            pltpu.SemaphoreType.DMA((320,)),
        ],
        compiler_params=pltpu.CompilerParams(
            collective_id=2, has_side_effects=True, vmem_limit_bytes=int(63.9 * 2**20)
        ),
        name="backward",
    )(
        grads, outs, eg, eu, ed, d_shared, d_down, h_probs, h_hidden, h_qkv,
        w_slices, residual, cot, tok, live, probs, attended, w_whole, gain_one, gain_two, cosine, sine,
    )


BLOCK = 256


def turn(values, cosine, sine):
    return values * cosine + pltpu.roll(values, HD // 2, 1) * sine


def attention_forward(tok, gain, w_slices, live, cosine, sine, hidden, qkv, probs, heads):
    group, width = hidden.shape
    span = HEADS_DEV * HD

    @pl.loop(0, group // BLOCK)
    def _(i):
        at = pl.ds(pl.multiple_of(i * BLOCK, BLOCK), BLOCK)
        values = tok[at, :width].astype(F32)
        scale = lax.rsqrt(jnp.sum(values * values, axis=1, keepdims=True) / width + EPS)
        low = (values * scale * gain[...]).astype(BF)
        hidden[at, :] = low
        raw = dot(low, w_slices[:, : 3 * span])
        cos, sin = cosine[at, :], sine[at, :]
        for h in range(2 * HEADS_DEV):
            c = slice(h * HD, (h + 1) * HD)
            qkv[at, c] = turn(raw[:, c], cos, sin).astype(BF)
        qkv[at, 2 * span :] = raw[:, 2 * span :].astype(BF)

    rows = lax.broadcasted_iota(jnp.int32, (BLOCK, BLOCK), 0)
    columns = lax.broadcasted_iota(jnp.int32, (BLOCK, BLOCK), 1)
    for h in range(HEADS_DEV):
        q, k, v = (slice(n * span + h * HD, n * span + (h + 1) * HD) for n in range(3))
        for i in range(group // BLOCK):
            at = slice(i * BLOCK, (i + 1) * BLOCK)
            n = (i + 1) * BLOCK
            scores = dot_nt(qkv[at, q], qkv[:n, k]) * HD**-0.5
            parts = []
            for j in range(i + 1):
                alive = live[:, j * BLOCK : (j + 1) * BLOCK] > 0.5
                if j == i:
                    alive = (alive & (columns < rows)) | (columns == rows)
                parts.append(jnp.where(alive, scores[:, j * BLOCK : (j + 1) * BLOCK], -1e30))
            scores = jnp.concatenate(parts, axis=1) if len(parts) > 1 else parts[0]
            top = jnp.max(scores, axis=1, keepdims=True)
            weights = jnp.exp(scores - top)
            low = (weights * (1.0 / jnp.sum(weights, axis=1, keepdims=True))).astype(BF)
            probs[h, at, :n] = low
            heads[at, h * HD : (h + 1) * HD] = dot(low, qkv[:n, v]).astype(BF)


def call_attention(tok, gain, w_slices, live, cosine, sine, width):
    group = tok.shape[0]
    vmem = pl.BlockSpec(memory_space=pltpu.VMEM)
    span = HEADS_DEV * HD
    return pl.pallas_call(
        attention_forward,
        out_shape=(
            jax.ShapeDtypeStruct((group, width), BF),
            jax.ShapeDtypeStruct((group, 3 * span), BF),
            jax.ShapeDtypeStruct((HEADS_DEV, group, group), BF),
            jax.ShapeDtypeStruct((group, span), BF),
        ),
        in_specs=[vmem] * 6,
        out_specs=(vmem,) * 4,
        compiler_params=pltpu.CompilerParams(vmem_limit_bytes=VMEM_LIMIT),
        name="attention_forward",
    )(tok, gain, w_slices, live, cosine, sine)


def attention_back_head(h, g_heads, qkv, probs, cosine, sine, g_keys, g_values, g_qkv):
    group = qkv.shape[0]
    blocks, rows = g_heads.shape[:2]
    per = BLOCK // rows
    span = HEADS_DEV * HD
    scale = HD**-0.5
    q, k, v = (slice(n * span + h * HD, n * span + (h + 1) * HD) for n in range(3))
    head = slice(h * HD, (h + 1) * HD)
    for i in reversed(range(group // BLOCK)):
        at = slice(i * BLOCK, (i + 1) * BLOCK)
        n = (i + 1) * BLOCK
        g_att = g_heads[i * per : (i + 1) * per, :, head].reshape(BLOCK, HD)
        low = probs[h, at, :n]
        weights = low.astype(F32)
        g_probs = dot_nt(g_att, qkv[:n, v])
        delta = jnp.sum(weights * g_probs, axis=1, keepdims=True)
        g_scores = (weights * (g_probs - delta)).astype(BF)
        g_query = dot(g_scores, qkv[:n, k]) * scale
        g_qkv[at, q] = turn(g_query, cosine[at, :], -sine[at, :]).astype(BF)
        g_key = dot_tn(g_scores, qkv[at, q])
        g_value = dot_tn(low, g_att)
        if i == group // BLOCK - 1:
            g_keys[...] = g_key
            g_values[...] = g_value
        else:
            g_keys[:n, :] += g_key
            g_values[:n, :] += g_value
    g_qkv[:, k] = turn(g_keys[...] * scale, cosine[...], -sine[...]).astype(BF)
    g_qkv[:, v] = g_values[...].astype(BF)


def one_expert(x, g, w_gate, w_up, w_down, weight, mask, wact, g_a, g_b, out, g_x, q_sum, first):
    group, width = g.shape

    @pl.loop(0, group // BLOCK)
    def _(i):
        at = pl.ds(pl.multiple_of(i * BLOCK, BLOCK), BLOCK)
        share = weight(at)
        gate = dot(x[at, :], w_gate[...])
        up = dot(x[at, :], w_up[...])
        raw = dot_nt(g[at, :], w_down[...])
        sig = 1.0 / (1.0 + jnp.exp(-gate))
        silu = gate * sig
        act = silu * up
        if q_sum is not None:
            q_sum(at, jnp.sum(act * raw, axis=1, keepdims=True))
        low = (act * share).astype(BF)
        wact[at, :] = low
        raw = raw * share
        a = (raw * up * (sig + silu * (1.0 - sig))).astype(BF)
        b = (raw * silu).astype(BF)
        g_a[at, :] = a
        g_b[at, :] = b
        part = dot(low, w_down[...])
        back = dot_nt(a, w_gate[...]) + dot_nt(b, w_up[...])
        if first:
            out[at, :] = part.astype(BF)
            g_x[at, :width] = back.astype(BF)
        else:
            out[at, :] = (out[at, :].astype(F32) + part).astype(BF)
            g_x[at, :width] = (g_x[at, :width].astype(F32) + back).astype(BF)


def expert_sums(x, g, wact, g_a, g_b, d_gate, d_up, d_down):
    width = g.shape[1]
    for c in range(0, width, BLOCK):
        left = x[:, c : c + BLOCK]
        d_gate[c : c + BLOCK, :] = dot_tn(left, g_a[...]).astype(BF)
        d_up[c : c + BLOCK, :] = dot_tn(left, g_b[...]).astype(BF)
    hidden = wact.shape[1]
    step = 128
    for c in range(0, hidden, step):
        d_down[c : c + step, :] = dot_tn(wact[:, c : c + step], g[...]).astype(BF)


def experts_kernel(
    experts, top,
    x, g, extra, w_router, s_both, s_padded, e_gate, e_up, e_down,
    out, g_x, probs_own, d_both, d_padded, d_gate, d_up, d_down,
    gates, named, wact, g_a, g_b, swact, sg_a, sg_b, s_down, d_sdown,
):
    step = pl.program_id(0)
    ep = lax.axis_index("ep")
    group, width = g.shape
    exp_dev = pl.num_programs(0)
    expert = ep * exp_dev + step
    lane = lax.broadcasted_iota(jnp.int32, (BLOCK, EXTRA), 1)

    @pl.when(step == 0)
    def _():
        @pl.loop(0, group // BLOCK)
        def _(i):
            at = pl.ds(pl.multiple_of(i * BLOCK, BLOCK), BLOCK)
            logits = jnp.where(lane < experts, dot(x[at, :], w_router[...]), -1e30)
            weights = jnp.exp(logits - jnp.max(logits, axis=1, keepdims=True))
            prob = weights / jnp.sum(weights, axis=1, keepdims=True)
            routes = extra[at, :].astype(F32).astype(jnp.int32)
            chosen = lane == routes[:, 0:1]
            for j in range(1, top):
                chosen = chosen | (lane == routes[:, j : j + 1])
            named[at, :] = jnp.where(chosen, 1.0, 0.0)
            live = extra[at, top : top + 1].astype(F32)
            gates[at, :] = jnp.where(chosen, prob, 0.0) * live
            g_x[at, width:] = jnp.zeros((BLOCK, EXTRA), BF)

        rows = group // 8
        mine = pl.ds(pl.multiple_of(ep * rows, rows), rows)
        own_lane = lane[:rows]
        logits = jnp.where(own_lane < experts, dot(x[mine, :], w_router[...]), -1e30)
        weights = jnp.exp(logits - jnp.max(logits, axis=1, keepdims=True))
        probs_own[...] = weights / jnp.sum(weights, axis=1, keepdims=True)
        shared = s_down.shape[0]
        used = shared // 16 * 7 // 8
        pack = spread_matrix(shared, 16, used).astype(BF)
        s_down[...] = dot(pack, s_padded[...]).astype(BF)
        one_expert(
            x, g, s_both.at[:, :shared], s_both.at[:, shared:], s_down,
            lambda at: extra[at, top : top + 1].astype(F32),
            None, swact, sg_a, sg_b, out, g_x, None, True,
        )
        expert_sums(x, g, swact, sg_a, sg_b, d_both.at[:, :shared], d_both.at[:, shared:], d_sdown)
        d_padded[...] = dot_tn(pack, d_sdown[...]).astype(BF)

    def picked(ref, at):
        return jnp.sum(jnp.where(lane == expert, ref[at, :], 0.0), axis=1, keepdims=True)

    def q_sum(at, value):
        g_x[at, width:] = jnp.where(
            lane == expert, value * named[at, :], g_x[at, width:].astype(F32)
        ).astype(BF)

    one_expert(
        x, g, e_gate.at[0], e_up.at[0], e_down.at[0], lambda at: picked(gates, at),
        None, wact, g_a, g_b, out, g_x, q_sum, False,
    )
    expert_sums(x, g, wact, g_a, g_b, d_gate.at[0], d_up.at[0], d_down.at[0])


def call_experts(x, g, extra, w_router, s_both, s_padded, e_gate, e_up, e_down, experts, top):
    group, width = x.shape
    exp_dev, _, hidden = e_gate.shape
    rows = group // 8
    once = lambda shape: pl.BlockSpec(shape, lambda i: (0,) * len(shape), pipeline_mode=pl.Buffered(1))
    per = lambda a: pl.BlockSpec((1,) + a.shape[1:], lambda i: (i, 0, 0))
    shared = s_both.shape[1] // 2
    return pl.pallas_call(
        functools.partial(experts_kernel, experts, top),
        grid=(exp_dev,),
        out_shape=(
            jax.ShapeDtypeStruct((group, width), BF),
            jax.ShapeDtypeStruct((group, width + EXTRA), BF),
            jax.ShapeDtypeStruct((rows, EXTRA), F32),
            jax.ShapeDtypeStruct((width, 2 * shared), BF),
            jax.ShapeDtypeStruct(s_padded.shape, BF),
            jax.ShapeDtypeStruct(e_gate.shape, BF),
            jax.ShapeDtypeStruct(e_up.shape, BF),
            jax.ShapeDtypeStruct(e_down.shape, BF),
        ),
        in_specs=[once(a.shape) for a in (x, g, extra, w_router, s_both, s_padded)]
        + [per(a) for a in (e_gate, e_up, e_down)],
        out_specs=(
            once((group, width)), once((group, width + EXTRA)), once((rows, EXTRA)),
            once((width, 2 * shared)), once(s_padded.shape),
            per(e_gate), per(e_up), per(e_down),
        ),
        scratch_shapes=[pltpu.VMEM((group, EXTRA), F32)] * 2
        + [pltpu.VMEM((group, hidden), BF)] * 3
        + [pltpu.VMEM((group, shared), BF)] * 3
        + [pltpu.VMEM((shared, width), BF)] * 2,
        compiler_params=pltpu.CompilerParams(
            vmem_limit_bytes=VMEM_LIMIT, dimension_semantics=("arbitrary",)
        ),
        name="experts",
    )(x, g, extra, w_router, s_both, s_padded, e_gate, e_up, e_down)


def pad_rows(values, rows):
    return jnp.pad(values, ((0, rows - values.shape[0]),) + ((0, 0),) * (values.ndim - 1))


def body(
    tokens, cotangent, lengths, token_mask, routes,
    w_query, w_key, w_value, w_output, w_router,
    shared_gate, shared_up, shared_down, norm_attn, norm_ffn,
    expert_gate, expert_up, expert_down,
):
    rows, width = tokens.shape
    top = routes.shape[1]
    used = w_query.shape[0]
    hidden = expert_gate.shape[2]
    experts = w_router.shape[1]
    exp_dev = expert_gate.shape[0]
    ep = lax.axis_index("ep")
    group = rows * 8
    span = HEADS_DEV * HD
    owners = width // span
    down_used = shared_down.shape[0]
    shared_cols = 16 * down_used

    def by_owner(w):
        return jnp.pad(w.reshape(used, owners, span), ((0, 0), (0, 8 - owners), (0, 0)))

    def by_shared(w):
        w = w.reshape(used, 16, 8, down_used).transpose(0, 2, 1, 3).reshape(used, 8, shared_cols)
        return jnp.pad(w, ((0, 0), (0, 0), (0, 128 - shared_cols)))

    slices = jnp.concatenate(
        [by_owner(w_query), by_owner(w_key), by_owner(w_value), by_shared(shared_gate), by_shared(shared_up)],
        axis=2,
    ).transpose(1, 0, 2)
    slices = jnp.pad(slices, ((0, 0), (0, ROW_PAD - used), (0, 0)))
    whole = jnp.concatenate(
        [w_output, w_router, norm_attn[:, None], norm_ffn[:, None]], axis=1
    )
    whole = jnp.pad(whole, ((0, ROW_PAD - used), (0, width + EXTRA - whole.shape[1])))
    down = pad_rows(shared_down, ROW_PAD)
    position = ep * rows + jnp.arange(rows, dtype=jnp.int32)
    live_own = ((position < lengths[0]) & (token_mask == 1)).astype(F32)
    tok_wide = jnp.concatenate(
        [
            tokens,
            jnp.pad(
                jnp.concatenate([routes.astype(BF), live_own[:, None].astype(BF)], axis=1),
                ((0, 0), (0, EXTRA - top - 1)),
            ),
        ],
        axis=1,
    )
    tok_all, cot_all, w_slices, w_whole, w_down = call_a(
        slices, whole, down, tok_wide, cotangent, used
    )
    tok_all = tok_all.reshape(group, width + EXTRA)
    cot_all = cot_all.reshape(group, width)
    w_slices = w_slices.reshape(width, -1)
    w_whole = w_whole.reshape(width, -1)
    w_down = w_down.reshape(-1, width)
    live_row = tok_all[:, width + top].astype(F32)[None]
    gain_one = w_whole[:, width + experts].astype(F32)[None]
    gain_two = w_whole[:, width + experts + 1].astype(F32)[None]
    router = w_whole[:, width:]

    frequency = 10000.0 ** (-(np.arange(HD // 2, dtype=np.float32) * np.float32(2.0) / HD))
    angles = np.arange(group, dtype=np.float32)[:, None] * frequency.astype(np.float32)[None, :]
    cosine = jnp.asarray(np.tile(np.cos(angles), (1, 2)), F32)
    sine = jnp.asarray(np.concatenate([-np.sin(angles), np.sin(angles)], axis=1), F32)
    hidden_one, qkv, attn_probs, heads = call_attention(
        tok_all, gain_one, w_slices, live_row, cosine, sine, width
    )

    live_col = live_own[:, None]
    residual, attended, hidden_all = call_b(
        heads.reshape(8, rows, span), tokens, live_col, w_whole, gain_two
    )
    hidden_all = hidden_all.reshape(group, width)
    out_part, grad_wide, probs_own, d_both, d_down, d_eg, d_eu, d_ed = call_experts(
        hidden_all, cot_all, tok_all[:, width:], router, w_slices[:, 3 * span :], w_down,
        expert_gate, expert_up, expert_down, experts, top,
    )
    part = width // 16
    out, d_tokens, e_gate, e_up, e_down, o_qkv, o_shared, o_whole, o_down = call_back(
        grad_wide.reshape(4, 2, rows, width + EXTRA),
        out_part.reshape(4, 2, rows, width),
        d_eg.reshape(exp_dev, 4, 2, width // 8, hidden),
        d_eu.reshape(exp_dev, 4, 2, width // 8, hidden),
        d_ed.reshape(exp_dev, 4, 2, hidden // 8, width),
        d_both.reshape(4, 2, 2, part, -1),
        d_down.reshape(4, 2, 2, ROW_PAD, width),
        attn_probs, hidden_one, qkv,
        w_slices, residual, cotangent, tokens, live_col, probs_own, attended, w_whole,
        gain_one, gain_two, cosine, sine,
    )
    o_qkv = o_qkv[:owners, :used].astype(F32)
    o_shared = o_shared[:, :used].astype(F32)
    o_whole = jnp.sum(o_whole[:, :used].astype(F32), axis=0)

    def from_owner(i):
        return o_qkv[:, :, i * span : (i + 1) * span].transpose(1, 0, 2).reshape(used, width)

    def from_shared(i):
        return (
            o_shared[:, :, 128 * i : 128 * i + shared_cols]
            .reshape(8, used, 16, down_used)
            .transpose(1, 2, 0, 3)
            .reshape(used, hidden)
        )

    d_query, d_key, d_value = (from_owner(i) for i in range(3))
    d_gain_one = sum(
        jnp.sum(w.astype(F32) * d, axis=1)
        for w, d in ((w_query, d_query), (w_key, d_key), (w_value, d_value))
    ) / norm_attn.astype(F32)
    return (
        out,
        d_tokens,
        d_query,
        d_key,
        d_value,
        o_whole[:, :width],
        o_whole[:, width : width + experts],
        from_shared(0),
        from_shared(1),
        o_down[:down_used].astype(F32),
        d_gain_one,
        o_whole[:, width + EXTRA - 1],
        e_gate.reshape(exp_dev, width, hidden).astype(F32),
        e_up.reshape(exp_dev, width, hidden).astype(F32),
        e_down.reshape(exp_dev, hidden, width).astype(F32),
    )


def solution(mesh):
    both = ("rep", "ep")
    row = P(both, None)
    expert = P("ep", None, None)
    in_specs = (
        row, row, P("rep"), P(both), row, row, row, row, row, row, row, row, row,
        P(both), P(both), expert, expert, expert,
    )
    out_specs = (
        row, row, row, row, row, row, row, row, row, row, P(both), P(both),
        expert, expert, expert,
    )
    return jax.shard_map(body, mesh=mesh, in_specs=in_specs, out_specs=out_specs, check_vma=False)
```

time: 594 us -> 444 us (0.75)
  matrix products: 148 us -> 0 us
  Pallas kernels: 313 us -> 378 us
  local copies, waits for them, and re-layouts: 74.9 us -> 25.3 us
  other arithmetic: 46.3 us -> 31.4 us
    dot_general x29 -> x0, matrix products: 139 us -> none  [the longest x1 15.1 us: body(): jnp.einsum('td,edf->etf', hidden_all, expert_up, preferred_element_type=F32)]
    pallas_call x2 -> x3, Pallas kernels: 211 us -> 276 us  [the longest x1 185 us: call_back(): pl.pallas_call(kernel_back, out_shape=(jax.ShapeDtypeStruct((rows, width)...]
    convert_element_type x4 -> x2, local copies, waits for them, and re-layouts: 16.5 us -> 1.19 us  [the longest x1 0.6 us: body(): gain_two = w_whole[:, width + experts + 1].astype(F32)[None]]
    concatenate x5 -> x0, local copies, waits for them, and re-layouts: 12.5 us -> none  [the longest x3 9.46 us: body(): jnp.concatenate([d_out, d_router, d_gain_one[:, None], d_gain_two.reshape...]
    unnamed x140 -> x24, local copies, waits for them, and re-layouts: 11 us -> 1.77 us
    sub x1 -> x0, matrix products: 8.94 us -> none  [body(): exponent = jnp.exp(scores - top_score)]
    convert_element_type x9 -> x4, other arithmetic: 13.8 us -> 5.15 us  [the longest x1 1.78 us: body(): live_row = tok_all[:, width + top].astype(F32)[None]]
    convert_element_type x1, other arithmetic: 4.61 us -> 11.6 us  [body(): e_up.reshape(exp_dev, width, hidden).astype(F32)]
where the time goes in v2:
time: 444 us; the launch traced here: 437 us
  Pallas kernels  378 us (85%)
  other arithmetic  31.4 us (7%)
  local copies, waits for them, and re-layouts  25.3 us (6%)
    pallas_call x1, Pallas kernels, call_back(): pl.pallas_call(kernel_back, out_shape=(jax.ShapeDtypeStruct((rows, width)...  185 us
    pallas_call x1, Pallas kernels, call_experts(): pl.pallas_call(functools.partial(experts_kernel, experts, top), grid=(exp...  77.9 us
    pallas_call x1, Pallas kernels, call_a(): pl.pallas_call(kernel_a, out_shape=(jax.ShapeDtypeStruct((8,) + tok.shape...  66.5 us
    pallas_call x1, Pallas kernels, call_b(): pl.pallas_call(kernel_b, out_shape=(jax.ShapeDtypeStruct((rows, width), F...  36.1 us
    pallas_call x1, Pallas kernels, call_attention(): pl.pallas_call(attention_forward, out_shape=(jax.ShapeDtypeStruct((group,...  12.7 us
    convert_element_type x1, other arithmetic, body(): e_up.reshape(exp_dev, width, hidden).astype(F32)  11.6 us

profile of v2, /device:TPU:1, one launch (start us, length us, event | category | flops | bytes accessed | tf_op | source)
XLA Modules:
  0.0 436.8 jit_solution(14190412962609118219)
XLA Ops:
  2.7 0.7 copy.73
  3.4 0.8 copy.72
  4.3 0.9 concatenate.13
  5.8 1.4 pad.40.down
  7.1 0.8 reshape.160
  8.0 0.8 reshape.161
  8.8 0.8 reshape.162
  9.7 0.7 copy.75.live
  10.5 1.7 fusion.1.tok
  12.2 1.3 reshape.163
  13.9 1.3 reshape.165
  16.4 66.5 %gather_inputs.1 = (bf16[8,128,1408]{2,1,0:T(8,128)(2,1)}, bf16[8,128,1280]{2,1,0:T(8,128)(2,1)}, bf16[16,80,1024]{2,1,0:T(8,128)(2,1)}, bf16[16,80,1408]{2,1,0:T(8,128)(2,1)}, bf16[16,16,1280]{2,1,0:T(8,128)(2,1)}) custom-call(bf16[8,16,1024]{2,1,0:T(8,128)(2,1)} %pad.38.slices, bf16[16,1408]{1,0:T(8,128)(2,1)} %pad.39.whole, bf16[16,1280]{1,0:T(8,128)(2,1)} %pad.40.down, ...), custom_call_target="tpu_custom_call" | custom-call | tf_op jit(solution)/shard_map/gather_inputs/pallas_call | solution.py:302
  82.9 1.8 convert_reduce_fusion.3
  84.7 1.6 convert_reduce_fusion.1
  87.5 1.7 slice.75.extra
  89.2 1.7 slice.76.w_router
  90.9 2.0 slice.77.s_both
  92.8 12.7 %attention_forward.1 = (bf16[1024,1280]{1,0:T(8,128)(2,1)}, bf16[1024,768]{1,0:T(8,128)(2,1)}, bf16[2,1024,1024]{2,1,0:T(8,128)(2,1)}, bf16[1024,256]{1,0:T(8,128)(2,1)}) custom-call(bf16[1024,1408]{1,0:T(8,128)(2,1)} %bitcast.79, f32[1,1280]{1,0:T(1,128)} %reshape.188.gain.gain_one, bf16[1280,1024]{1,0:T(8,128)(2,1)} %bitcast.72, f32[1,1024]{1,0:T(1,128)} %bitcast.102, ...), custom_call_target="tpu_custom_call" | custom-call | tf_op jit(solution)/shard_map/attention_forward/pallas_call | solution.py:911
  105.5 36.1 %attention_out.1 = (f32[128,1280]{1,0:T(8,128)}, bf16[128,1280]{1,0:T(8,128)(2,1)}, bf16[8,128,1280]{2,1,0:T(8,128)(2,1)}) custom-call(bf16[8,128,256]{2,1,0:T(8,128)(2,1)} %bitcast.91, bf16[128,1280]{1,0:T(8,128)(2,1)} %tok.3, f32[128,1]{1,0:T(8,128)} %copy.75.live, bf16[1280,1408]{1,0:T(8,128)(2,1)} %bitcast.69, f32[1,1280]{1,0:T(1,128)} %reshape.190.gain.gain_two), custom_call_target="tpu_custom_call" | custom-call | tf_op jit(solution)/shard_map/attention_out/pallas_call | solution.py:363
  141.6 77.9 %experts.1 = (bf16[1024,1280]{1,0:T(8,128)(2,1)}, bf16[1024,1408]{1,0:T(8,128)(2,1)}, f32[128,128]{1,0:T(8,128)}, bf16[1280,256]{1,0:T(8,128)(2,1)}, bf16[256,12...) custom-call(bf16[1024,1280]{1,0:T(8,128)(2,1)} %bitcast.82, ...), custom_call_target="tpu_custom_call" | custom-call | tf_op jit(solution)/shard_map/experts/pallas_call | solution.py:1071
  219.5 185.1 %backward.1 = (bf16[128,1280]{1,0:T(8,128)(2,1)}, f32[128,1280]{1,0:T(8,128)}, bf16[2,4,2,160,896]{4,3,2,1,0:T(8,128)(2,1)}, bf16[2,4,2,160,896]{4,3,2,1,0:T(8,1...) custom-call(bf16[4,2,128,1408]{3,2,1,0:T(8,128)(2,1)} %bitcast.80, ...), custom_call_target="tpu_custom_call" | custom-call | tf_op jit(solution)/shard_map/backward/pallas_call | solution.py:802
  404.6 1.3 slice_convert_fusion.2
  405.9 1.1 convert_reduce_fusion
  408.9 0.8 slice_convert_fusion.1
  409.8 0.9 slice_convert_fusion
  411.0 1.0 multiply_reduce_fusion
  412.1 0.9 multiply_reduce_fusion.2
  414.1 1.0 reshape.185
  415.7 1.0 reshape.187
  416.7 6.7 %bitcast_convert_fusion = f32[2,896,1280]{2,1,0:T(8,128)} fusion(bf16[2,4,2,112,1280]{4,3,2,1,0:T(8,128)(2,1)} %get-tuple-element.72), kind=kLoop, calls=%fused_computation | loop fusion | flops 2293760 | bytes 13762560 | tf_op jit(solution)/shard_map/convert_element_type | solution.py:1232
  423.4 11.6 %bitcast_convert_fusion.1 = (f32[2,1280,896]{2,1,0:T(8,128)}, f32[2,1280,896]{2,1,0:T(8,128)}) fusion(bf16[2,4,2,160,896]{4,3,2,1,0:T(8,128)(2,1)} %get-tuple-element.71, bf16[2,4,2,160,896]{4,3,2,1,0:T(8,128)(2,1)} %get-tuple-element.70), kind=kLoop, calls=%fused_computation.1 | loop fusion | flops 4587520 | bytes 27525120 | tf_op jit(solution)/shard_map/convert_element_type | solution.py:1231
  435.7 0.8 copy.99
  (54 shorter events, 9.5 us)
Async XLA Ops:
  219.5 193.5 %copy-start.5 = (bf16[10]{0:T(256)(128)(2,1)S(1)}, bf16[10]{0:T(256)(128)(2,1)}, u32[]{:S(2)}) copy-start(bf16[10]{0:T(256)(128)(2,1)} %param.33) | copy-start | bytes 64
  410.9 12.5 %copy-start.3 = (f32[2,8,5,256]{3,1,2,0:T(8,128)}, f32[2,8,5,256]{3,1,2,0:T(8,128)S(1)}, u32[]{:S(2)}) copy-start(f32[2,8,5,256]{3,1,2,0:T(8,128)S(1)} %copy.90) | copy-start | bytes 245764
  411.0 12.4 %copy-start.4 = (f32[2,8,5,256]{3,1,2,0:T(8,128)}, f32[2,8,5,256]{3,1,2,0:T(8,128)S(1)}, u32[]{:S(2)}) copy-start(f32[2,8,5,256]{3,1,2,0:T(8,128)S(1)} %copy.89) | copy-start | bytes 245764
  412.1 11.3 %copy-start.2 = (f32[2,8,5,256]{3,1,2,0:T(8,128)}, f32[2,8,5,256]{3,1,2,0:T(8,128)S(1)}, u32[]{:S(2)}) copy-start(f32[2,8,5,256]{3,1,2,0:T(8,128)S(1)} %copy.88) | copy-start | bytes 245764
  423.4 11.6 %copy-start.1 = (bf16[128,1280]{1,0:T(8,128)(2,1)S(1)}, bf16[128,1280]{1,0:T(8,128)(2,1)}, u32[]{:S(2)}) copy-start(bf16[128,1280]{1,0:T(8,128)(2,1)} %get-tuple-element.101) | copy-start | bytes 983044
  423.4 12.4 %copy-start = (f32[128,1280]{1,0:T(8,128)S(1)}, f32[128,1280]{1,0:T(8,128)}, u32[]{:S(2)}) copy-start(f32[128,1280]{1,0:T(8,128)} %get-tuple-element.102) | copy-start | bytes 1966084

commit v3 on v2

v3 whole, which is shorter than its diff:
```python
import functools
import itertools
import math

import jax
import jax.numpy as jnp
import numpy as np
from jax import lax
from jax.experimental import pallas as pl
from jax.experimental.pallas import tpu as pltpu
from jax.sharding import PartitionSpec as P

HD = 128
EPS = 1e-6
BF = jnp.bfloat16
F32 = jnp.float32
MESH = pl.DeviceIdType.MESH
HIGH = lax.Precision.HIGHEST
HEADS_DEV = 2
EXTRA = 128
ROW_PAD = 16
VMEM_LIMIT = 60 << 20
LIVE = 7


def dot(a, b):
    return jnp.dot(a, b, preferred_element_type=F32)


def dot_nt(a, b):
    return lax.dot_general(a, b, (((1,), (1,)), ((), ())), preferred_element_type=F32)


def dot_tn(a, b):
    return lax.dot_general(a, b, (((0,), (0,)), ((), ())), preferred_element_type=F32)


class Place:
    def __init__(self):
        self.rep = lax.axis_index("rep")
        self.ep = lax.axis_index("ep")
        self.y = self.rep // 4
        self.zl = (self.rep // 2) % 2
        self.core = self.rep % 2
        self.x = self.ep // 2
        self.zh = self.ep % 2

        self.mate = 1 - self.core
        self.y_at = {k: (self.y + k) % 4 for k in (-1, 0, 1, 2)}
        self._x = {k: (self.rep, self.ep_at(self.x + k, self.zh)) for k in (-1, 1)}
        self._y = {k: (self.rep_at(self.y + k, self.zl, self.core), self.ep) for k in (-1, 1)}
        self._ep = {k: (self.rep, (self.ep + k) % 8) for k in range(1, 8)}
        self._zh = (self.rep, self.ep_at(self.x, 1 - self.zh))
        self._zl = (self.rep_at(self.y, 1 - self.zl, self.core), self.ep)
        self._core = (self.rep_at(self.y, self.zl, self.mate), self.ep)

    def rep_at(self, y, zl, core):
        return (y % 4) * 4 + zl * 2 + core

    def ep_at(self, x, zh):
        return (x % 4) * 2 + zh

    def to_x(self, step):
        return self._x[step]

    def to_zh(self):
        return self._zh

    def to_ep(self, shift):
        return self._ep[shift]

    def to_y(self, step):
        return self._y[step]

    def to_zl(self):
        return self._zl

    def to_core(self):
        return self._core


class Later:
    def __init__(self, ref, path=()):
        self.ref, self.path = ref, path

    @property
    def at(self):
        return LaterAt(self)

    @property
    def shape(self):
        return self.made().shape

    @property
    def dtype(self):
        return self.ref.dtype

    def made(self):
        ref = self.ref
        for index in self.path:
            ref = ref.at[index]
        return ref

    def __getitem__(self, index):
        return self.made()[index]

    def __setitem__(self, index, value):
        self.made()[index] = value


class LaterAt:
    def __init__(self, later):
        self.later = later

    def __getitem__(self, index):
        return Later(self.later.ref, self.later.path + (index,))


def made(ref):
    return ref.made() if isinstance(ref, Later) else ref


class Copies:
    def __init__(self, send_sem, recv_sem):
        self.send_sem, self.recv_sem = send_sem, recv_sem
        self.number = itertools.count()
        self.sent, self.open = [], []

    def send(self, src, dst, device):
        i = next(self.number)

        def copy():
            return pltpu.make_async_remote_copy(
                src_ref=made(src),
                dst_ref=made(dst),
                send_sem=self.send_sem.at[i],
                recv_sem=self.recv_sem.at[i],
                device_id=device,
                device_id_type=MESH,
            )

        copy().start()
        self.sent.append(copy)
        self.open.append(copy)
        return copy

    def local(self, src, dst):
        i = next(self.number)

        def copy():
            return pltpu.make_async_copy(made(src), made(dst), self.recv_sem.at[i])

        copy().start()
        self.open.append(copy)
        return copy

    def arrived(self, copy):
        if any(copy is c for c in self.sent):
            copy().wait_recv()
        else:
            copy().wait()
        self.open = [c for c in self.open if c is not copy]

    def sent_off(self, copy):
        copy().wait_send()
        self.sent = [c for c in self.sent if c is not copy]

    def drain(self, stream):
        for _ in stream:
            pass

    def finish(self):
        for copy in list(self.open):
            self.arrived(copy)
        for copy in list(self.sent):
            self.sent_off(copy)


def greet(devices):
    barrier = pltpu.get_barrier_semaphore()
    for device in devices:
        pl.semaphore_signal(barrier, inc=1, device_id=device, device_id_type=MESH)
    pl.semaphore_wait(barrier, len(devices))


def run_streams(*streams):
    live = list(streams)
    while live:
        for stream in list(live):
            try:
                next(stream)
            except StopIteration:
                live.remove(stream)


def half_columns(columns):
    return (columns // 128 + 1) // 2 * 128


def ep_peers(place):
    return [place.to_ep(k) for k in range(1, 8)]


def rep_peers(place):
    return [place.to_y(1), place.to_y(-1), place.to_zl(), place.to_core()]


def gather_ep(cp, place, src, dst, columns):
    cut = half_columns(columns)
    lo, hi = pl.ds(0, cut), pl.ds(cut, columns - cut)
    mine = place.ep
    own = cp.local(src, dst.at[mine])
    right = cp.send(src, dst.at[mine], place.to_x(1))
    left = cp.send(src, dst.at[mine], place.to_x(-1))
    over = cp.send(src, dst.at[mine], place.to_zh())
    yield
    from_left = place.ep_at(place.x - 1, place.zh)
    from_right = place.ep_at(place.x + 1, place.zh)
    from_over = place.ep_at(place.x, 1 - place.zh)
    far = place.ep_at(place.x + 2, place.zh)
    cp.arrived(right)
    half_a = cp.send(dst.at[from_left, :, lo], dst.at[from_left, :, lo], place.to_x(1))
    cp.arrived(left)
    half_b = cp.send(dst.at[from_right, :, hi], dst.at[from_right, :, hi], place.to_x(-1))
    yield
    cp.arrived(over)
    last = [own]
    last.append(cp.send(dst.at[from_over], dst.at[from_over], place.to_x(1)))
    last.append(cp.send(dst.at[from_over], dst.at[from_over], place.to_x(-1)))
    yield
    cp.arrived(half_a)
    cp.arrived(half_b)
    last.append(cp.send(dst.at[far], dst.at[far], place.to_zh()))
    yield
    for copy in last:
        cp.arrived(copy)


def gather_ring_y(cp, place, src, dst, columns, slot):
    cut = half_columns(columns)
    lo, hi = pl.ds(0, cut), pl.ds(cut, columns - cut)
    up = cp.send(src, dst.at[slot(place.y)], place.to_y(1))
    down = cp.send(src, dst.at[slot(place.y)], place.to_y(-1))
    yield
    cp.arrived(up)
    below = slot(place.y - 1)
    half_a = cp.send(dst.at[below, :, lo], dst.at[below, :, lo], place.to_y(1))
    cp.arrived(down)
    above = slot(place.y + 1)
    half_b = cp.send(dst.at[above, :, hi], dst.at[above, :, hi], place.to_y(-1))
    yield
    cp.arrived(half_a)
    cp.arrived(half_b)


def gather_rep(cp, place, src, dst, columns, z_first):
    mine = place.rep
    last = [cp.local(src, dst.at[mine]), cp.send(src, dst.at[mine], place.to_core())]

    def slot(zl):
        return lambda y: place.rep_at(y, zl, place.core)

    def pass_core(index):
        last.append(cp.send(dst.at[index], dst.at[index], place.to_core()))

    here, there = slot(place.zl), slot(1 - place.zl)
    if z_first:
        over = cp.send(src, dst.at[mine], place.to_zl())
        first = gather_ring_y(cp, place, src, dst, columns, here)
        next(first)
        yield
        cp.arrived(over)
        second = gather_ring_y(
            cp, place, dst.at[there(place.y)], dst, columns, there
        )
        next(second)
        pass_core(there(place.y))
        yield
        next(first)
        for k in (-1, 1):
            pass_core(here(place.y + k))
        yield
        next(second)
        for k in (-1, 1):
            pass_core(there(place.y + k))
        yield
        next(first, None)
        pass_core(here(place.y + 2))
        yield
        next(second, None)
        pass_core(there(place.y + 2))
    else:
        over = [cp.send(src, dst.at[mine], place.to_zl())]
        ring = gather_ring_y(cp, place, src, dst, columns, here)
        next(ring)
        yield
        next(ring)
        for k in (-1, 1):
            block = dst.at[here(place.y + k)]
            over.append(cp.send(block, block, place.to_zl()))
            pass_core(here(place.y + k))
        yield
        next(ring, None)
        block = dst.at[here(place.y + 2)]
        over.append(cp.send(block, block, place.to_zl()))
        pass_core(here(place.y + 2))
        yield
        for copy, k in zip(over, (0, -1, 1, 2)):
            cp.arrived(copy)
            pass_core(there(place.y + k))
            yield
    yield
    for copy in last:
        cp.arrived(copy)


def spread_matrix(rows, blocks, used):
    shape = (rows, blocks * ROW_PAD)
    to = lax.broadcasted_iota(jnp.int32, shape, 0)
    at = lax.broadcasted_iota(jnp.int32, shape, 1)
    return jnp.where((at // ROW_PAD) * used + at % ROW_PAD == to, 1.0, 0.0) * jnp.where(
        at % ROW_PAD < used, 1.0, 0.0
    )


def kernel_front(
    slices, whole, down, tok, cot, live, cosine, sine,
    w_slices, w_both, w_whole, w_router, w_down, cot_all, extra,
    hidden_one, qkv, probs, gains, residual, attended, hidden_all,
    land_slices, land_whole, pack_slices, pack_whole, v_slices, v_whole, v_tok,
    heads, land_heads, hidden, live_row, send_sem, recv_sem,
):
    place = Place()
    cp = Copies(send_sem, recv_sem)
    greet(ep_peers(place) + rep_peers(place))
    rows = tok.shape[0]
    width = cot.shape[1]
    group = 8 * rows
    span = HEADS_DEV * HD
    mine = place.ep

    to_slices = [cp.local(slices.at[mine], land_slices.at[mine])]
    to_whole = [cp.local(whole, land_whole.at[mine])]
    for k in range(1, 8):
        to_slices.append(cp.send(slices.at[(mine + k) % 8], land_slices.at[mine], place.to_ep(k)))
    for k in range(1, 8):
        to_whole.append(cp.send(whole, land_whole.at[mine], place.to_ep(k)))
    toks = gather_ep(cp, place, tok, v_tok, tok.shape[1])
    advance(toks)
    downs = gather_rep(cp, place, down, w_down, down.shape[1], True)
    advance(downs)
    used = pack_slices.shape[0] // 8
    spread = spread_matrix(8 * used, 8, used).astype(BF)

    def pack(land, packed):
        for c in range(0, land.shape[2], 128):
            block = land[:, :, c : c + 128].reshape(8 * ROW_PAD, 128)
            packed[:, c : c + 128] = dot(spread, block).astype(BF)

    for copy in to_slices:
        cp.arrived(copy)
    pack(land_slices, pack_slices)
    sls = gather_rep(cp, place, pack_slices, v_slices, slices.shape[2], True)
    advance(sls)
    for copy in to_whole:
        cp.arrived(copy)
    pack(land_whole, pack_whole)
    advance(toks)
    whs = gather_rep(cp, place, pack_whole, v_whole, whole.shape[1], True)
    advance(sls, whs, toks, sls, toks)
    cots = gather_ep(cp, place, cot, cot_all, width)
    advance(whs, sls)
    cp.drain(toks)
    advance(cots)
    cp.drain(sls)
    outs = [
        cp.local(v_slices, w_slices),
        cp.local(v_slices.at[:, :, pl.ds(3 * span, 256)], w_both),
        cp.local(v_tok.at[:, :, pl.ds(width, EXTRA)], extra),
    ]

    block = v_slices[:, :, 3 * span : 3 * span + 128].reshape(width, 128).astype(F32).T
    gains[...] = block[112:120, :]
    live_row[...] = jnp.concatenate(
        [v_tok[i, :, width:].astype(F32).T[:8, :] for i in range(8)], axis=1
    )
    weights = lambda: v_slices[:, :, : 3 * span].reshape(width, 3 * span)
    per = BLOCK // rows

    @pl.loop(0, group // BLOCK)
    def _(i):
        at = pl.ds(pl.multiple_of(i * BLOCK, BLOCK), BLOCK)
        values = v_tok[pl.ds(i * per, per), :, :width].reshape(BLOCK, width).astype(F32)
        scale = lax.rsqrt(jnp.sum(values * values, axis=1, keepdims=True) / width + EPS)
        low = (values * scale * gains[0:1, :]).astype(BF)
        hidden_one[at, :] = low
        raw = dot(low, weights())
        cos, sin = cosine[at, :], sine[at, :]
        for h in range(2 * HEADS_DEV):
            c = slice(h * HD, (h + 1) * HD)
            qkv[at, c] = turn(raw[:, c], cos, sin).astype(BF)
        qkv[at, 2 * span :] = raw[:, 2 * span :].astype(BF)

    advance(whs, cots)
    for h in range(HEADS_DEV):
        attention_head(h, qkv, live_row, probs, heads)
        advance(whs, cots, downs)
    column = pl.ds(pl.multiple_of(mine * span, 128), span)
    first = [cp.local(heads.at[mine], land_heads.at[:, column])]
    for k in range(1, 8):
        first.append(cp.send(heads.at[(mine + k) % 8], land_heads.at[:, column], place.to_ep(k)))
    cp.drain(whs)
    outs += [
        cp.local(v_whole, w_whole),
        cp.local(v_whole.at[:, :, pl.ds(width, EXTRA)], w_router),
    ]
    advance(cots, downs)
    for copy in first:
        cp.arrived(copy)

    low = land_heads[:, :width]
    attended[...] = low
    step = 256
    squares = jnp.zeros((rows, 1), F32)
    for c in range(0, width, step):
        matrix = v_whole[:, :, c : c + step].reshape(width, step)
        part = tok[:, c : c + step].astype(F32) + live[...] * dot(low, matrix)
        residual[:, c : c + step] = part
        squares += jnp.sum(part * part, axis=1, keepdims=True)
    scale = lax.rsqrt(squares / width + EPS)
    hidden[...] = (residual[...] * scale * gains[1:2, :]).astype(BF)
    run_streams(gather_ep(cp, place, hidden, hidden_all, width), cots, downs)
    cp.finish()


def call_front(slices, whole, down, tok, cot, live, cosine, sine, used):
    anyspace = pl.BlockSpec(memory_space=pl.ANY)
    vmem = pl.BlockSpec(memory_space=pltpu.VMEM)
    rows, width = cot.shape
    group = 8 * rows
    span = HEADS_DEV * HD
    shape = jax.ShapeDtypeStruct
    columns, wide = slices.shape[2], whole.shape[1]
    return pl.pallas_call(
        kernel_front,
        out_shape=(
            shape((16, 8 * used, columns), BF),
            shape((16, 8 * used, columns - 3 * span), BF),
            shape((16, 8 * used, wide), BF),
            shape((16, 8 * used, EXTRA), BF),
            shape((16,) + down.shape, BF),
            shape((8,) + cot.shape, BF),
            shape((8, rows, EXTRA), BF),
            shape((group, width), BF),
            shape((group, 3 * span), BF),
            shape((HEADS_DEV, group, group), BF),
            shape((8, width), F32),
            shape((rows, width), F32),
            shape((rows, width), BF),
            shape((8, rows, width), BF),
        ),
        in_specs=[anyspace] * 3 + [vmem] + [anyspace] + [vmem] * 3,
        out_specs=(anyspace,) * 7 + (vmem,) * 6 + (anyspace,),
        scratch_shapes=[
            pltpu.VMEM((8, ROW_PAD, columns), BF),
            pltpu.VMEM((8, ROW_PAD, wide), BF),
            pltpu.VMEM((8 * used, columns), BF),
            pltpu.VMEM((8 * used, wide), BF),
            pltpu.VMEM((16, 8 * used, columns), BF),
            pltpu.VMEM((16, 8 * used, wide), BF),
            pltpu.VMEM((8,) + tok.shape, BF),
            pltpu.VMEM((8, rows, span), BF),
            pltpu.VMEM((rows, 8 * span), BF),
            pltpu.VMEM((rows, width), BF),
            pltpu.VMEM((8, group), F32),
            pltpu.SemaphoreType.DMA((200,)),
            pltpu.SemaphoreType.DMA((200,)),
        ],
        compiler_params=pltpu.CompilerParams(
            collective_id=0, has_side_effects=True, vmem_limit_bytes=VMEM_LIMIT
        ),
        name="front",
    )(slices, whole, down, tok, cot, live, cosine, sine)


def add_into(out, terms):
    lead = out.shape[:-2]
    count = math.prod(lead)

    def add(index):
        if len(terms) == 2 and out.dtype == BF:
            out[index] = terms[0][index] + terms[1][index]
            return
        total = terms[0][index].astype(F32)
        for term in terms[1:]:
            total += term[index].astype(F32)
        out[index] = total.astype(out.dtype)

    if count == 1:
        add((0,) * len(lead) + (slice(None),))
    else:
        inner = lead[-1] if lead else 1

        @pl.loop(0, count)
        def _(i):
            add(((i // inner, i % inner) if len(lead) == 2 else (i,)) + (slice(None),))


class Grid:
    def __init__(self, ring, pair, up, down, over):
        self.here, self.up_at, self.down_at, self.far = ring, (ring + 1) % 4, (ring + 3) % 4, (ring + 2) % 4
        self.pair, self.other = pair, 1 - pair
        self.up, self.down, self.over = up, down, over


def grid_rep(place):
    return Grid(place.y, place.zl, place.to_y(1), place.to_y(-1), place.to_zl())


def grid_ep(place):
    return Grid(place.x, place.zh, place.to_x(1), place.to_x(-1), place.to_zh())


def ring_pair_bufs(rows, columns):
    return [pltpu.VMEM((7, rows, columns), BF)]


def sum_ring_pair(cp, g, source, mine, bufs, out, more=()):
    (buf,) = bufs
    near, last, half, over = (0, 1), ((2, 3), (4, 5)), 0, 6
    b = lambda i: buf.at[i]
    s1 = cp.send(source.at[g.far, 0], b(near[0]), g.up)
    s2 = cp.send(source.at[g.far, 1], b(near[1]), g.down)
    s3 = cp.send(source.at[g.up_at, 1], b(last[0][1]), g.up)
    s4 = cp.send(source.at[g.down_at, 0], b(last[1][0]), g.down)
    yield
    cp.arrived(s1)
    add_into(mine.at[g.up_at, 0], [mine.at[g.up_at, 0], b(near[0])])
    s5 = cp.send(mine.at[g.up_at, 0], b(last[0][0]), g.up)
    cp.arrived(s2)
    add_into(mine.at[g.down_at, 1], [mine.at[g.down_at, 1], b(near[1])])
    s6 = cp.send(mine.at[g.down_at, 1], b(last[1][1]), g.down)
    yield
    for copy in (s3, s4, s5, s6):
        cp.arrived(copy)
    add_into(
        b(half),
        [mine.at[g.here, g.other], buf.at[2 + g.other], buf.at[4 + g.other]],
    )
    s7 = cp.send(b(half), b(over), g.over)
    yield
    cp.arrived(s7)
    add_into(
        out, [mine.at[g.here, g.pair], buf.at[2 + g.pair], buf.at[4 + g.pair], b(over), *more]
    )
    for copy in (s1, s2, s3, s4, s5, s6, s7):
        cp.sent_off(copy)


def pair_ring_bufs(rows, columns):
    cut = half_columns(columns)
    return [
        pltpu.VMEM((4, rows, columns), BF),
        pltpu.VMEM((2, rows, columns), BF),
        pltpu.VMEM((rows, cut), BF),
        pltpu.VMEM((rows, columns - cut), BF),
    ]


def sum_pair_ring(cp, g, source, mine, bufs, out):
    acc, last, near_lo, near_hi = bufs
    columns = acc.shape[2]
    cut = half_columns(columns)
    lo, hi = pl.ds(0, cut), pl.ds(cut, columns - cut)
    s0 = cp.send(source.at[:, g.other], acc, g.over)
    yield
    cp.arrived(s0)
    add_into(acc, [acc, mine.at[:, g.pair]])
    s1 = cp.send(acc.at[g.far, :, lo], near_lo, g.up)
    s2 = cp.send(acc.at[g.far, :, hi], near_hi, g.down)
    s3 = cp.send(acc.at[g.up_at, :, hi], last.at[0, :, hi], g.up)
    s4 = cp.send(acc.at[g.down_at, :, lo], last.at[1, :, lo], g.down)
    yield
    cp.arrived(s1)
    part = acc.at[g.up_at, :, lo]
    add_into(part, [part, near_lo])
    s5 = cp.send(part, last.at[0, :, lo], g.up)
    cp.arrived(s2)
    part = acc.at[g.down_at, :, hi]
    add_into(part, [part, near_hi])
    s6 = cp.send(part, last.at[1, :, hi], g.down)
    yield
    for copy in (s3, s4, s5, s6):
        cp.arrived(copy)
    add_into(out, [acc.at[g.here], last.at[0], last.at[1]])
    for copy in (s0, s1, s2, s3, s4, s5, s6):
        cp.sent_off(copy)


def gather_expert(cp, place, grid, src, at, z_first):
    zl, other = grid.pair, grid.other
    columns = src.shape[1]
    cut = half_columns(columns)
    lo, hi = pl.ds(0, cut), pl.ds(cut, columns - cut)
    up, down, over, mate = place.to_y(1), place.to_y(-1), place.to_zl(), place.to_core()

    def forward(k, z, to):
        return cp.send(at(k, z), at(k, z), to)

    def ring_halves(z):
        a = cp.send(at(-1, z).at[:, lo], at(-1, z).at[:, lo], up)
        b = cp.send(at(1, z).at[:, hi], at(1, z).at[:, hi], down)
        return a, b

    own = cp.local(src, at(0, zl))
    first = [cp.send(src, at(0, zl), to) for to in (up, down)]
    across = cp.send(src, at(0, zl), over)
    cp.send(src, at(0, zl), mate)
    yield
    if z_first:
        cp.arrived(across)
        second = [forward(0, other, to) for to in (up, down)]
        forward(0, other, mate)
        yield
        halves = []
        for pair, z in ((first, zl), (second, other)):
            for copy in pair:
                cp.arrived(copy)
            halves.append(ring_halves(z))
            forward(-1, z, mate)
            forward(1, z, mate)
            yield
        for pair, z in zip(halves, (zl, other)):
            for copy in pair:
                cp.arrived(copy)
            forward(2, z, mate)
            yield
    else:
        for copy in first:
            cp.arrived(copy)
        halves = ring_halves(zl)
        crossed = [across]
        for k in (-1, 1):
            crossed.append(forward(k, zl, over))
            forward(k, zl, mate)
        yield
        for copy in halves:
            cp.arrived(copy)
        crossed.append(forward(2, zl, over))
        forward(2, zl, mate)
        yield
        for copy, k in zip(crossed, (0, -1, 1, 2)):
            cp.arrived(copy)
            forward(k, other, mate)
            yield
    cp.arrived(own)


def expert_stream(cp, place, grid, sent, kept, got, bufs, total, at, ring_first, free, again):
    neighbours = rep_peers(place)
    if again:
        pl.semaphore_wait(free, len(neighbours))
    b = cp.send(sent, got, place.to_core())
    yield
    cp.arrived(b)
    add_into(got, [got, kept])
    cp.sent_off(b)
    summed = sum_ring_pair if ring_first else sum_pair_ring
    yield from summed(cp, grid, got, got, bufs, total)
    if not again:
        for device in neighbours:
            pl.semaphore_signal(free, inc=1, device_id=device, device_id_type=MESH)
    yield from gather_expert(cp, place, grid, total, at, True)


def dense_stream(cp, place, grid, grad, got, bufs, total, ring_first):
    b = cp.send(grad.at[:, :, 1 - place.core], got, place.to_core())
    yield
    cp.arrived(b)
    own = grad.at[:, :, place.core]
    add_into(got, [got, own])
    summed = sum_ring_pair if ring_first else sum_pair_ring
    yield from summed(cp, grid, got, got, bufs, total)


def spread_stream(cp, place, stream, total, padded, result):
    yield from stream
    used = total.shape[0] // 8
    spread = spread_matrix(8 * used, 8, used).astype(BF)
    columns = total.shape[1]
    for c in range(0, columns, 128):
        padded[:, :, c : c + 128] = (
            dot_tn(spread, total[:, c : c + 128]).astype(BF).reshape(8, ROW_PAD, 128)
        )
    cp.local(padded.at[place.ep], result.at[place.ep])
    for k in range(1, 8):
        cp.send(padded.at[(place.ep + k) % 8], result.at[place.ep], place.to_ep(k))


def advance(*streams):
    for stream in streams:
        next(stream, None)


BLOCK = 256


def turn(values, cosine, sine):
    return values * cosine + pltpu.roll(values, HD // 2, 1) * sine


def attention_head(h, qkv, live, probs, heads):
    group = qkv.shape[0]
    span = HEADS_DEV * HD
    per = BLOCK // heads.shape[1]
    rows = lax.broadcasted_iota(jnp.int32, (BLOCK, BLOCK), 0)
    columns = lax.broadcasted_iota(jnp.int32, (BLOCK, BLOCK), 1)
    q, k, v = (slice(n * span + h * HD, n * span + (h + 1) * HD) for n in range(3))
    for i in range(group // BLOCK):
        at = slice(i * BLOCK, (i + 1) * BLOCK)
        n = (i + 1) * BLOCK
        scores = dot_nt(qkv[at, q], qkv[:n, k]) * HD**-0.5
        parts = []
        for j in range(i + 1):
            alive = live[LIVE : LIVE + 1, j * BLOCK : (j + 1) * BLOCK] > 0.5
            if j == i:
                alive = (alive & (columns < rows)) | (columns == rows)
            parts.append(jnp.where(alive, scores[:, j * BLOCK : (j + 1) * BLOCK], -1e30))
        scores = jnp.concatenate(parts, axis=1) if len(parts) > 1 else parts[0]
        top = jnp.max(scores, axis=1, keepdims=True)
        weights = jnp.exp(scores - top)
        low = (weights * (1.0 / jnp.sum(weights, axis=1, keepdims=True))).astype(BF)
        probs[h, at, :n] = low
        heads[i * per : (i + 1) * per, :, h * HD : (h + 1) * HD] = (
            dot(low, qkv[:n, v]).astype(BF).reshape(per, BLOCK // per, HD)
        )


def attention_back_head(h, g_heads, qkv, probs, cosine, sine, g_keys, g_values, g_qkv):
    group = qkv.shape[0]
    blocks, rows = g_heads.shape[:2]
    per = BLOCK // rows
    span = HEADS_DEV * HD
    scale = HD**-0.5
    q, k, v = (slice(n * span + h * HD, n * span + (h + 1) * HD) for n in range(3))
    head = slice(h * HD, (h + 1) * HD)
    for i in reversed(range(group // BLOCK)):
        at = slice(i * BLOCK, (i + 1) * BLOCK)
        n = (i + 1) * BLOCK
        g_att = g_heads[i * per : (i + 1) * per, :, head].reshape(BLOCK, HD)
        low = probs[h, at, :n]
        weights = low.astype(F32)
        g_probs = dot_nt(g_att, qkv[:n, v])
        delta = jnp.sum(weights * g_probs, axis=1, keepdims=True)
        g_scores = (weights * (g_probs - delta)).astype(BF)
        g_query = dot(g_scores, qkv[:n, k]) * scale
        g_qkv[at, q] = turn(g_query, cosine[at, :], -sine[at, :]).astype(BF)
        g_key = dot_tn(g_scores, qkv[at, q])
        g_value = dot_tn(low, g_att)
        if i == group // BLOCK - 1:
            g_keys[...] = g_key
            g_values[...] = g_value
        else:
            g_keys[:n, :] += g_key
            g_values[:n, :] += g_value
    g_qkv[:, k] = turn(g_keys[...] * scale, cosine[...], -sine[...]).astype(BF)
    g_qkv[:, v] = g_values[...].astype(BF)


def store_rows(ref, lead, columns, row, value):
    depth = ref.shape[len(lead)]
    done = 0
    while done < value.shape[0]:
        block, offset = divmod(row + done, depth)
        take = min(depth - offset, value.shape[0] - done)
        at = tuple(int(i) for i in np.unravel_index(block, lead))
        ref[at + (slice(offset, offset + take), columns)] = value[done : done + take]
        done += take


def one_expert(blocks, x, g, w_gate, w_up, w_down, weight, wact, g_a, g_b, outs, grads, q_sum, first):
    width = g.shape[1]

    @pl.loop(*blocks)
    def _(i):
        at = pl.ds(pl.multiple_of(i * BLOCK, BLOCK), BLOCK)
        share = weight(at)
        gate = dot(x[at, :], w_gate[...])
        up = dot(x[at, :], w_up[...])
        raw = dot_nt(g[at, :], w_down[...])
        sig = 1.0 / (1.0 + jnp.exp(-gate))
        silu = gate * sig
        act = silu * up
        if q_sum is not None:
            q_sum(i, at, jnp.sum(act * raw, axis=1, keepdims=True))
        low = (act * share).astype(BF)
        wact[at, :] = low
        raw = raw * share
        a = (raw * up * (sig + silu * (1.0 - sig))).astype(BF)
        b = (raw * silu).astype(BF)
        g_a[at, :] = a
        g_b[at, :] = b
        shape = (2, BLOCK // 2, width)
        part = dot(low, w_down[...]).reshape(shape)
        back = (dot_nt(a, w_gate[...]) + dot_nt(b, w_up[...])).reshape(shape)
        if not first:
            part += outs[i].astype(F32)
            back += grads[i, :, :, :width].astype(F32)
        outs[i] = part.astype(BF)
        grads[i, :, :, :width] = back.astype(BF)


ORDER_A = (
    "p0", "g0", "u0", "d0", "G0", "sp", "G0", "U0", "D0", "q1", "G0", "U0", "r1", "G0",
    "U0", "D0", "x", "g1", "G0", "G0", "X0", "D0", "U0", "u1", "G0", "G0", "G1", "U0",
    "X1", "D0", "d1", "U0", "U1", "G0", "G0", "D0", "ss", "X0", "G1", "D1",
)
ORDER_B = (
    "X1", "U0", "X0", "D0", "U0", "U1", "D1", "D0", "G1", "X1", "n2", "U0", "U0", "D0",
    "G1", "U1", "dw", "D1", "sn", "D0", "D0", "G1", "o", "G1", "U1", "D1", "h0", "G1",
    "G1", "U1", "U1", "D1", "W", "S", "D1", "N", "O", "h1", "G1", "G1", "U1", "U1",
    "D1", "O", "hp", "D1", "S", "dq", "N", "U1", "U1", "H0", "D1", "D1", "S", "N",
    "Q", "W", "H1", "Q", "O", "S", "W", "N", "H0", "Q", "H1", "H0", "W", "Q",
    "H1", "n1",
)


def kernel_rest(
    experts, top,
    x_all, g_all, e_gate, e_up, e_down, h_probs, h_hidden, h_qkv, w_slices, h_whole,
    h_residual, h_cot, h_tok, h_attended, h_cosine, h_sine,
    extra, w_router, s_both, s_padded, live, gains,
    out, d_tok, x_gate, x_up, x_down, o_qkv, o_shared, o_whole, o_down,
    m_grads, m_outs, b_grads, b_outs, total_grads, total_hidden, e_got, e_bufs, e_total,
    v_shared, v_down, got, bufs, g_heads, probs, free, send_sem, recv_sem,
):
    place = Place()
    cp = Copies(send_sem, recv_sem)
    group, width = x_all.shape
    rows = group // 8
    mine, core = place.ep, place.core
    ge, gr = grid_ep(place), grid_rep(place)
    wide = width + EXTRA
    exp_dev, _, hidden = e_gate.shape
    span = HEADS_DEV * HD
    cut = wide // 2 // 128 * 128
    cuts = (pl.ds(0, cut), pl.ds(cut, wide - cut))
    m_grads, m_outs, total_grads, total_hidden, x_gate, x_up, x_down = (
        Later(ref) for ref in (m_grads, m_outs, total_grads, total_hidden, x_gate, x_up, x_down)
    )
    later = lambda refs: [Later(ref) if hasattr(ref, "at") else later(ref) for ref in refs]
    b_grads, b_outs, e_got, e_bufs, e_total = (
        later(refs) for refs in (b_grads, b_outs, e_got, e_bufs, e_total)
    )
    half_part = width // 16
    half = width // 2
    ours = pl.ds(pl.multiple_of(core * half, 128), half)
    theirs = pl.ds(pl.multiple_of(place.mate * half, 128), half)
    streams = {}

    def view(ref, c):
        return ref.at[:, :, :, c]

    def phase_a(
        x, g, w_gate, w_up, w_down, wact, g_a, g_b, gates, named,
        swact, sg_a, sg_b, s_down, d_sdown, d_gate, d_up, d_down,
    ):
        first = [cp.local(a, b) for a, b in ((x_all, x), (g_all, g))]
        weights = ((e_gate, w_gate), (e_up, w_up), (e_down, w_down))
        loads = [cp.local(a.at[0], b) for a, b in weights]
        greet(ep_peers(place) + rep_peers(place))
        for copy in first:
            cp.arrived(copy)
        lane = lax.broadcasted_iota(jnp.int32, (BLOCK, EXTRA), 1)

        def router(at, lanes):
            logits = jnp.where(lanes < experts, dot(x[at, :], w_router[...]), -1e30)
            weights = jnp.exp(logits - jnp.max(logits, axis=1, keepdims=True))
            return weights / jnp.sum(weights, axis=1, keepdims=True)

        @pl.loop(0, group // BLOCK)
        def _(i):
            at = pl.ds(pl.multiple_of(i * BLOCK, BLOCK), BLOCK)
            prob = router(at, lane)
            routes = extra[at, :].astype(F32).astype(jnp.int32)
            chosen = lane == routes[:, 0:1]
            for j in range(1, top):
                chosen = chosen | (lane == routes[:, j : j + 1])
            named[at, :] = jnp.where(chosen, 1.0, 0.0)
            alive = extra[at, top : top + 1].astype(F32)
            gates[at, :] = jnp.where(chosen, prob, 0.0) * alive
            m_grads[i, :, :, width:] = jnp.zeros((2, BLOCK // 2, EXTRA), BF)

        probs[...] = router(pl.ds(pl.multiple_of(mine * rows, rows), rows), lane[:rows])

        shared = s_down.shape[0]
        used = s_padded.shape[0] // ROW_PAD * 7 // 16
        steps = group // BLOCK

        def shared_pass():
            pack = spread_matrix(shared, 16, used).astype(BF)
            s_down[...] = dot(pack, s_padded[...]).astype(BF)
            one_expert(
                (0, steps), x, g, s_both.at[:, :shared], s_both.at[:, shared:], s_down,
                lambda at: extra[at, top : top + 1].astype(F32),
                swact, sg_a, sg_b, m_outs, m_grads, None, False,
            )

        def shared_sums():
            for c in range(0, width, BLOCK):
                left = x[:, c : c + BLOCK]
                for n, back in enumerate((sg_a, sg_b)):
                    store_rows(
                        v_shared, (4, 2, 2), slice(n * shared, (n + 1) * shared), c,
                        dot_tn(left, back[...]).astype(BF),
                    )
            d_sdown[...] = dot_tn(swact[...], g[...]).astype(BF)
            pack = spread_matrix(shared, 16, used).astype(BF)
            for c in range(0, s_padded.shape[0], BLOCK):
                store_rows(
                    v_down, (4, 2, 2), slice(0, width), c,
                    dot_tn(pack[:, c : c + BLOCK], d_sdown[...]).astype(BF),
                )

        def expert_pass(e, part):
            expert = mine * exp_dev + e

            def picked(at):
                return jnp.sum(jnp.where(lane == expert, gates[at, :], 0.0), axis=1, keepdims=True)

            def q_sum(i, at, value):
                old = m_grads[i, :, :, width:].reshape(BLOCK, EXTRA).astype(F32)
                new = jnp.where(lane == expert, value * named[at, :], old)
                m_grads[i, :, :, width:] = new.astype(BF).reshape(2, BLOCK // 2, EXTRA)

            if part[0] == 0:
                for copy in loads:
                    cp.arrived(copy)
                loads.clear()
            one_expert(
                part, x, g, w_gate, w_up, w_down, picked,
                wact, g_a, g_b, m_outs, m_grads, q_sum, e == 0,
            )
            if part[1] == steps and e + 1 < exp_dev:
                loads.extend(cp.local(a.at[e + 1], b) for a, b in weights)

        def stream(e, n, sent, kept, at, ring_first):
            streams["GUD"[n] + str(e)] = one = expert_stream(
                cp, place, gr, sent, kept, e_got[n], e_bufs[n], e_total[e][n], at, ring_first,
                free.at[n], e > 0,
            )
            next(one)

        def expert_sums(e, n):
            if n < 2:
                d, back, x_out = ((d_gate, g_a, x_gate), (d_up, g_b, x_up))[n]
                for c in range(0, width, BLOCK):
                    store_rows(
                        d, (2, 4, 2), slice(0, hidden), c, dot_tn(x[:, c : c + BLOCK], back[...]).astype(BF)
                    )
                stream(
                    e, n, d.at[place.mate], d.at[core],
                    lambda k, z: x_out.at[e, core, place.y_at[k], z], True,
                )
            else:
                for c in range(0, hidden, 128):
                    store_rows(
                        d_down, (4, 2), slice(0, width), c, dot_tn(wact[:, c : c + 128], g[...]).astype(BF)
                    )
                stream(
                    e, n, d_down.at[:, :, :, theirs], d_down.at[:, :, :, ours],
                    lambda k, z: x_down.at[e, place.y_at[k], z, :, ours], False,
                )

        def start_x():
            for n, (c, b) in enumerate(zip(cuts, b_grads)):
                streams["X" + str(n)] = one = sum_ring_pair(
                    cp, ge, view(m_grads, c), view(m_grads, c), b, total_grads.at[:, c]
                )
                next(one)

        pieces = {"sp": shared_pass, "ss": shared_sums, "x": start_x}
        for e in range(exp_dev):
            half_steps = steps // 2
            pieces["p" + str(e)] = functools.partial(expert_pass, e, (0, steps))
            pieces["q" + str(e)] = functools.partial(expert_pass, e, (0, half_steps))
            pieces["r" + str(e)] = functools.partial(expert_pass, e, (half_steps, steps))
            for n in range(3):
                pieces["gud"[n] + str(e)] = functools.partial(expert_sums, e, n)
        follow(ORDER_A, pieces)

    def follow(order, pieces):
        for name in order:
            if name in pieces:
                pieces[name]()
            else:
                next(streams[name], None)

    pl.run_scoped(
        phase_a,
        pltpu.VMEM((group, width), BF),
        pltpu.VMEM((group, width), BF),
        pltpu.VMEM((width, hidden), BF),
        pltpu.VMEM((width, hidden), BF),
        pltpu.VMEM((hidden, width), BF),
        *[pltpu.VMEM((group, hidden), BF)] * 3,
        *[pltpu.VMEM((group, EXTRA), F32)] * 2,
        *[pltpu.VMEM((group, s_both.shape[1] // 2), BF)] * 3,
        *[pltpu.VMEM((s_both.shape[1] // 2, width), BF)] * 2,
        pltpu.VMEM((2, 4, 2, half_part, hidden), BF),
        pltpu.VMEM((2, 4, 2, half_part, hidden), BF),
        pltpu.VMEM((4, 2, hidden // 8, width), BF),
    )

    def phase_b(
        v_probs, v_hidden, v_qkvs, v_w, w_whole, residual, cot, tok, attended, cosine, sine,
        v_whole, v_qkv, totals, padded, g_att, g_residual, g_keys, g_values, g_qkv, g_branch,
    ):
        loads = [
            cp.local(a, b)
            for a, b in (
                (h_residual, residual), (h_cot, cot), (h_whole, w_whole), (h_attended, attended),
                (h_qkv, v_qkvs), (h_probs, v_probs), (h_cosine, cosine), (h_sine, sine),
                (w_slices.at[:, : v_w.shape[1]], v_w), (h_hidden, v_hidden), (h_tok, tok),
            )
        ]
        alive = live[...]
        kept = {}

        step = 256

        def second_norm():
            for copy in loads:
                cp.arrived(copy)
            router_grad = total_grads[:, width:] * alive
            prob = probs[...]
            logit_grad = prob * (router_grad - jnp.sum(prob * router_grad, axis=1, keepdims=True))
            squares = jnp.zeros((rows, 1), F32)
            mean_k = jnp.zeros((rows, 1), F32)
            for c in range(0, width, step):
                part = residual[:, c : c + step]
                squares += jnp.sum(part * part, axis=1, keepdims=True)
            scale = lax.rsqrt(squares / width + EPS)
            gain_rows = []
            for c in range(0, width, step):
                k = total_grads[:, c : c + step] + lax.dot_general(
                    logit_grad, w_whole[c : c + step, width:].astype(F32), (((1,), (1,)), ((), ())),
                    preferred_element_type=F32, precision=HIGH,
                )
                normed = residual[:, c : c + step] * scale
                gain_rows.append(jnp.sum(k * normed, axis=0, keepdims=True))
                k = k * gains[1:2, c : c + step]
                mean_k += jnp.sum(k * normed, axis=1, keepdims=True)
                g_residual[:, c : c + step] = k
            mean_k = mean_k / width
            for c in range(0, width, step):
                normed = residual[:, c : c + step] * scale
                grad = cot[:, c : c + step].astype(F32) + scale * (
                    g_residual[:, c : c + step] - normed * mean_k
                )
                g_residual[:, c : c + step] = grad
                g_branch[:, c : c + step] = (alive * grad).astype(BF)
            for c in range(0, width, step):
                g_att[c // step] = dot_nt(g_branch[...], w_whole[c : c + step, :width]).astype(BF)
            for c in range(width // step, 8):
                g_att[c] = jnp.zeros((rows, span), BF)
            kept["third"] = [cp.local(g_att.at[mine], g_heads.at[mine])] + [
                cp.send(g_att.at[(mine + k) % 8], g_heads.at[mine], place.to_ep(k)) for k in range(1, 8)
            ]
            kept["norm"] = logit_grad, scale, gain_rows

        def whole_sums():
            logit_grad, scale, gain_rows = kept["norm"]
            for i in range(2):
                c = slice(i * width // 2, (i + 1) * width // 2)
                v_whole[2 * i : 2 * i + 2, :, :, :, :width] = (
                    dot_tn(attended[:, c], g_branch[...]).astype(BF).reshape(2, 2, 2, width // 16, width)
                )
                hid = (residual[:, c] * scale * gains[1:2, c]).astype(BF).astype(F32)
                small = lax.dot_general(
                    hid, logit_grad, (((0,), (0,)), ((), ())), preferred_element_type=F32, precision=HIGH
                )
                gain_row = jnp.concatenate(gain_rows, axis=1)[:, c]
                lane = lax.broadcasted_iota(jnp.int32, (width // 2, EXTRA), 1)
                column = jnp.broadcast_to(gain_row, (8, width // 2)).T[:, :1]
                small = jnp.where(lane == EXTRA - 1, column, small)
                v_whole[2 * i : 2 * i + 2, :, :, :, width:] = small.astype(BF).reshape(
                    2, 2, 2, width // 16, EXTRA
                )
            dense("W", 0, v_whole, False, 0, o_whole)

        def dense(name, i, v, ring_first, spread, result):
            one = dense_stream(cp, place, gr, v, got[i], bufs[i], totals[i], ring_first)
            if spread is not None:
                one = spread_stream(cp, place, one, totals[i], padded[spread], result)
            streams[name] = one
            next(one)

        def small_dense():
            dense("S", 1, v_shared, True, 1, o_shared)
            dense("N", 2, v_down, True, None, None)

        def start_out():
            streams["O"] = sum_ring_pair(cp, ge, m_outs, m_outs, b_outs, out, (residual,))
            next(streams["O"])

        def head(h):
            if h == 0:
                for copy in kept["third"]:
                    cp.arrived(copy)
            attention_back_head(h, g_heads, v_qkvs, v_probs, cosine, sine, g_keys, g_values, g_qkv)

        def hidden_part():
            @pl.loop(0, group // BLOCK)
            def _(i):
                at = pl.ds(pl.multiple_of(i * BLOCK, BLOCK), BLOCK)
                part = dot_nt(g_qkv[at, :], v_w[...]).astype(BF)
                m_grads[i, :, :, :width] = part.reshape(2, rows, width)

            hcuts = (pl.ds(0, half), pl.ds(half, width - half))
            for n, ((b,), c) in enumerate(zip(b_grads, hcuts)):
                streams["H" + str(n)] = one = sum_ring_pair(
                    cp, ge, view(m_grads, c), view(m_grads, c), [b.at[:, :, pl.ds(0, c.size)]],
                    total_hidden.at[:, c],
                )
                next(one)

        def qkv_sums():
            for i in range(2):
                c = slice(i * width // 2, (i + 1) * width // 2)
                v_qkv[2 * i : 2 * i + 2] = (
                    dot_tn(v_hidden[:, c], g_qkv[...]).astype(BF).reshape(2, 2, 2, width // 16, 3 * span)
                )
            dense("Q", 3, v_qkv, True, 2, o_qkv)

        def first_norm():
            squares = jnp.zeros((rows, 1), F32)
            mean_k = jnp.zeros((rows, 1), F32)
            for c in range(0, width, step):
                part = tok[:, c : c + step].astype(F32)
                squares += jnp.sum(part * part, axis=1, keepdims=True)
            scale = lax.rsqrt(squares / width + EPS)
            for c in range(0, width, step):
                normed = tok[:, c : c + step].astype(F32) * scale
                k = total_hidden[:, c : c + step] * gains[0:1, c : c + step]
                mean_k += jnp.sum(k * normed, axis=1, keepdims=True)
            mean_k = mean_k / width
            for c in range(0, width, step):
                normed = tok[:, c : c + step].astype(F32) * scale
                k = total_hidden[:, c : c + step] * gains[0:1, c : c + step]
                d_tok[:, c : c + step] = g_residual[:, c : c + step] + scale * (k - normed * mean_k)

        follow(
            ORDER_B,
            {
                "n2": second_norm, "dw": whole_sums, "sn": small_dense, "o": start_out,
                "h0": functools.partial(head, 0), "h1": functools.partial(head, 1),
                "hp": hidden_part, "dq": qkv_sums, "n1": first_norm,
            },
        )
        run_streams(*streams.values())
        o_down[...] = totals[2][...]
        cp.finish()

    columns = (wide, s_both.shape[1], width, 3 * span)
    depth = (half_part, half_part, ROW_PAD, half_part)
    pl.run_scoped(
        phase_b,
        pltpu.VMEM(h_probs.shape, BF),
        pltpu.VMEM(h_hidden.shape, BF),
        pltpu.VMEM(h_qkv.shape, BF),
        pltpu.VMEM((width, 3 * span), BF),
        pltpu.VMEM(h_whole.shape, BF),
        pltpu.VMEM((rows, width), F32),
        *[pltpu.VMEM((rows, width), BF)] * 3,
        *[pltpu.VMEM((group, HD), F32)] * 2,
        pltpu.VMEM((4, 2, 2, half_part, wide), BF),
        pltpu.VMEM((4, 2, 2, half_part, 3 * span), BF),
        [pltpu.VMEM((r, c), BF) for r, c in zip(depth, columns)],
        [pltpu.VMEM((8, ROW_PAD, columns[i]), BF) for i in (0, 1, 3)],
        pltpu.VMEM((8, rows, span), BF),
        pltpu.VMEM((rows, width), F32),
        *[pltpu.VMEM((group, HD), F32)] * 2,
        pltpu.VMEM((group, 3 * span), BF),
        pltpu.VMEM((rows, width), BF),
    )


def call_rest(
    experts, top, x_all, g_all, e_gate, e_up, e_down, h_probs, h_hidden, h_qkv, w_slices, h_whole,
    h_residual, h_cot, h_tok, h_attended, h_cosine, h_sine,
    extra, w_router, s_both, s_padded, live, gains,
):
    anyspace = pl.BlockSpec(memory_space=pl.ANY)
    vmem = pl.BlockSpec(memory_space=pltpu.VMEM)
    rows, width = h_cot.shape
    span = HEADS_DEV * HD
    wide = width + EXTRA
    cut = wide // 2 // 128 * 128
    exp_dev, _, hidden = e_gate.shape
    part = width // 16
    columns = (wide, s_both.shape[1], width, 3 * span)
    depth = (part, part, ROW_PAD, part)
    orders = (False, True, True, True)
    halves = ((part, hidden), (part, hidden), (hidden // 8, width // 2))
    bufs_of = lambda first, r, c: (ring_pair_bufs if first else pair_ring_bufs)(r, c)
    shape = jax.ShapeDtypeStruct
    return pl.pallas_call(
        functools.partial(kernel_rest, experts, top),
        out_shape=(
            shape((rows, width), BF),
            shape((rows, width), F32),
            shape((exp_dev, 2, 4, 2, part, hidden), BF),
            shape((exp_dev, 2, 4, 2, part, hidden), BF),
            shape((exp_dev, 4, 2, hidden // 8, width), BF),
            shape((8, ROW_PAD, 3 * span), BF),
            shape((8, ROW_PAD, columns[1]), BF),
            shape((8, ROW_PAD, wide), BF),
            shape((ROW_PAD, width), BF),
        ),
        in_specs=[anyspace] * 16 + [vmem] * 6,
        out_specs=(vmem, vmem) + (anyspace,) * 6 + (vmem,),
        scratch_shapes=[
            pltpu.VMEM((4, 2, rows, wide), BF),
            pltpu.VMEM((4, 2, rows, width), BF),
            [ring_pair_bufs(rows, c) for c in (cut, wide - cut)],
            ring_pair_bufs(rows, width),
            pltpu.VMEM((rows, wide), F32),
            pltpu.VMEM((rows, width), F32),
            [pltpu.VMEM((4, 2) + h, BF) for h in halves],
            [bufs_of(first, *h) for first, h in zip((True, True, False), halves)],
            [[pltpu.VMEM(h, BF) for h in halves] for _ in range(exp_dev)],
            pltpu.VMEM((4, 2, 2, part, columns[1]), BF),
            pltpu.VMEM((4, 2, 2, ROW_PAD, width), BF),
            [pltpu.VMEM((4, 2, r, c), BF) for r, c in zip(depth, columns)],
            [bufs_of(first, r, c) for first, r, c in zip(orders, depth, columns)],
            pltpu.VMEM((8, rows, span), BF),
            pltpu.VMEM((rows, EXTRA), F32),
            pltpu.SemaphoreType.REGULAR((3,)),
            pltpu.SemaphoreType.DMA((440,)),
            pltpu.SemaphoreType.DMA((440,)),
        ],
        compiler_params=pltpu.CompilerParams(
            collective_id=2, has_side_effects=True, vmem_limit_bytes=int(63.9 * 2**20)
        ),
        name="rest",
    )(
        x_all, g_all, e_gate, e_up, e_down, h_probs, h_hidden, h_qkv, w_slices, h_whole,
        h_residual, h_cot, h_tok, h_attended, h_cosine, h_sine,
        extra, w_router, s_both, s_padded, live, gains,
    )


def pad_rows(values, rows):
    return jnp.pad(values, ((0, rows - values.shape[0]),) + ((0, 0),) * (values.ndim - 1))


def body(
    tokens, cotangent, lengths, token_mask, routes,
    w_query, w_key, w_value, w_output, w_router,
    shared_gate, shared_up, shared_down, norm_attn, norm_ffn,
    expert_gate, expert_up, expert_down,
):
    rows, width = tokens.shape
    top = routes.shape[1]
    used = w_query.shape[0]
    hidden = expert_gate.shape[2]
    experts = w_router.shape[1]
    exp_dev = expert_gate.shape[0]
    ep = lax.axis_index("ep")
    group = rows * 8
    span = HEADS_DEV * HD
    owners = width // span
    down_used = shared_down.shape[0]
    shared_cols = 16 * down_used

    def by_owner(w):
        return jnp.pad(w.reshape(used, owners, span), ((0, 0), (0, 8 - owners), (0, 0)))

    def by_shared(w):
        w = w.reshape(used, 16, 8, down_used).transpose(0, 2, 1, 3).reshape(used, 8, shared_cols)
        return w

    gains = jnp.broadcast_to(jnp.stack([norm_attn, norm_ffn], axis=1)[:, None], (used, 8, 2))
    zeros = lambda n: jnp.zeros((used, 8, n), BF)
    slices = jnp.concatenate(
        [
            by_owner(w_query), by_owner(w_key), by_owner(w_value),
            by_shared(shared_gate), gains, zeros(126 - shared_cols),
            by_shared(shared_up), zeros(128 - shared_cols),
        ],
        axis=2,
    ).transpose(1, 0, 2)
    slices = jnp.pad(slices, ((0, 0), (0, ROW_PAD - used), (0, 0)))
    whole = jnp.concatenate([w_output, w_router], axis=1)
    whole = jnp.pad(whole, ((0, ROW_PAD - used), (0, width + EXTRA - whole.shape[1])))
    down = pad_rows(shared_down, ROW_PAD)
    position = ep * rows + jnp.arange(rows, dtype=jnp.int32)
    live_own = ((position < lengths[0]) & (token_mask == 1)).astype(F32)
    tok_wide = jnp.concatenate(
        [
            tokens,
            jnp.pad(
                jnp.concatenate([routes.astype(BF), live_own[:, None].astype(BF)], axis=1),
                ((0, 0), (0, EXTRA - top - 1)),
            ),
        ],
        axis=1,
    )
    frequency = 10000.0 ** (-(np.arange(HD // 2, dtype=np.float32) * np.float32(2.0) / HD))
    angles = np.arange(group, dtype=np.float32)[:, None] * frequency.astype(np.float32)[None, :]
    cosine = jnp.asarray(np.tile(np.cos(angles), (1, 2)), F32)
    sine = jnp.asarray(np.concatenate([-np.sin(angles), np.sin(angles)], axis=1), F32)
    live_col = live_own[:, None]
    (
        w_slices, w_both, w_whole, w_router_all, w_down, cot_all, extra,
        hidden_one, qkv, attn_probs, gain_rows, residual, attended, hidden_all,
    ) = call_front(slices, whole, down, tok_wide, cotangent, live_col, cosine, sine, used)
    w_slices = w_slices.reshape(width, -1)
    w_whole = w_whole.reshape(width, -1)
    out, d_tokens, e_gate, e_up, e_down, o_qkv, o_shared, o_whole, o_down = call_rest(
        experts, top,
        hidden_all.reshape(group, width), cot_all.reshape(group, width),
        expert_gate, expert_up, expert_down, attn_probs, hidden_one, qkv, w_slices, w_whole,
        residual, cotangent, tokens, attended, cosine, sine,
        extra.reshape(group, EXTRA), w_router_all.reshape(width, EXTRA),
        w_both.reshape(width, -1), w_down.reshape(-1, width), live_col, gain_rows,
    )
    o_qkv = o_qkv[:owners, :used].astype(F32)
    o_shared = o_shared[:, :used].astype(F32)
    o_whole = jnp.sum(o_whole[:, :used].astype(F32), axis=0)

    def from_owner(i):
        return o_qkv[:, :, i * span : (i + 1) * span].transpose(1, 0, 2).reshape(used, width)

    def from_shared(i):
        return (
            o_shared[:, :, 128 * i : 128 * i + shared_cols]
            .reshape(8, used, 16, down_used)
            .transpose(1, 2, 0, 3)
            .reshape(used, hidden)
        )

    d_query, d_key, d_value = (from_owner(i) for i in range(3))
    d_gain_one = sum(
        jnp.sum(w.astype(F32) * d, axis=1)
        for w, d in ((w_query, d_query), (w_key, d_key), (w_value, d_value))
    ) / norm_attn.astype(F32)
    return (
        out,
        d_tokens,
        d_query,
        d_key,
        d_value,
        o_whole[:, :width],
        o_whole[:, width : width + experts],
        from_shared(0),
        from_shared(1),
        o_down[:down_used].astype(F32),
        d_gain_one,
        o_whole[:, width + EXTRA - 1],
        e_gate.reshape(exp_dev, width, hidden).astype(F32),
        e_up.reshape(exp_dev, width, hidden).astype(F32),
        e_down.reshape(exp_dev, hidden, width).astype(F32),
    )


def solution(mesh):
    both = ("rep", "ep")
    row = P(both, None)
    expert = P("ep", None, None)
    in_specs = (
        row, row, P("rep"), P(both), row, row, row, row, row, row, row, row, row,
        P(both), P(both), expert, expert, expert,
    )
    out_specs = (
        row, row, row, row, row, row, row, row, row, row, P(both), P(both),
        expert, expert, expert,
    )
    return jax.shard_map(body, mesh=mesh, in_specs=in_specs, out_specs=out_specs, check_vma=False)
```

time: 444 us -> 348 us (0.78)
  the two profiles are of different devices: /device:TPU:1 before, /device:TPU:0 now
where the time goes in v3:
time: 348 us; the launch traced here: 345 us
  Pallas kernels  297 us (85%)
  other arithmetic  30.1 us (9%)
  local copies, waits for them, and re-layouts  16 us (5%)
    pallas_call x1, Pallas kernels, call_rest(): pl.pallas_call(functools.partial(kernel_rest, experts, top), out_shape=(s...  191 us
    pallas_call x1, Pallas kernels, call_front(): pl.pallas_call(kernel_front, out_shape=(shape((16, 8 * used, columns), BF...  106 us
    convert_element_type x1, other arithmetic, body(): e_up.reshape(exp_dev, width, hidden).astype(F32)  11.6 us

profile of v3, /device:TPU:0, one launch (start us, length us, event | category | flops | bytes accessed | tf_op | source)
XLA Modules:
  0.0 344.7 jit_solution(15762432642974375000)
XLA Ops:
  1.3 0.7 convert_bitcast_fusion
  2.0 0.7 pad_maximum_fusion.1
  2.6 0.7 convert_element_type.66
  3.6 1.4 pad.31.down
  4.9 0.8 reshape.107
  5.8 0.8 reshape.108
  6.7 0.8 reshape.109
  7.5 1.4 fusion.7.whole
  9.0 0.7 copy.72.live
  9.7 1.7 fusion.1.tok
  11.4 1.3 reshape.110
  13.1 1.3 reshape.112
  14.9 0.7 pad.29.slices
  15.7 106.0 %front.1 = (bf16[16,80,1024]{2,1,0:T(8,128)(2,1)}, bf16[16,80,256]{2,1,0:T(8,128)(2,1)}, bf16[16,80,1408]{2,1,0:T(8,128)(2,1)}, bf16[16,80,128]{2,1,0:T(8,128)(2...) custom-call(bf16[8,16,1024]{2,1,0:T(8,128)(2,1)} %pad.29.slices, ...), custom_call_target="tpu_custom_call" | custom-call | tf_op jit(solution)/shard_map/front/pallas_call | solution.py:444
  121.7 190.7 %rest.1 = (bf16[128,1280]{1,0:T(8,128)(2,1)}, f32[128,1280]{1,0:T(8,128)}, bf16[2,2,4,2,80,896]{5,4,3,2,1,0:T(8,128)(2,1)}, bf16[2,2,4,2,80,896]{5,4,3,2,1,0:T(8...) custom-call(bf16[1024,1280]{1,0:T(8,128)(2,1)} %bitcast.63, ...), custom_call_target="tpu_custom_call" | custom-call | tf_op jit(solution)/shard_map/rest/pallas_call | solution.py:1208
  312.5 1.3 slice_convert_fusion.2
  313.8 1.1 convert_reduce_fusion
  314.9 0.7 slice_reduce_fusion
  315.6 0.6 slice.52
  316.2 0.6 slice.51
  316.8 0.8 slice_convert_fusion.1
  317.7 0.9 slice_convert_fusion
  318.9 1.0 multiply_reduce_fusion
  320.0 0.9 multiply_reduce_fusion.2
  320.9 0.5 convert_divide_fusion
  321.4 0.4 reshape.125
  322.0 1.0 reshape.126
  323.6 1.0 reshape.128
  324.6 6.7 %bitcast_convert_fusion = f32[2,896,1280]{2,1,0:T(8,128)} fusion(bf16[2,4,2,112,1280]{4,3,2,1,0:T(8,128)(2,1)} %get-tuple-element.60), kind=kLoop, calls=%fused_computation | loop fusion | flops 2293760 | bytes 13762560 | tf_op jit(solution)/shard_map/convert_element_type | solution.py:1364
  331.3 11.6 %bitcast_convert_fusion.1 = (f32[2,1280,896]{2,1,0:T(8,128)}, f32[2,1280,896]{2,1,0:T(8,128)}) fusion(bf16[2,2,4,2,80,896]{5,4,3,2,1,0:T(8,128)(2,1)} %get-tuple-element.59, bf16[2,2,4,2,80,896]{5,4,3,2,1,0:T(8,128)(2,1)} %get-tuple-element.58), kind=kLoop, calls=%fused_computation.1 | loop fusion | flops 4587520 | bytes 27525120 | tf_op jit(solution)/shard_map/convert_element_type | solution.py:1363
  342.9 0.7 copy.91
  343.6 0.8 copy.92
  (45 shorter events, 2.3 us)
Async XLA Ops:
  121.7 199.2 %copy-start.5 = (bf16[10]{0:T(256)(128)(2,1)S(1)}, bf16[10]{0:T(256)(128)(2,1)}, u32[]{:S(2)}) copy-start(bf16[10]{0:T(256)(128)(2,1)} %param.33) | copy-start | bytes 64
  318.8 12.5 %copy-start.3 = (f32[2,8,5,256]{3,1,2,0:T(8,128)}, f32[2,8,5,256]{3,1,2,0:T(8,128)S(1)}, u32[]{:S(2)}) copy-start(f32[2,8,5,256]{3,1,2,0:T(8,128)S(1)} %copy.87) | copy-start | bytes 245764
  318.9 12.4 %copy-start.4 = (f32[2,8,5,256]{3,1,2,0:T(8,128)}, f32[2,8,5,256]{3,1,2,0:T(8,128)S(1)}, u32[]{:S(2)}) copy-start(f32[2,8,5,256]{3,1,2,0:T(8,128)S(1)} %copy.86) | copy-start | bytes 245764
  320.0 11.3 %copy-start.2 = (f32[2,8,5,256]{3,1,2,0:T(8,128)}, f32[2,8,5,256]{3,1,2,0:T(8,128)S(1)}, u32[]{:S(2)}) copy-start(f32[2,8,5,256]{3,1,2,0:T(8,128)S(1)} %copy.85) | copy-start | bytes 245764
  331.2 11.6 %copy-start.1 = (bf16[128,1280]{1,0:T(8,128)(2,1)S(1)}, bf16[128,1280]{1,0:T(8,128)(2,1)}, u32[]{:S(2)}) copy-start(bf16[128,1280]{1,0:T(8,128)(2,1)} %get-tuple-element.87) | copy-start | bytes 983044
  331.3 12.4 %copy-start = (f32[128,1280]{1,0:T(8,128)S(1)}, f32[128,1280]{1,0:T(8,128)}, u32[]{:S(2)}) copy-start(f32[128,1280]{1,0:T(8,128)} %get-tuple-element.88) | copy-start | bytes 1966084

commit v4 on v3

--- a/solution.py
+++ b/solution.py
@@ -47,6 +47,8 @@
 
         self.mate = 1 - self.core
         self.y_at = {k: (self.y + k) % 4 for k in (-1, 0, 1, 2)}
+        self.from_x = {k: self.ep_at(self.x + k, self.zh) for k in (-1, 1, 2)}
+        self.from_z = {k: self.ep_at(self.x + k, 1 - self.zh) for k in (-1, 0, 1, 2)}
         self._x = {k: (self.rep, self.ep_at(self.x + k, self.zh)) for k in (-1, 1)}
         self._y = {k: (self.rep_at(self.y + k, self.zl, self.core), self.ep) for k in (-1, 1)}
         self._ep = {k: (self.rep, (self.ep + k) % 8) for k in range(1, 8)}
@@ -176,11 +178,32 @@
             self.sent_off(copy)
 
 
-def greet(devices):
+def greet(devices, meanwhile=lambda: None):
     barrier = pltpu.get_barrier_semaphore()
     for device in devices:
         pl.semaphore_signal(barrier, inc=1, device_id=device, device_id_type=MESH)
+    meanwhile()
     pl.semaphore_wait(barrier, len(devices))
+
+
+def as_column(row):
+    shape = (row.shape[1],) * 2
+    same = lax.broadcasted_iota(jnp.int32, shape, 0) == lax.broadcasted_iota(jnp.int32, shape, 1)
+    return jnp.sum(jnp.where(same, row, 0.0), axis=1, keepdims=True)
+
+
+def as_row(column):
+    shape = (column.shape[0],) * 2
+    same = lax.broadcasted_iota(jnp.int32, shape, 0) == lax.broadcasted_iota(jnp.int32, shape, 1)
+    return jnp.sum(jnp.where(same, column, 0.0), axis=0, keepdims=True)
+
+
+def shared_columns(owner, hidden, used):
+    shape = (hidden, 128)
+    unit = lax.broadcasted_iota(jnp.int32, shape, 0)
+    k = lax.broadcasted_iota(jnp.int32, shape, 1)
+    taken = (k < 16 * used) & (unit == (k // used) * 8 * used + owner * used + k % used)
+    return jnp.where(taken, 1.0, 0.0).astype(BF)
 
 
 def run_streams(*streams):
@@ -214,17 +237,16 @@
     left = cp.send(src, dst.at[mine], place.to_x(-1))
     over = cp.send(src, dst.at[mine], place.to_zh())
     yield
-    from_left = place.ep_at(place.x - 1, place.zh)
-    from_right = place.ep_at(place.x + 1, place.zh)
-    from_over = place.ep_at(place.x, 1 - place.zh)
-    far = place.ep_at(place.x + 2, place.zh)
+    from_left, from_right, far = (place.from_x[k] for k in (-1, 1, 2))
+    from_over = place.from_z[0]
+    cp.arrived(own)
     cp.arrived(right)
     half_a = cp.send(dst.at[from_left, :, lo], dst.at[from_left, :, lo], place.to_x(1))
     cp.arrived(left)
     half_b = cp.send(dst.at[from_right, :, hi], dst.at[from_right, :, hi], place.to_x(-1))
     yield
     cp.arrived(over)
-    last = [own]
+    last = []
     last.append(cp.send(dst.at[from_over], dst.at[from_over], place.to_x(1)))
     last.append(cp.send(dst.at[from_over], dst.at[from_over], place.to_x(-1)))
     yield
@@ -234,6 +256,8 @@
     yield
     for copy in last:
         cp.arrived(copy)
+    for copy in [right, left, over, half_a, half_b] + last:
+        cp.sent_off(copy)
 
 
 def gather_ring_y(cp, place, src, dst, columns, slot):
@@ -323,124 +347,173 @@
     )
 
 
+ORDER_F = (
+    "a", "k1", "T", "T", "L", "L", "T", "L", "k2", "L", "c", "L", "L", "T",
+    "pr", "W", "h0", "h1", "W", "W", "C", "C", "W", "C", "D", "D", "W", "D",
+    "D", "W", "D", "D", "op", "C",
+)
+
+
 def kernel_front(
-    slices, whole, down, tok, cot, live, cosine, sine,
+    tok, cot, length, mask, routes, w_query, w_key, w_value, w_output, w_route,
+    shared_gate, shared_up, shared_down, norm_attn, norm_ffn, cosine, sine,
     w_slices, w_both, w_whole, w_router, w_down, cot_all, extra,
-    hidden_one, qkv, probs, gains, residual, attended, hidden_all,
+    hidden_one, qkv, probs, gains, residual, attended, hidden, live,
+    slices, whole, down, wide_tok,
     land_slices, land_whole, pack_slices, pack_whole, v_slices, v_whole, v_tok,
-    heads, land_heads, hidden, live_row, send_sem, recv_sem,
+    heads, land_heads, live_row, send_sem, recv_sem,
 ):
     place = Place()
     cp = Copies(send_sem, recv_sem)
-    greet(ep_peers(place) + rep_peers(place))
-    rows = tok.shape[0]
-    width = cot.shape[1]
+    rows, width = tok.shape
     group = 8 * rows
     span = HEADS_DEV * HD
     mine = place.ep
-
-    to_slices = [cp.local(slices.at[mine], land_slices.at[mine])]
-    to_whole = [cp.local(whole, land_whole.at[mine])]
-    for k in range(1, 8):
-        to_slices.append(cp.send(slices.at[(mine + k) % 8], land_slices.at[mine], place.to_ep(k)))
-    for k in range(1, 8):
-        to_whole.append(cp.send(whole, land_whole.at[mine], place.to_ep(k)))
-    toks = gather_ep(cp, place, tok, v_tok, tok.shape[1])
-    advance(toks)
-    downs = gather_rep(cp, place, down, w_down, down.shape[1], True)
-    advance(downs)
+    top = routes.shape[0]
+
+    def own_inputs():
+        position = mine * rows + lax.broadcasted_iota(jnp.int32, (1, rows), 1)
+        alive = jnp.where((position < length[...]) & (mask[...] == 1), 1.0, 0.0)
+        live[...] = as_column(alive)
+        block = jnp.concatenate(
+            [routes[...].astype(F32), alive, jnp.zeros((EXTRA - top - 1, rows), F32)], axis=0
+        )
+        wide_tok[:, :width] = tok[...]
+        wide_tok[:, width:] = block.T.astype(BF)
+        for ref in (slices, whole, down):
+            ref[...] = jnp.zeros_like(ref)
+        rows_of = slice(0, w_query.shape[0])
+        whole[rows_of, :width] = w_output[...]
+        whole[rows_of, width : width + w_route.shape[1]] = w_route[...]
+        down[: shared_down.shape[0], :] = shared_down[...]
+        gains_of = [as_column(g[...].astype(F32)) for g in (norm_attn, norm_ffn)]
+        lane = lax.broadcasted_iota(jnp.int32, (w_query.shape[0], 128), 1)
+        spare = 16 * shared_down.shape[0]
+        for owner in range(8):
+            if owner * span < width:
+                for n, w in enumerate((w_query, w_key, w_value)):
+                    slices[owner, rows_of, n * span : (n + 1) * span] = w[:, owner * span : (owner + 1) * span]
+            pick = shared_columns(owner, shared_gate.shape[1], shared_down.shape[0])
+            gate = dot(shared_gate[...], pick)
+            gate = jnp.where(lane == spare, gains_of[0], jnp.where(lane == spare + 1, gains_of[1], gate))
+            slices[owner, rows_of, 3 * span : 3 * span + 128] = gate.astype(BF)
+            slices[owner, rows_of, 3 * span + 128 :] = dot(shared_up[...], pick).astype(BF)
+
+    greet(ep_peers(place) + rep_peers(place), own_inputs)
+    streams, kept = {}, {}
     used = pack_slices.shape[0] // 8
-    spread = spread_matrix(8 * used, 8, used).astype(BF)
+    per = BLOCK // rows
 
     def pack(land, packed):
+        spread = spread_matrix(8 * used, 8, used).astype(BF)
         for c in range(0, land.shape[2], 128):
             block = land[:, :, c : c + 128].reshape(8 * ROW_PAD, 128)
             packed[:, c : c + 128] = dot(spread, block).astype(BF)
 
-    for copy in to_slices:
-        cp.arrived(copy)
-    pack(land_slices, pack_slices)
-    sls = gather_rep(cp, place, pack_slices, v_slices, slices.shape[2], True)
-    advance(sls)
-    for copy in to_whole:
-        cp.arrived(copy)
-    pack(land_whole, pack_whole)
-    advance(toks)
-    whs = gather_rep(cp, place, pack_whole, v_whole, whole.shape[1], True)
-    advance(sls, whs, toks, sls, toks)
-    cots = gather_ep(cp, place, cot, cot_all, width)
-    advance(whs, sls)
-    cp.drain(toks)
-    advance(cots)
-    cp.drain(sls)
-    outs = [
-        cp.local(v_slices, w_slices),
-        cp.local(v_slices.at[:, :, pl.ds(3 * span, 256)], w_both),
-        cp.local(v_tok.at[:, :, pl.ds(width, EXTRA)], extra),
-    ]
-
-    block = v_slices[:, :, 3 * span : 3 * span + 128].reshape(width, 128).astype(F32).T
-    gains[...] = block[112:120, :]
-    live_row[...] = jnp.concatenate(
-        [v_tok[i, :, width:].astype(F32).T[:8, :] for i in range(8)], axis=1
-    )
-    weights = lambda: v_slices[:, :, : 3 * span].reshape(width, 3 * span)
-    per = BLOCK // rows
-
-    @pl.loop(0, group // BLOCK)
-    def _(i):
-        at = pl.ds(pl.multiple_of(i * BLOCK, BLOCK), BLOCK)
-        values = v_tok[pl.ds(i * per, per), :, :width].reshape(BLOCK, width).astype(F32)
-        scale = lax.rsqrt(jnp.sum(values * values, axis=1, keepdims=True) / width + EPS)
-        low = (values * scale * gains[0:1, :]).astype(BF)
-        hidden_one[at, :] = low
-        raw = dot(low, weights())
-        cos, sin = cosine[at, :], sine[at, :]
-        for h in range(2 * HEADS_DEV):
-            c = slice(h * HD, (h + 1) * HD)
-            qkv[at, c] = turn(raw[:, c], cos, sin).astype(BF)
-        qkv[at, 2 * span :] = raw[:, 2 * span :].astype(BF)
-
-    advance(whs, cots)
-    for h in range(HEADS_DEV):
+    def start(name, stream):
+        streams[name] = stream
+        next(stream)
+
+    def to_owners():
+        kept["slices"] = [cp.local(slices.at[mine], land_slices.at[mine])] + [
+            cp.send(slices.at[(mine + k) % 8], land_slices.at[mine], place.to_ep(k)) for k in range(1, 8)
+        ]
+        kept["whole"] = [cp.local(whole, land_whole.at[mine])] + [
+            cp.send(whole, land_whole.at[mine], place.to_ep(k)) for k in range(1, 8)
+        ]
+        start("T", gather_ep(cp, place, wide_tok, v_tok, wide_tok.shape[1]))
+
+    def pack_first():
+        for copy in kept["slices"]:
+            cp.arrived(copy)
+        pack(land_slices, pack_slices)
+        start("L", gather_rep(cp, place, pack_slices, v_slices, slices.shape[2], True))
+
+    def pack_second():
+        for copy in kept["whole"]:
+            cp.arrived(copy)
+        pack(land_whole, pack_whole)
+        start("W", gather_rep(cp, place, pack_whole, v_whole, whole.shape[1], True))
+        start("D", gather_rep(cp, place, down, w_down, down.shape[1], True))
+
+    def start_cot():
+        start("C", gather_ep(cp, place, cot, cot_all, width))
+
+    def projections():
+        cp.local(v_slices, w_slices)
+        cp.local(v_slices.at[:, :, pl.ds(3 * span, 256)], w_both)
+        cp.local(v_tok.at[:, :, pl.ds(width, EXTRA)], extra)
+        block = v_slices[:, :, 3 * span : 3 * span + 128].reshape(width, 128).astype(F32).T
+        gains[...] = block[112:120, :]
+        live_row[...] = jnp.concatenate(
+            [v_tok[i, :, width:].astype(F32).T[:8, :] for i in range(8)], axis=1
+        )
+
+        @pl.loop(0, group // BLOCK)
+        def _(i):
+            at = pl.ds(pl.multiple_of(i * BLOCK, BLOCK), BLOCK)
+            values = v_tok[pl.ds(i * per, per), :, :width].reshape(BLOCK, width).astype(F32)
+            scale = lax.rsqrt(jnp.sum(values * values, axis=1, keepdims=True) / width + EPS)
+            low = (values * scale * gains[0:1, :]).astype(BF)
+            hidden_one[at, :] = low
+            raw = dot(low, v_slices[:, :, : 3 * span].reshape(width, 3 * span))
+            cos, sin = cosine[at, :], sine[at, :]
+            for h in range(2 * HEADS_DEV):
+                c = slice(h * HD, (h + 1) * HD)
+                qkv[at, c] = turn(raw[:, c], cos, sin).astype(BF)
+            qkv[at, 2 * span :] = raw[:, 2 * span :].astype(BF)
+
+    def head(h):
         attention_head(h, qkv, live_row, probs, heads)
-        advance(whs, cots, downs)
-    column = pl.ds(pl.multiple_of(mine * span, 128), span)
-    first = [cp.local(heads.at[mine], land_heads.at[:, column])]
-    for k in range(1, 8):
-        first.append(cp.send(heads.at[(mine + k) % 8], land_heads.at[:, column], place.to_ep(k)))
-    cp.drain(whs)
-    outs += [
-        cp.local(v_whole, w_whole),
-        cp.local(v_whole.at[:, :, pl.ds(width, EXTRA)], w_router),
-    ]
-    advance(cots, downs)
-    for copy in first:
-        cp.arrived(copy)
-
-    low = land_heads[:, :width]
-    attended[...] = low
-    step = 256
-    squares = jnp.zeros((rows, 1), F32)
-    for c in range(0, width, step):
-        matrix = v_whole[:, :, c : c + step].reshape(width, step)
-        part = tok[:, c : c + step].astype(F32) + live[...] * dot(low, matrix)
-        residual[:, c : c + step] = part
-        squares += jnp.sum(part * part, axis=1, keepdims=True)
-    scale = lax.rsqrt(squares / width + EPS)
-    hidden[...] = (residual[...] * scale * gains[1:2, :]).astype(BF)
-    run_streams(gather_ep(cp, place, hidden, hidden_all, width), cots, downs)
+        if h == HEADS_DEV - 1:
+            column = pl.ds(pl.multiple_of(mine * span, 128), span)
+            kept["heads"] = [cp.local(heads.at[mine], land_heads.at[:, column])] + [
+                cp.send(heads.at[(mine + k) % 8], land_heads.at[:, column], place.to_ep(k))
+                for k in range(1, 8)
+            ]
+
+    def output():
+        cp.local(v_whole, w_whole)
+        cp.local(v_whole.at[:, :, pl.ds(width, EXTRA)], w_router)
+        for copy in kept["heads"]:
+            cp.arrived(copy)
+        low = land_heads[:, :width]
+        attended[...] = low
+        step = 256
+        squares = jnp.zeros((rows, 1), F32)
+        for c in range(0, width, step):
+            matrix = v_whole[:, :, c : c + step].reshape(width, step)
+            part = tok[:, c : c + step].astype(F32) + live[...] * dot(low, matrix)
+            residual[:, c : c + step] = part
+            squares += jnp.sum(part * part, axis=1, keepdims=True)
+        scale = lax.rsqrt(squares / width + EPS)
+        hidden[...] = (residual[...] * scale * gains[1:2, :]).astype(BF)
+
+    pieces = {
+        "a": to_owners, "k1": pack_first, "k2": pack_second, "c": start_cot, "pr": projections,
+        "h0": functools.partial(head, 0), "h1": functools.partial(head, 1), "op": output,
+    }
+    for name in ORDER_F:
+        if name in pieces:
+            pieces[name]()
+        else:
+            next(streams[name], None)
+    run_streams(*streams.values())
     cp.finish()
 
 
-def call_front(slices, whole, down, tok, cot, live, cosine, sine, used):
+def call_front(
+    tok, cot, length, mask, routes, w_query, w_key, w_value, w_output, w_route,
+    shared_gate, shared_up, shared_down, norm_attn, norm_ffn, cosine, sine,
+):
     anyspace = pl.BlockSpec(memory_space=pl.ANY)
     vmem = pl.BlockSpec(memory_space=pltpu.VMEM)
     rows, width = cot.shape
+    used = w_query.shape[0]
     group = 8 * rows
     span = HEADS_DEV * HD
     shape = jax.ShapeDtypeStruct
-    columns, wide = slices.shape[2], whole.shape[1]
+    columns, wide = 3 * span + 256, width + EXTRA
     return pl.pallas_call(
         kernel_front,
         out_shape=(
@@ -448,7 +521,7 @@
             shape((16, 8 * used, columns - 3 * span), BF),
             shape((16, 8 * used, wide), BF),
             shape((16, 8 * used, EXTRA), BF),
-            shape((16,) + down.shape, BF),
+            shape((16, ROW_PAD, width), BF),
             shape((8,) + cot.shape, BF),
             shape((8, rows, EXTRA), BF),
             shape((group, width), BF),
@@ -457,21 +530,25 @@
             shape((8, width), F32),
             shape((rows, width), F32),
             shape((rows, width), BF),
-            shape((8, rows, width), BF),
+            shape((rows, width), BF),
+            shape((rows, 1), F32),
         ),
-        in_specs=[anyspace] * 3 + [vmem] + [anyspace] + [vmem] * 3,
-        out_specs=(anyspace,) * 7 + (vmem,) * 6 + (anyspace,),
+        in_specs=[vmem, anyspace] + [vmem] * 15,
+        out_specs=(anyspace,) * 7 + (vmem,) * 8,
         scratch_shapes=[
+            pltpu.VMEM((8, ROW_PAD, columns), BF),
+            pltpu.VMEM((ROW_PAD, wide), BF),
+            pltpu.VMEM((ROW_PAD, width), BF),
+            pltpu.VMEM((rows, wide), BF),
             pltpu.VMEM((8, ROW_PAD, columns), BF),
             pltpu.VMEM((8, ROW_PAD, wide), BF),
             pltpu.VMEM((8 * used, columns), BF),
             pltpu.VMEM((8 * used, wide), BF),
             pltpu.VMEM((16, 8 * used, columns), BF),
             pltpu.VMEM((16, 8 * used, wide), BF),
-            pltpu.VMEM((8,) + tok.shape, BF),
+            pltpu.VMEM((8, rows, wide), BF),
             pltpu.VMEM((8, rows, span), BF),
             pltpu.VMEM((rows, 8 * span), BF),
-            pltpu.VMEM((rows, width), BF),
             pltpu.VMEM((8, group), F32),
             pltpu.SemaphoreType.DMA((200,)),
             pltpu.SemaphoreType.DMA((200,)),
@@ -480,7 +557,10 @@
             collective_id=0, has_side_effects=True, vmem_limit_bytes=VMEM_LIMIT
         ),
         name="front",
-    )(slices, whole, down, tok, cot, live, cosine, sine)
+    )(
+        tok, cot, length, mask, routes, w_query, w_key, w_value, w_output, w_route,
+        shared_gate, shared_up, shared_down, norm_attn, norm_ffn, cosine, sine,
+    )
 
 
 def add_into(out, terms):
@@ -656,7 +736,7 @@
     cp.arrived(own)
 
 
-def expert_stream(cp, place, grid, sent, kept, got, bufs, total, at, ring_first, free, again):
+def expert_stream(cp, place, grid, sent, kept, got, bufs, total, at, ring_first, z_first, free, again):
     neighbours = rep_peers(place)
     if again:
         pl.semaphore_wait(free, len(neighbours))
@@ -670,7 +750,7 @@
     if not again:
         for device in neighbours:
             pl.semaphore_signal(free, inc=1, device_id=device, device_id_type=MESH)
-    yield from gather_expert(cp, place, grid, total, at, True)
+    yield from gather_expert(cp, place, grid, total, at, z_first)
 
 
 def dense_stream(cp, place, grid, grad, got, bufs, total, ring_first):
@@ -778,66 +858,83 @@
         done += take
 
 
-def one_expert(blocks, x, g, w_gate, w_up, w_down, weight, wact, g_a, g_b, outs, grads, q_sum, first):
-    width = g.shape[1]
-
-    @pl.loop(*blocks)
+def one_expert(
+    loop, blocks, x, g, w_gate, w_up, w_down, weight, wact, g_a, g_b, outs, grads, before, q_sum, first
+):
+    width = g.shape[2]
+
+    @pl.loop(*loop)
     def _(i):
-        at = pl.ds(pl.multiple_of(i * BLOCK, BLOCK), BLOCK)
-        share = weight(at)
-        gate = dot(x[at, :], w_gate[...])
-        up = dot(x[at, :], w_up[...])
-        raw = dot_nt(g[at, :], w_down[...])
+        pair = blocks(i)
+
+        def load(ref):
+            return jnp.concatenate([ref[b] for b in pair], axis=0)
+
+        def store(ref, value):
+            for n, b in enumerate(pair):
+                ref[b] = value[n * (BLOCK // 2) : (n + 1) * (BLOCK // 2)]
+
+        if before is not None:
+            before(pair, load, store)
+        share = weight(load)
+        rows = load(x)
+        gate = dot(rows, w_gate[...])
+        up = dot(rows, w_up[...])
+        raw = dot_nt(load(g), w_down[...])
         sig = 1.0 / (1.0 + jnp.exp(-gate))
         silu = gate * sig
         act = silu * up
         if q_sum is not None:
-            q_sum(i, at, jnp.sum(act * raw, axis=1, keepdims=True))
+            q_sum(pair, load, jnp.sum(act * raw, axis=1, keepdims=True))
         low = (act * share).astype(BF)
-        wact[at, :] = low
+        store(wact, low)
         raw = raw * share
         a = (raw * up * (sig + silu * (1.0 - sig))).astype(BF)
         b = (raw * silu).astype(BF)
-        g_a[at, :] = a
-        g_b[at, :] = b
-        shape = (2, BLOCK // 2, width)
-        part = dot(low, w_down[...]).reshape(shape)
-        back = (dot_nt(a, w_gate[...]) + dot_nt(b, w_up[...])).reshape(shape)
-        if not first:
-            part += outs[i].astype(F32)
-            back += grads[i, :, :, :width].astype(F32)
-        outs[i] = part.astype(BF)
-        grads[i, :, :, :width] = back.astype(BF)
+        store(g_a, a)
+        store(g_b, b)
+        part = dot(low, w_down[...])
+        back = dot_nt(a, w_gate[...]) + dot_nt(b, w_up[...])
+        for n, k in enumerate(pair):
+            at = slice(n * (BLOCK // 2), (n + 1) * (BLOCK // 2))
+            more, behind = part[at], back[at]
+            if not first:
+                more += outs[k // 2, k % 2].astype(F32)
+                behind += grads[k // 2, k % 2, :, :width].astype(F32)
+            outs[k // 2, k % 2] = more.astype(BF)
+            grads[k // 2, k % 2, :, :width] = behind.astype(BF)
 
 
 ORDER_A = (
-    "p0", "g0", "u0", "d0", "G0", "sp", "G0", "U0", "D0", "q1", "G0", "U0", "r1", "G0",
-    "U0", "D0", "x", "g1", "G0", "G0", "X0", "D0", "U0", "u1", "G0", "G0", "G1", "U0",
-    "X1", "D0", "d1", "U0", "U1", "G0", "G0", "D0", "ss", "X0", "G1", "D1",
+    "A", "A", "p0", "A", "p1", "A", "p2", "p3", "g0", "d0", "u0", "G0", "sp", "G0",
+    "U0", "D0", "w1", "q1", "G0", "U0", "r1", "G0", "U0", "D0", "pr", "x", "g1", "G0",
+    "X0", "D0", "U0", "u1", "G1", "G0", "G0", "G0", "ss", "G0", "X1", "U1", "G1", "D0",
+    "d1", "X0", "U0", "U0", "U1", "G0", "G0", "X1", "D1",
 )
 ORDER_B = (
-    "X1", "U0", "X0", "D0", "U0", "U1", "D1", "D0", "G1", "X1", "n2", "U0", "U0", "D0",
-    "G1", "U1", "dw", "D1", "sn", "D0", "D0", "G1", "o", "G1", "U1", "D1", "h0", "G1",
-    "G1", "U1", "U1", "D1", "W", "S", "D1", "N", "O", "h1", "G1", "G1", "U1", "U1",
-    "D1", "O", "hp", "D1", "S", "dq", "N", "U1", "U1", "H0", "D1", "D1", "S", "N",
-    "Q", "W", "H1", "Q", "O", "S", "W", "N", "H0", "Q", "H1", "H0", "W", "Q",
-    "H1", "n1",
+    "sn", "o", "G1", "S", "N", "X0", "D0", "X1", "n2", "O", "U1", "G1", "U0", "U0",
+    "dw", "D1", "S", "U1", "N", "O", "G1", "D0", "h0", "D1", "U1", "G1", "W", "O",
+    "S", "U0", "U0", "h1", "D1", "G1", "hp", "dq", "U1", "U1", "H0", "U1", "G1", "G1",
+    "G1", "Q", "U1", "U1", "Q", "H1", "W", "S", "Q", "H0", "W", "Q", "D1", "D1",
+    "H1", "N", "W", "H0", "D0", "D0", "D0", "D0", "D0", "D1", "H1", "n1", "N", "D1",
+    "D1", "D1",
 )
+Y_FIRST = ((0, 0), (0, 2))
 
 
 def kernel_rest(
     experts, top,
-    x_all, g_all, e_gate, e_up, e_down, h_probs, h_hidden, h_qkv, w_slices, h_whole,
+    x_own, g_all, e_gate, e_up, e_down, h_probs, h_hidden, h_qkv, w_slices, h_whole,
     h_residual, h_cot, h_tok, h_attended, h_cosine, h_sine,
     extra, w_router, s_both, s_padded, live, gains,
     out, d_tok, x_gate, x_up, x_down, o_qkv, o_shared, o_whole, o_down,
-    m_grads, m_outs, b_grads, b_outs, total_grads, total_hidden, e_got, e_bufs, e_total,
+    x, m_grads, m_outs, b_grads, b_outs, total_grads, total_hidden, e_got, e_bufs, e_total,
     v_shared, v_down, got, bufs, g_heads, probs, free, send_sem, recv_sem,
 ):
     place = Place()
     cp = Copies(send_sem, recv_sem)
-    group, width = x_all.shape
-    rows = group // 8
+    rows, width = x_own.shape
+    group = 8 * rows
     mine, core = place.ep, place.core
     ge, gr = grid_ep(place), grid_rep(place)
     wide = width + EXTRA
@@ -857,64 +954,70 @@
     ours = pl.ds(pl.multiple_of(core * half, 128), half)
     theirs = pl.ds(pl.multiple_of(place.mate * half, 128), half)
     streams = {}
+    from_x, from_z = place.from_x, place.from_z
 
     def view(ref, c):
         return ref.at[:, :, :, c]
 
     def phase_a(
-        x, g, w_gate, w_up, w_down, wact, g_a, g_b, gates, named,
+        g, w_gate, w_up, w_down, wact, g_a, g_b, gates, named,
         swact, sg_a, sg_b, s_down, d_sdown, d_gate, d_up, d_down,
     ):
-        first = [cp.local(a, b) for a, b in ((x_all, x), (g_all, g))]
+        first = [cp.local(g_all, g)]
         weights = ((e_gate, w_gate), (e_up, w_up), (e_down, w_down))
         loads = [cp.local(a.at[0], b) for a, b in weights]
         greet(ep_peers(place) + rep_peers(place))
+        streams["A"] = gather_ep(cp, place, x_own, Later(x), width)
+        next(streams["A"])
         for copy in first:
             cp.arrived(copy)
         lane = lax.broadcasted_iota(jnp.int32, (BLOCK, EXTRA), 1)
 
-        def router(at, lanes):
-            logits = jnp.where(lanes < experts, dot(x[at, :], w_router[...]), -1e30)
+        def router(values, lanes):
+            logits = jnp.where(lanes < experts, dot(values, w_router[...]), -1e30)
             weights = jnp.exp(logits - jnp.max(logits, axis=1, keepdims=True))
             return weights / jnp.sum(weights, axis=1, keepdims=True)
 
-        @pl.loop(0, group // BLOCK)
-        def _(i):
-            at = pl.ds(pl.multiple_of(i * BLOCK, BLOCK), BLOCK)
-            prob = router(at, lane)
-            routes = extra[at, :].astype(F32).astype(jnp.int32)
-            chosen = lane == routes[:, 0:1]
+        def route(pair, load, store):
+            prob = router(load(x), lane)
+            routes = load(extra)
+            whole = routes.astype(F32).astype(jnp.int32)
+            chosen = lane == whole[:, 0:1]
             for j in range(1, top):
-                chosen = chosen | (lane == routes[:, j : j + 1])
-            named[at, :] = jnp.where(chosen, 1.0, 0.0)
-            alive = extra[at, top : top + 1].astype(F32)
-            gates[at, :] = jnp.where(chosen, prob, 0.0) * alive
-            m_grads[i, :, :, width:] = jnp.zeros((2, BLOCK // 2, EXTRA), BF)
-
-        probs[...] = router(pl.ds(pl.multiple_of(mine * rows, rows), rows), lane[:rows])
+                chosen = chosen | (lane == whole[:, j : j + 1])
+            store(named, jnp.where(chosen, 1.0, 0.0))
+            store(gates, jnp.where(chosen, prob, 0.0) * routes[:, top : top + 1].astype(F32))
+            for b in pair:
+                m_grads[b // 2, b % 2, :, width:] = jnp.zeros((BLOCK // 2, EXTRA), BF)
 
         shared = s_down.shape[0]
         used = s_padded.shape[0] // ROW_PAD * 7 // 16
         steps = group // BLOCK
+        in_turn = lambda i: (2 * i, 2 * i + 1)
+        flat = lambda ref: ref[...].reshape(group, ref.shape[2])
+        columns_of = lambda ref, c: ref[:, :, c : c + BLOCK].reshape(group, BLOCK)
+        arrivals = (
+            (place.ep, from_x[-1]), (from_x[1], from_z[0]), (from_x[2], from_z[-1]), (from_z[1], from_z[2]),
+        )
 
         def shared_pass():
             pack = spread_matrix(shared, 16, used).astype(BF)
             s_down[...] = dot(pack, s_padded[...]).astype(BF)
             one_expert(
-                (0, steps), x, g, s_both.at[:, :shared], s_both.at[:, shared:], s_down,
-                lambda at: extra[at, top : top + 1].astype(F32),
-                swact, sg_a, sg_b, m_outs, m_grads, None, False,
+                (0, steps), in_turn, x, g, s_both.at[:, :shared], s_both.at[:, shared:], s_down,
+                lambda load: load(extra)[:, top : top + 1].astype(F32),
+                swact, sg_a, sg_b, m_outs, m_grads, None, None, False,
             )
 
         def shared_sums():
             for c in range(0, width, BLOCK):
-                left = x[:, c : c + BLOCK]
+                left = columns_of(x, c)
                 for n, back in enumerate((sg_a, sg_b)):
                     store_rows(
                         v_shared, (4, 2, 2), slice(n * shared, (n + 1) * shared), c,
-                        dot_tn(left, back[...]).astype(BF),
+                        dot_tn(left, flat(back)).astype(BF),
                     )
-            d_sdown[...] = dot_tn(swact[...], g[...]).astype(BF)
+            d_sdown[...] = dot_tn(flat(swact), flat(g)).astype(BF)
             pack = spread_matrix(shared, 16, used).astype(BF)
             for c in range(0, s_padded.shape[0], BLOCK):
                 store_rows(
@@ -922,32 +1025,35 @@
                     dot_tn(pack[:, c : c + BLOCK], d_sdown[...]).astype(BF),
                 )
 
-        def expert_pass(e, part):
+        def expert_pass(e, loop, blocks):
             expert = mine * exp_dev + e
 
-            def picked(at):
-                return jnp.sum(jnp.where(lane == expert, gates[at, :], 0.0), axis=1, keepdims=True)
-
-            def q_sum(i, at, value):
-                old = m_grads[i, :, :, width:].reshape(BLOCK, EXTRA).astype(F32)
-                new = jnp.where(lane == expert, value * named[at, :], old)
-                m_grads[i, :, :, width:] = new.astype(BF).reshape(2, BLOCK // 2, EXTRA)
-
-            if part[0] == 0:
-                for copy in loads:
-                    cp.arrived(copy)
-                loads.clear()
+            def picked(load):
+                return jnp.sum(jnp.where(lane == expert, load(gates), 0.0), axis=1, keepdims=True)
+
+            def q_sum(pair, load, value):
+                value = value * load(named)
+                for n, b in enumerate(pair):
+                    at = slice(n * (BLOCK // 2), (n + 1) * (BLOCK // 2))
+                    old = m_grads[b // 2, b % 2, :, width:].astype(F32)
+                    new = jnp.where(lane[: BLOCK // 2] == expert, value[at], old)
+                    m_grads[b // 2, b % 2, :, width:] = new.astype(BF)
+
+            for copy in loads:
+                cp.arrived(copy)
+            loads.clear()
             one_expert(
-                part, x, g, w_gate, w_up, w_down, picked,
-                wact, g_a, g_b, m_outs, m_grads, q_sum, e == 0,
+                loop, blocks, x, g, w_gate, w_up, w_down, picked,
+                wact, g_a, g_b, m_outs, m_grads, route if e == 0 else None, q_sum, e == 0,
             )
-            if part[1] == steps and e + 1 < exp_dev:
-                loads.extend(cp.local(a.at[e + 1], b) for a, b in weights)
+
+        def next_weights(e):
+            loads.extend(cp.local(a.at[e], b) for a, b in weights)
 
         def stream(e, n, sent, kept, at, ring_first):
             streams["GUD"[n] + str(e)] = one = expert_stream(
                 cp, place, gr, sent, kept, e_got[n], e_bufs[n], e_total[e][n], at, ring_first,
-                free.at[n], e > 0,
+                (e, n) not in Y_FIRST, free.at[n], e > 0,
             )
             next(one)
 
@@ -956,7 +1062,7 @@
                 d, back, x_out = ((d_gate, g_a, x_gate), (d_up, g_b, x_up))[n]
                 for c in range(0, width, BLOCK):
                     store_rows(
-                        d, (2, 4, 2), slice(0, hidden), c, dot_tn(x[:, c : c + BLOCK], back[...]).astype(BF)
+                        d, (2, 4, 2), slice(0, hidden), c, dot_tn(columns_of(x, c), flat(back)).astype(BF)
                     )
                 stream(
                     e, n, d.at[place.mate], d.at[core],
@@ -964,13 +1070,15 @@
                 )
             else:
                 for c in range(0, hidden, 128):
-                    store_rows(
-                        d_down, (4, 2), slice(0, width), c, dot_tn(wact[:, c : c + 128], g[...]).astype(BF)
-                    )
+                    left = wact[:, :, c : c + 128].reshape(group, 128)
+                    store_rows(d_down, (4, 2), slice(0, width), c, dot_tn(left, flat(g)).astype(BF))
                 stream(
                     e, n, d_down.at[:, :, :, theirs], d_down.at[:, :, :, ours],
-                    lambda k, z: x_down.at[e, place.y_at[k], z, :, ours], False,
+                    lambda k, z: x_down.at[e, place.y_at[k], z, :, ours], True,
                 )
+
+        def own_probs():
+            probs[...] = router(x[mine], lane[:rows])
 
         def start_x():
             for n, (c, b) in enumerate(zip(cuts, b_grads)):
@@ -979,12 +1087,13 @@
                 )
                 next(one)
 
-        pieces = {"sp": shared_pass, "ss": shared_sums, "x": start_x}
+        pieces = {"sp": shared_pass, "ss": shared_sums, "x": start_x, "w1": functools.partial(next_weights, 1)}
+        for n, pair in enumerate(arrivals):
+            pieces["p" + str(n)] = functools.partial(expert_pass, 0, (0, 1), lambda i, pair=pair: pair)
+        pieces["q1"] = functools.partial(expert_pass, 1, (0, steps // 2), in_turn)
+        pieces["r1"] = functools.partial(expert_pass, 1, (steps // 2, steps), in_turn)
+        pieces["pr"] = own_probs
         for e in range(exp_dev):
-            half_steps = steps // 2
-            pieces["p" + str(e)] = functools.partial(expert_pass, e, (0, steps))
-            pieces["q" + str(e)] = functools.partial(expert_pass, e, (0, half_steps))
-            pieces["r" + str(e)] = functools.partial(expert_pass, e, (half_steps, steps))
             for n in range(3):
                 pieces["gud"[n] + str(e)] = functools.partial(expert_sums, e, n)
         follow(ORDER_A, pieces)
@@ -998,14 +1107,13 @@
 
     pl.run_scoped(
         phase_a,
-        pltpu.VMEM((group, width), BF),
-        pltpu.VMEM((group, width), BF),
+        pltpu.VMEM((8, rows, width), BF),
         pltpu.VMEM((width, hidden), BF),
         pltpu.VMEM((width, hidden), BF),
         pltpu.VMEM((hidden, width), BF),
-        *[pltpu.VMEM((group, hidden), BF)] * 3,
-        *[pltpu.VMEM((group, EXTRA), F32)] * 2,
-        *[pltpu.VMEM((group, s_both.shape[1] // 2), BF)] * 3,
+        *[pltpu.VMEM((8, rows, hidden), BF)] * 3,
+        *[pltpu.VMEM((8, rows, EXTRA), F32)] * 2,
+        *[pltpu.VMEM((8, rows, s_both.shape[1] // 2), BF)] * 3,
         *[pltpu.VMEM((s_both.shape[1] // 2, width), BF)] * 2,
         pltpu.VMEM((2, 4, 2, half_part, hidden), BF),
         pltpu.VMEM((2, 4, 2, half_part, hidden), BF),
@@ -1013,7 +1121,7 @@
     )
 
     def phase_b(
-        v_probs, v_hidden, v_qkvs, v_w, w_whole, residual, cot, tok, attended, cosine, sine,
+        v_probs, v_qkvs, v_w, w_whole, residual, cot, tok, attended, cosine, sine,
         v_whole, v_qkv, totals, padded, g_att, g_residual, g_keys, g_values, g_qkv, g_branch,
     ):
         loads = [
@@ -1021,7 +1129,7 @@
             for a, b in (
                 (h_residual, residual), (h_cot, cot), (h_whole, w_whole), (h_attended, attended),
                 (h_qkv, v_qkvs), (h_probs, v_probs), (h_cosine, cosine), (h_sine, sine),
-                (w_slices.at[:, : v_w.shape[1]], v_w), (h_hidden, v_hidden), (h_tok, tok),
+                (w_slices.at[:, : v_w.shape[1]], v_w), (h_hidden, x), (h_tok, tok),
             )
         ]
         alive = live[...]
@@ -1129,7 +1237,7 @@
             for i in range(2):
                 c = slice(i * width // 2, (i + 1) * width // 2)
                 v_qkv[2 * i : 2 * i + 2] = (
-                    dot_tn(v_hidden[:, c], g_qkv[...]).astype(BF).reshape(2, 2, 2, width // 16, 3 * span)
+                    dot_tn(x[:, :, c].reshape(group, width // 2), g_qkv[...]).astype(BF).reshape(2, 2, 2, width // 16, 3 * span)
                 )
             dense("Q", 3, v_qkv, True, 2, o_qkv)
 
@@ -1167,7 +1275,6 @@
     pl.run_scoped(
         phase_b,
         pltpu.VMEM(h_probs.shape, BF),
-        pltpu.VMEM(h_hidden.shape, BF),
         pltpu.VMEM(h_qkv.shape, BF),
         pltpu.VMEM((width, 3 * span), BF),
         pltpu.VMEM(h_whole.shape, BF),
@@ -1187,7 +1294,7 @@
 
 
 def call_rest(
-    experts, top, x_all, g_all, e_gate, e_up, e_down, h_probs, h_hidden, h_qkv, w_slices, h_whole,
+    experts, top, x_own, g_all, e_gate, e_up, e_down, h_probs, h_hidden, h_qkv, w_slices, h_whole,
     h_residual, h_cot, h_tok, h_attended, h_cosine, h_sine,
     extra, w_router, s_both, s_padded, live, gains,
 ):
@@ -1221,6 +1328,7 @@
         in_specs=[anyspace] * 16 + [vmem] * 6,
         out_specs=(vmem, vmem) + (anyspace,) * 6 + (vmem,),
         scratch_shapes=[
+            pltpu.VMEM((8, rows, width), BF),
             pltpu.VMEM((4, 2, rows, wide), BF),
             pltpu.VMEM((4, 2, rows, width), BF),
             [ring_pair_bufs(rows, c) for c in (cut, wide - cut)],
@@ -1228,7 +1336,7 @@
             pltpu.VMEM((rows, wide), F32),
             pltpu.VMEM((rows, width), F32),
             [pltpu.VMEM((4, 2) + h, BF) for h in halves],
-            [bufs_of(first, *h) for first, h in zip((True, True, False), halves)],
+            [ring_pair_bufs(*h) for h in halves],
             [[pltpu.VMEM(h, BF) for h in halves] for _ in range(exp_dev)],
             pltpu.VMEM((4, 2, 2, part, columns[1]), BF),
             pltpu.VMEM((4, 2, 2, ROW_PAD, width), BF),
@@ -1245,14 +1353,88 @@
         ),
         name="rest",
     )(
-        x_all, g_all, e_gate, e_up, e_down, h_probs, h_hidden, h_qkv, w_slices, h_whole,
+        x_own, g_all, e_gate, e_up, e_down, h_probs, h_hidden, h_qkv, w_slices, h_whole,
         h_residual, h_cot, h_tok, h_attended, h_cosine, h_sine,
         extra, w_router, s_both, s_padded, live, gains,
     )
 
 
-def pad_rows(values, rows):
-    return jnp.pad(values, ((0, rows - values.shape[0]),) + ((0, 0),) * (values.ndim - 1))
+def kernel_finish(
+    o_qkv, o_shared, o_whole, o_down, w_query, w_key, w_value, norm_attn, b_gate, b_up, b_down,
+    d_query, d_key, d_value, d_output, d_router, d_sgate, d_sup, d_sdown, d_norm_one, d_norm_two,
+    d_gate, d_up, d_down,
+):
+    used, width = w_query.shape
+    hidden = d_sgate.shape[1]
+    span = HEADS_DEV * HD
+    for low, full in ((b_gate, d_gate), (b_up, d_up), (b_down, d_down)):
+        full[...] = low[...].astype(F32)
+
+    step = pl.program_id(0)
+
+    @pl.when(step == 1)
+    def _():
+        gain = jnp.zeros((used, 1), F32)
+        for n, (w, d) in enumerate(((w_query, d_query), (w_key, d_key), (w_value, d_value))):
+            for owner in range(width // span):
+                c = slice(owner * span, (owner + 1) * span)
+                part = o_qkv[owner, :used, n * span : (n + 1) * span].astype(F32)
+                d[:, c] = part
+                gain += jnp.sum(part * w[:, c].astype(F32), axis=1, keepdims=True)
+        d_norm_one[...] = as_row(gain) / norm_attn[...].astype(F32)
+
+    for n, d in enumerate((d_sgate, d_sup)):
+        for half in range(2):
+
+            @pl.when(step == 3 + 4 * n + 2 * half)
+            def _(n=n, d=d, half=half):
+                total = jnp.zeros((ROW_PAD, hidden), F32)
+                for owner in range(4 * half, 4 * half + 4):
+                    pick = shared_columns(owner, hidden, d_sdown.shape[0])
+                    total += dot_nt(o_shared[owner, :, n * 128 : (n + 1) * 128], pick)
+                d[...] = total[:used] if half == 0 else d[...] + total[:used]
+
+    @pl.when(step == 11)
+    def _():
+        total = o_whole[0].astype(F32)
+        for i in range(1, 8):
+            total += o_whole[i].astype(F32)
+        d_output[...] = total[:used, :width]
+        d_router[...] = total[:used, width : width + d_router.shape[1]]
+        d_norm_two[...] = as_row(total[:used, width + EXTRA - 1 :])
+        d_sdown[...] = o_down[: d_sdown.shape[0]].astype(F32)
+
+
+def call_finish(
+    o_qkv, o_shared, o_whole, o_down, w_query, w_key, w_value, norm_attn, b_gate, b_up, b_down,
+    experts, hidden,
+):
+    used, width = w_query.shape
+    down_used = hidden // 128
+    shape = jax.ShapeDtypeStruct
+    steps = 16
+    fixed = lambda a: pl.BlockSpec(a.shape, lambda i: (0,) * len(a.shape))
+    part = lambda a: pl.BlockSpec((a.shape[0] // steps, a.shape[1]), lambda i: (i, 0))
+    small = (
+        [shape((used, width), F32)] * 4
+        + [shape((used, experts), F32)]
+        + [shape((used, hidden), F32)] * 2
+        + [shape((down_used, width), F32)]
+        + [shape((1, used), F32)] * 2
+    )
+    large = [shape(a.shape, F32) for a in (b_gate, b_up, b_down)]
+    operands = (o_qkv, o_shared, o_whole, o_down, w_query, w_key, w_value, norm_attn)
+    return pl.pallas_call(
+        kernel_finish,
+        grid=(steps,),
+        out_shape=tuple(small + large),
+        in_specs=[fixed(a) for a in operands] + [part(a) for a in (b_gate, b_up, b_down)],
+        out_specs=tuple([fixed(a) for a in small] + [part(a) for a in large]),
+        compiler_params=pltpu.CompilerParams(
+            vmem_limit_bytes=VMEM_LIMIT, dimension_semantics=("arbitrary",)
+        ),
+        name="finish",
+    )(*operands, b_gate, b_up, b_down)
 
 
 def body(
@@ -1262,106 +1444,44 @@
     expert_gate, expert_up, expert_down,
 ):
     rows, width = tokens.shape
-    top = routes.shape[1]
     used = w_query.shape[0]
-    hidden = expert_gate.shape[2]
+    exp_dev, _, hidden = expert_gate.shape
     experts = w_router.shape[1]
-    exp_dev = expert_gate.shape[0]
-    ep = lax.axis_index("ep")
     group = rows * 8
-    span = HEADS_DEV * HD
-    owners = width // span
-    down_used = shared_down.shape[0]
-    shared_cols = 16 * down_used
-
-    def by_owner(w):
-        return jnp.pad(w.reshape(used, owners, span), ((0, 0), (0, 8 - owners), (0, 0)))
-
-    def by_shared(w):
-        w = w.reshape(used, 16, 8, down_used).transpose(0, 2, 1, 3).reshape(used, 8, shared_cols)
-        return w
-
-    gains = jnp.broadcast_to(jnp.stack([norm_attn, norm_ffn], axis=1)[:, None], (used, 8, 2))
-    zeros = lambda n: jnp.zeros((used, 8, n), BF)
-    slices = jnp.concatenate(
-        [
-            by_owner(w_query), by_owner(w_key), by_owner(w_value),
-            by_shared(shared_gate), gains, zeros(126 - shared_cols),
-            by_shared(shared_up), zeros(128 - shared_cols),
-        ],
-        axis=2,
-    ).transpose(1, 0, 2)
-    slices = jnp.pad(slices, ((0, 0), (0, ROW_PAD - used), (0, 0)))
-    whole = jnp.concatenate([w_output, w_router], axis=1)
-    whole = jnp.pad(whole, ((0, ROW_PAD - used), (0, width + EXTRA - whole.shape[1])))
-    down = pad_rows(shared_down, ROW_PAD)
-    position = ep * rows + jnp.arange(rows, dtype=jnp.int32)
-    live_own = ((position < lengths[0]) & (token_mask == 1)).astype(F32)
-    tok_wide = jnp.concatenate(
-        [
-            tokens,
-            jnp.pad(
-                jnp.concatenate([routes.astype(BF), live_own[:, None].astype(BF)], axis=1),
-                ((0, 0), (0, EXTRA - top - 1)),
-            ),
-        ],
-        axis=1,
-    )
     frequency = 10000.0 ** (-(np.arange(HD // 2, dtype=np.float32) * np.float32(2.0) / HD))
     angles = np.arange(group, dtype=np.float32)[:, None] * frequency.astype(np.float32)[None, :]
     cosine = jnp.asarray(np.tile(np.cos(angles), (1, 2)), F32)
     sine = jnp.asarray(np.concatenate([-np.sin(angles), np.sin(angles)], axis=1), F32)
-    live_col = live_own[:, None]
     (
         w_slices, w_both, w_whole, w_router_all, w_down, cot_all, extra,
-        hidden_one, qkv, attn_probs, gain_rows, residual, attended, hidden_all,
-    ) = call_front(slices, whole, down, tok_wide, cotangent, live_col, cosine, sine, used)
-    w_slices = w_slices.reshape(width, -1)
-    w_whole = w_whole.reshape(width, -1)
+        hidden_one, qkv, attn_probs, gain_rows, residual, attended, hidden_two, live,
+    ) = call_front(
+        tokens, cotangent, lengths[None], token_mask[None], routes.T,
+        w_query, w_key, w_value, w_output, w_router,
+        shared_gate, shared_up, shared_down, norm_attn[None], norm_ffn[None], cosine, sine,
+    )
     out, d_tokens, e_gate, e_up, e_down, o_qkv, o_shared, o_whole, o_down = call_rest(
-        experts, top,
-        hidden_all.reshape(group, width), cot_all.reshape(group, width),
-        expert_gate, expert_up, expert_down, attn_probs, hidden_one, qkv, w_slices, w_whole,
+        experts, routes.shape[1],
+        hidden_two, cot_all, expert_gate, expert_up, expert_down,
+        attn_probs, hidden_one.reshape(8, rows, width), qkv,
+        w_slices.reshape(width, -1), w_whole.reshape(width, -1),
         residual, cotangent, tokens, attended, cosine, sine,
-        extra.reshape(group, EXTRA), w_router_all.reshape(width, EXTRA),
-        w_both.reshape(width, -1), w_down.reshape(-1, width), live_col, gain_rows,
+        extra, w_router_all.reshape(width, EXTRA),
+        w_both.reshape(width, -1), w_down.reshape(-1, width), live, gain_rows,
     )
-    o_qkv = o_qkv[:owners, :used].astype(F32)
-    o_shared = o_shared[:, :used].astype(F32)
-    o_whole = jnp.sum(o_whole[:, :used].astype(F32), axis=0)
-
-    def from_owner(i):
-        return o_qkv[:, :, i * span : (i + 1) * span].transpose(1, 0, 2).reshape(used, width)
-
-    def from_shared(i):
-        return (
-            o_shared[:, :, 128 * i : 128 * i + shared_cols]
-            .reshape(8, used, 16, down_used)
-            .transpose(1, 2, 0, 3)
-            .reshape(used, hidden)
-        )
-
-    d_query, d_key, d_value = (from_owner(i) for i in range(3))
-    d_gain_one = sum(
-        jnp.sum(w.astype(F32) * d, axis=1)
-        for w, d in ((w_query, d_query), (w_key, d_key), (w_value, d_value))
-    ) / norm_attn.astype(F32)
+    (
+        d_query, d_key, d_value, d_output, d_router, d_sgate, d_sup, d_sdown, d_norm_one, d_norm_two,
+        d_gate, d_up, d_down,
+    ) = call_finish(
+        o_qkv, o_shared, o_whole, o_down, w_query, w_key, w_value, norm_attn[None],
+        e_gate.reshape(-1, hidden), e_up.reshape(-1, hidden), e_down.reshape(-1, width),
+        experts, hidden,
+    )
     return (
-        out,
-        d_tokens,
-        d_query,
-        d_key,
-        d_value,
-        o_whole[:, :width],
-        o_whole[:, width : width + experts],
-        from_shared(0),
-        from_shared(1),
-        o_down[:down_used].astype(F32),
-        d_gain_one,
-        o_whole[:, width + EXTRA - 1],
-        e_gate.reshape(exp_dev, width, hidden).astype(F32),
-        e_up.reshape(exp_dev, width, hidden).astype(F32),
-        e_down.reshape(exp_dev, hidden, width).astype(F32),
+        out, d_tokens, d_query, d_key, d_value, d_output, d_router, d_sgate, d_sup, d_sdown,
+        d_norm_one.reshape(used), d_norm_two.reshape(used),
+        d_gate.reshape(exp_dev, width, hidden), d_up.reshape(exp_dev, width, hidden),
+        d_down.reshape(exp_dev, hidden, width),
     )
 
 

time: 348 us -> 309 us (0.89)
  the two profiles are of different devices: /device:TPU:0 before, /device:TPU:1 now
where the time goes in v4:
time: 309 us; the launch traced here: 303 us
  Pallas kernels  300 us (97%)
    pallas_call x1, Pallas kernels, call_rest(): pl.pallas_call(functools.partial(kernel_rest, experts, top), out_shape=(s...  199 us
    pallas_call x1, Pallas kernels, call_front(): pl.pallas_call(kernel_front, out_shape=(shape((16, 8 * used, columns), BF...  81.4 us
    pallas_call x1, Pallas kernels, call_finish(): pl.pallas_call(kernel_finish, grid=(steps,), out_shape=tuple(small + larg...  19.4 us

profile of v4, /device:TPU:1, one launch (start us, length us, event | category | flops | bytes accessed | tf_op | source)
XLA Modules:
  0.0 303.2 jit_solution(8312371117259736963)
XLA Ops:
  1.3 81.4 %front.1 = (bf16[16,80,1024]{2,1,0:T(8,128)(2,1)}, bf16[16,80,256]{2,1,0:T(8,128)(2,1)}, bf16[16,80,1408]{2,1,0:T(8,128)(2,1)}, bf16[16,80,128]{2,1,0:T(8,128)(2...) custom-call(bf16[128,1280]{1,0:T(8,128)(2,1)} %h_tok.1, ...), custom_call_target="tpu_custom_call" | custom-call | tf_op jit(solution)/shard_map/front/pallas_call | solution.py:517
  82.7 199.3 %rest.1 = (bf16[128,1280]{1,0:T(8,128)(2,1)}, f32[128,1280]{1,0:T(8,128)}, bf16[2,2,4,2,80,896]{5,4,3,2,1,0:T(8,128)(2,1)}, bf16[2,2,4,2,80,896]{5,4,3,2,1,0:T(8...) custom-call(bf16[128,1280]{1,0:T(8,128)(2,1)} %get-tuple-element.52., ...), custom_call_target="tpu_custom_call" | custom-call | tf_op jit(solution)/shard_map/rest/pallas_call | solution.py:1315
  282.0 0.0 copy-start.1
  282.0 0.0 copy-start
  282.0 19.4 %finish.1 = (f32[10,1280]{1,0:T(8,128)}, f32[10,1280]{1,0:T(8,128)}, f32[10,1280]{1,0:T(8,128)}, f32[10,1280]{1,0:T(8,128)}, f32[10,16]{1,0:T(8,128)}, /*index=5...) custom-call(bf16[8,16,768]{2,1,0:T(8,128)(2,1)} %get-tuple-element.6, ...), custom_call_target="tpu_custom_call" | custom-call | tf_op jit(solution)/shard_map/finish/pallas_call | solution.py:1427
  301.4 0.0 copy-done.1
  301.4 0.7 copy.38
  302.1 0.0 copy-done
  302.1 0.8 copy.39
Async XLA Ops:
  282.0 19.4 %copy-start.1 = (bf16[128,1280]{1,0:T(8,128)(2,1)S(1)}, bf16[128,1280]{1,0:T(8,128)(2,1)}, u32[]{:S(2)}) copy-start(bf16[128,1280]{1,0:T(8,128)(2,1)} %get-tuple-element.104) | copy-start | bytes 983044
  282.0 20.2 %copy-start = (f32[128,1280]{1,0:T(8,128)S(1)}, f32[128,1280]{1,0:T(8,128)}, u32[]{:S(2)}) copy-start(f32[128,1280]{1,0:T(8,128)} %get-tuple-element.105) | copy-start | bytes 1966084

commit v5 on v4

--- a/solution.py
+++ b/solution.py
@@ -348,18 +348,18 @@
 
 
 ORDER_F = (
-    "a", "k1", "T", "T", "L", "L", "T", "L", "k2", "L", "c", "L", "L", "T",
-    "pr", "W", "h0", "h1", "W", "W", "C", "C", "W", "C", "D", "D", "W", "D",
-    "D", "W", "D", "D", "op", "C",
+    "a", "k1", "wa", "T", "T", "L", "L", "T", "L", "k2", "L", "c", "L", "L",
+    "T", "pr", "W", "h0", "C", "h1", "W", "W", "C", "W", "C", "D", "D", "W",
+    "D", "D", "W", "D", "D", "op", "C",
 )
 
 
 def kernel_front(
     tok, cot, length, mask, routes, w_query, w_key, w_value, w_output, w_route,
-    shared_gate, shared_up, shared_down, norm_attn, norm_ffn, cosine, sine,
+    shared_gate, shared_up, shared_down, norm_attn, norm_ffn, h_cosine, h_sine,
     w_slices, w_both, w_whole, w_router, w_down, cot_all, extra,
-    hidden_one, qkv, probs, gains, residual, attended, hidden, live,
-    slices, whole, down, wide_tok,
+    o_hidden, o_qkv, o_probs, gains, residual, attended, hidden, live,
+    hidden_one, qkv, probs, cosine, sine, slices, whole, down, wide_tok,
     land_slices, land_whole, pack_slices, pack_whole, v_slices, v_whole, v_tok,
     heads, land_heads, live_row, send_sem, recv_sem,
 ):
@@ -399,6 +399,7 @@
             slices[owner, rows_of, 3 * span : 3 * span + 128] = gate.astype(BF)
             slices[owner, rows_of, 3 * span + 128 :] = dot(shared_up[...], pick).astype(BF)
 
+    tables = [cp.local(h_cosine, cosine), cp.local(h_sine, sine)]
     greet(ep_peers(place) + rep_peers(place), own_inputs)
     streams, kept = {}, {}
     used = pack_slices.shape[0] // 8
@@ -418,10 +419,12 @@
         kept["slices"] = [cp.local(slices.at[mine], land_slices.at[mine])] + [
             cp.send(slices.at[(mine + k) % 8], land_slices.at[mine], place.to_ep(k)) for k in range(1, 8)
         ]
+        start("T", gather_ep(cp, place, wide_tok, v_tok, wide_tok.shape[1]))
+
+    def to_all():
         kept["whole"] = [cp.local(whole, land_whole.at[mine])] + [
             cp.send(whole, land_whole.at[mine], place.to_ep(k)) for k in range(1, 8)
         ]
-        start("T", gather_ep(cp, place, wide_tok, v_tok, wide_tok.shape[1]))
 
     def pack_first():
         for copy in kept["slices"]:
@@ -448,6 +451,9 @@
         live_row[...] = jnp.concatenate(
             [v_tok[i, :, width:].astype(F32).T[:8, :] for i in range(8)], axis=1
         )
+
+        for copy in tables:
+            cp.arrived(copy)
 
         @pl.loop(0, group // BLOCK)
         def _(i):
@@ -463,8 +469,12 @@
                 qkv[at, c] = turn(raw[:, c], cos, sin).astype(BF)
             qkv[at, 2 * span :] = raw[:, 2 * span :].astype(BF)
 
+        cp.local(hidden_one, o_hidden)
+        cp.local(qkv, o_qkv)
+
     def head(h):
         attention_head(h, qkv, live_row, probs, heads)
+        cp.local(probs.at[h], o_probs.at[h])
         if h == HEADS_DEV - 1:
             column = pl.ds(pl.multiple_of(mine * span, 128), span)
             kept["heads"] = [cp.local(heads.at[mine], land_heads.at[:, column])] + [
@@ -490,7 +500,7 @@
         hidden[...] = (residual[...] * scale * gains[1:2, :]).astype(BF)
 
     pieces = {
-        "a": to_owners, "k1": pack_first, "k2": pack_second, "c": start_cot, "pr": projections,
+        "a": to_owners, "wa": to_all, "k1": pack_first, "k2": pack_second, "c": start_cot, "pr": projections,
         "h0": functools.partial(head, 0), "h1": functools.partial(head, 1), "op": output,
     }
     for name in ORDER_F:
@@ -533,9 +543,14 @@
             shape((rows, width), BF),
             shape((rows, 1), F32),
         ),
-        in_specs=[vmem, anyspace] + [vmem] * 15,
-        out_specs=(anyspace,) * 7 + (vmem,) * 8,
+        in_specs=[vmem, anyspace] + [vmem] * 13 + [anyspace] * 2,
+        out_specs=(anyspace,) * 10 + (vmem,) * 5,
         scratch_shapes=[
+            pltpu.VMEM((group, width), BF),
+            pltpu.VMEM((group, 3 * span), BF),
+            pltpu.VMEM((HEADS_DEV, group, group), BF),
+            pltpu.VMEM((group, HD), F32),
+            pltpu.VMEM((group, HD), F32),
             pltpu.VMEM((8, ROW_PAD, columns), BF),
             pltpu.VMEM((ROW_PAD, wide), BF),
             pltpu.VMEM((ROW_PAD, width), BF),
@@ -906,27 +921,27 @@
 
 
 ORDER_A = (
-    "A", "A", "p0", "A", "p1", "A", "p2", "p3", "g0", "d0", "u0", "G0", "sp", "G0",
-    "U0", "D0", "w1", "q1", "G0", "U0", "r1", "G0", "U0", "D0", "pr", "x", "g1", "G0",
-    "X0", "D0", "U0", "u1", "G1", "G0", "G0", "G0", "ss", "G0", "X1", "U1", "G1", "D0",
-    "d1", "X0", "U0", "U0", "U1", "G0", "G0", "X1", "D1",
+    "A", "A", "p0", "A", "p1", "A", "p2", "p3", "w1", "pr", "g0", "u0", "d0", "G0",
+    "sp", "G0", "U0", "D0", "q1", "G0", "U0", "r1", "G0", "U0", "D0", "x", "g1", "G0",
+    "G0", "X0", "D0", "U0", "u1", "G1", "G0", "G0", "D0", "X1", "d1", "U1", "G1", "U0",
+    "U0", "D0", "ss", "X0", "D1",
 )
 ORDER_B = (
-    "sn", "o", "G1", "S", "N", "X0", "D0", "X1", "n2", "O", "U1", "G1", "U0", "U0",
-    "dw", "D1", "S", "U1", "N", "O", "G1", "D0", "h0", "D1", "U1", "G1", "W", "O",
-    "S", "U0", "U0", "h1", "D1", "G1", "hp", "dq", "U1", "U1", "H0", "U1", "G1", "G1",
-    "G1", "Q", "U1", "U1", "Q", "H1", "W", "S", "Q", "H0", "W", "Q", "D1", "D1",
-    "H1", "N", "W", "H0", "D0", "D0", "D0", "D0", "D0", "D1", "H1", "n1", "N", "D1",
-    "D1", "D1",
+    "G0", "G0", "X1", "D0", "X0", "U1", "X1", "n2", "G1", "U0", "dw", "U0", "sn", "D0",
+    "o", "G1", "D1", "G1", "W", "h0", "O", "S", "N", "U1", "U0", "U0", "D0", "D0",
+    "D0", "h1", "O", "S", "G1", "G1", "D1", "N", "hp", "W", "S", "G1", "dq", "N",
+    "G1", "G1", "U1", "H0", "W", "Q", "O", "H1", "D1", "W", "S", "N", "Q", "U1",
+    "U1", "H0", "D1", "D1", "H1", "Q", "H0", "U1", "H1", "n1", "U1", "Q", "D1", "D1",
+    "U1", "U1", "D1", "D1",
 )
-Y_FIRST = ((0, 0), (0, 2))
+Y_FIRST = ()
 
 
 def kernel_rest(
     experts, top,
     x_own, g_all, e_gate, e_up, e_down, h_probs, h_hidden, h_qkv, w_slices, h_whole,
     h_residual, h_cot, h_tok, h_attended, h_cosine, h_sine,
-    extra, w_router, s_both, s_padded, live, gains,
+    h_extra, h_router, h_both, h_padded, live, gains,
     out, d_tok, x_gate, x_up, x_down, o_qkv, o_shared, o_whole, o_down,
     x, m_grads, m_outs, b_grads, b_outs, total_grads, total_hidden, e_got, e_bufs, e_total,
     v_shared, v_down, got, bufs, g_heads, probs, free, send_sem, recv_sem,
@@ -960,10 +975,11 @@
         return ref.at[:, :, :, c]
 
     def phase_a(
-        g, w_gate, w_up, w_down, wact, g_a, g_b, gates, named,
+        g, extra, w_router, s_both, s_padded, w_gate, w_up, w_down, wact, g_a, g_b, gates, named,
         swact, sg_a, sg_b, s_down, d_sdown, d_gate, d_up, d_down,
     ):
-        first = [cp.local(g_all, g)]
+        first = [cp.local(h_extra, extra), cp.local(h_router, w_router), cp.local(g_all, g)]
+        small = [cp.local(h_both, s_both), cp.local(h_padded, s_padded)]
         weights = ((e_gate, w_gate), (e_up, w_up), (e_down, w_down))
         loads = [cp.local(a.at[0], b) for a, b in weights]
         greet(ep_peers(place) + rep_peers(place))
@@ -1001,6 +1017,8 @@
         )
 
         def shared_pass():
+            for copy in small:
+                cp.arrived(copy)
             pack = spread_matrix(shared, 16, used).astype(BF)
             s_down[...] = dot(pack, s_padded[...]).astype(BF)
             one_expert(
@@ -1108,13 +1126,17 @@
     pl.run_scoped(
         phase_a,
         pltpu.VMEM((8, rows, width), BF),
+        pltpu.VMEM(h_extra.shape, BF),
+        pltpu.VMEM(h_router.shape, BF),
+        pltpu.VMEM(h_both.shape, BF),
+        pltpu.VMEM(h_padded.shape, BF),
         pltpu.VMEM((width, hidden), BF),
         pltpu.VMEM((width, hidden), BF),
         pltpu.VMEM((hidden, width), BF),
         *[pltpu.VMEM((8, rows, hidden), BF)] * 3,
         *[pltpu.VMEM((8, rows, EXTRA), F32)] * 2,
-        *[pltpu.VMEM((8, rows, s_both.shape[1] // 2), BF)] * 3,
-        *[pltpu.VMEM((s_both.shape[1] // 2, width), BF)] * 2,
+        *[pltpu.VMEM((8, rows, h_both.shape[1] // 2), BF)] * 3,
+        *[pltpu.VMEM((h_both.shape[1] // 2, width), BF)] * 2,
         pltpu.VMEM((2, 4, 2, half_part, hidden), BF),
         pltpu.VMEM((2, 4, 2, half_part, hidden), BF),
         pltpu.VMEM((4, 2, hidden // 8, width), BF),
@@ -1270,7 +1292,7 @@
         o_down[...] = totals[2][...]
         cp.finish()
 
-    columns = (wide, s_both.shape[1], width, 3 * span)
+    columns = (wide, h_both.shape[1], width, 3 * span)
     depth = (half_part, half_part, ROW_PAD, half_part)
     pl.run_scoped(
         phase_b,
@@ -1325,7 +1347,7 @@
             shape((8, ROW_PAD, wide), BF),
             shape((ROW_PAD, width), BF),
         ),
-        in_specs=[anyspace] * 16 + [vmem] * 6,
+        in_specs=[anyspace] * 20 + [vmem] * 2,
         out_specs=(vmem, vmem) + (anyspace,) * 6 + (vmem,),
         scratch_shapes=[
             pltpu.VMEM((8, rows, width), BF),
@@ -1383,18 +1405,16 @@
                 gain += jnp.sum(part * w[:, c].astype(F32), axis=1, keepdims=True)
         d_norm_one[...] = as_row(gain) / norm_attn[...].astype(F32)
 
-    for n, d in enumerate((d_sgate, d_sup)):
-        for half in range(2):
-
-            @pl.when(step == 3 + 4 * n + 2 * half)
-            def _(n=n, d=d, half=half):
-                total = jnp.zeros((ROW_PAD, hidden), F32)
-                for owner in range(4 * half, 4 * half + 4):
-                    pick = shared_columns(owner, hidden, d_sdown.shape[0])
-                    total += dot_nt(o_shared[owner, :, n * 128 : (n + 1) * 128], pick)
-                d[...] = total[:used] if half == 0 else d[...] + total[:used]
-
-    @pl.when(step == 11)
+    @pl.when(step == 2)
+    def _():
+        for n, d in enumerate((d_sgate, d_sup)):
+            total = jnp.zeros((ROW_PAD, hidden), F32)
+            for owner in range(8):
+                pick = shared_columns(owner, hidden, d_sdown.shape[0])
+                total += dot_nt(o_shared[owner, :, n * 128 : (n + 1) * 128], pick)
+            d[...] = total[:used]
+
+    @pl.when(step == 3)
     def _():
         total = o_whole[0].astype(F32)
         for i in range(1, 8):
@@ -1412,7 +1432,7 @@
     used, width = w_query.shape
     down_used = hidden // 128
     shape = jax.ShapeDtypeStruct
-    steps = 16
+    steps = 4
     fixed = lambda a: pl.BlockSpec(a.shape, lambda i: (0,) * len(a.shape))
     part = lambda a: pl.BlockSpec((a.shape[0] // steps, a.shape[1]), lambda i: (i, 0))
     small = (

time: 309 us -> 289 us (0.935)
  Pallas kernels: 300 us -> 281 us
    pallas_call x1, Pallas kernels: 81.4 us -> 70.9 us  [call_front(): pl.pallas_call(kernel_front, out_shape=(shape((16, 8 * used, columns), BF...]
    pallas_call x1, Pallas kernels: 19.4 us -> 14.5 us  [call_finish(): pl.pallas_call(kernel_finish, grid=(steps,), out_shape=tuple(small + larg...]
    pallas_call x1, Pallas kernels: 199 us -> 196 us  [call_rest(): pl.pallas_call(functools.partial(kernel_rest, experts, top), out_shape=(s...]
where the time goes in v5:
time: 289 us; the launch traced here: 284 us
  Pallas kernels  281 us (97%)
    pallas_call x1, Pallas kernels, call_rest(): pl.pallas_call(functools.partial(kernel_rest, experts, top), out_shape=(s...  196 us
    pallas_call x1, Pallas kernels, call_front(): pl.pallas_call(kernel_front, out_shape=(shape((16, 8 * used, columns), BF...  70.9 us
    pallas_call x1, Pallas kernels, call_finish(): pl.pallas_call(kernel_finish, grid=(steps,), out_shape=tuple(small + larg...  14.5 us

profile of v5, /device:TPU:1, one launch (start us, length us, event | category | flops | bytes accessed | tf_op | source)
XLA Modules:
  0.0 284.4 jit_solution(18315697087181907242)
XLA Ops:
  1.3 70.9 %front.1 = (bf16[16,80,1024]{2,1,0:T(8,128)(2,1)}, bf16[16,80,256]{2,1,0:T(8,128)(2,1)}, bf16[16,80,1408]{2,1,0:T(8,128)(2,1)}, bf16[16,80,128]{2,1,0:T(8,128)(2...) custom-call(bf16[128,1280]{1,0:T(8,128)(2,1)} %h_tok.1, ...), custom_call_target="tpu_custom_call" | custom-call | tf_op jit(solution)/shard_map/front/pallas_call | solution.py:527
  72.2 195.7 %rest.1 = (bf16[128,1280]{1,0:T(8,128)(2,1)}, f32[128,1280]{1,0:T(8,128)}, bf16[2,2,4,2,80,896]{5,4,3,2,1,0:T(8,128)(2,1)}, bf16[2,2,4,2,80,896]{5,4,3,2,1,0:T(8...) custom-call(bf16[128,1280]{1,0:T(8,128)(2,1)} %get-tuple-element.52., ...), custom_call_target="tpu_custom_call" | custom-call | tf_op jit(solution)/shard_map/rest/pallas_call | solution.py:1337
  267.9 0.0 copy-start.1
  267.9 0.0 copy-start
  267.9 14.5 %finish.1 = (f32[10,1280]{1,0:T(8,128)}, f32[10,1280]{1,0:T(8,128)}, f32[10,1280]{1,0:T(8,128)}, f32[10,1280]{1,0:T(8,128)}, f32[10,16]{1,0:T(8,128)}, /*index=5...) custom-call(bf16[8,16,768]{2,1,0:T(8,128)(2,1)} %get-tuple-element.6, ...), custom_call_target="tpu_custom_call" | custom-call | tf_op jit(solution)/shard_map/finish/pallas_call | solution.py:1447
  282.4 0.0 copy-done.1
  282.4 0.7 copy.38
  283.2 0.0 copy-done
  283.2 0.8 copy.39
Async XLA Ops:
  267.9 14.6 %copy-start.1 = (bf16[128,1280]{1,0:T(8,128)(2,1)S(1)}, bf16[128,1280]{1,0:T(8,128)(2,1)}, u32[]{:S(2)}) copy-start(bf16[128,1280]{1,0:T(8,128)(2,1)} %get-tuple-element.104) | copy-start | bytes 983044
  267.9 15.3 %copy-start = (f32[128,1280]{1,0:T(8,128)S(1)}, f32[128,1280]{1,0:T(8,128)}, u32[]{:S(2)}) copy-start(f32[128,1280]{1,0:T(8,128)} %get-tuple-element.105) | copy-start | bytes 1966084

commit v6 on v5

--- a/solution.py
+++ b/solution.py
@@ -1382,11 +1382,13 @@
 
 
 def kernel_finish(
-    o_qkv, o_shared, o_whole, o_down, w_query, w_key, w_value, norm_attn, b_gate, b_up, b_down,
+    o_qkv, o_shared, o_whole, o_down, w_query, w_key, w_value, norm_attn, b_gate, b_up, b_down, out_in, tok_in,
     d_query, d_key, d_value, d_output, d_router, d_sgate, d_sup, d_sdown, d_norm_one, d_norm_two,
-    d_gate, d_up, d_down,
+    d_gate, d_up, d_down, out, d_tok,
 ):
     used, width = w_query.shape
+    out[...] = out_in[...]
+    d_tok[...] = tok_in[...]
     hidden = d_sgate.shape[1]
     span = HEADS_DEV * HD
     for low, full in ((b_gate, d_gate), (b_up, d_up), (b_down, d_down)):
@@ -1427,7 +1429,7 @@
 
 def call_finish(
     o_qkv, o_shared, o_whole, o_down, w_query, w_key, w_value, norm_attn, b_gate, b_up, b_down,
-    experts, hidden,
+    out, d_tok, experts, hidden,
 ):
     used, width = w_query.shape
     down_used = hidden // 128
@@ -1442,19 +1444,20 @@
         + [shape((down_used, width), F32)]
         + [shape((1, used), F32)] * 2
     )
-    large = [shape(a.shape, F32) for a in (b_gate, b_up, b_down)]
+    cast = (b_gate, b_up, b_down, out, d_tok)
+    large = [shape(a.shape, F32) for a in cast[:3]] + [shape(a.shape, a.dtype) for a in cast[3:]]
     operands = (o_qkv, o_shared, o_whole, o_down, w_query, w_key, w_value, norm_attn)
     return pl.pallas_call(
         kernel_finish,
         grid=(steps,),
         out_shape=tuple(small + large),
-        in_specs=[fixed(a) for a in operands] + [part(a) for a in (b_gate, b_up, b_down)],
+        in_specs=[fixed(a) for a in operands] + [part(a) for a in cast],
         out_specs=tuple([fixed(a) for a in small] + [part(a) for a in large]),
         compiler_params=pltpu.CompilerParams(
             vmem_limit_bytes=VMEM_LIMIT, dimension_semantics=("arbitrary",)
         ),
         name="finish",
-    )(*operands, b_gate, b_up, b_down)
+    )(*operands, *cast)
 
 
 def body(
@@ -1491,11 +1494,11 @@
     )
     (
         d_query, d_key, d_value, d_output, d_router, d_sgate, d_sup, d_sdown, d_norm_one, d_norm_two,
-        d_gate, d_up, d_down,
+        d_gate, d_up, d_down, out, d_tokens,
     ) = call_finish(
         o_qkv, o_shared, o_whole, o_down, w_query, w_key, w_value, norm_attn[None],
         e_gate.reshape(-1, hidden), e_up.reshape(-1, hidden), e_down.reshape(-1, width),
-        experts, hidden,
+        out, d_tokens, experts, hidden,
     )
     return (
         out, d_tokens, d_query, d_key, d_value, d_output, d_router, d_sgate, d_sup, d_sdown,

time: 289 us -> 288 us (level)
  no operation moved by 1% of the time
where the time goes in v6:
time: 288 us; the launch traced here: 283 us
  Pallas kernels  282 us (98%)
    pallas_call x1, Pallas kernels, call_rest(): pl.pallas_call(functools.partial(kernel_rest, experts, top), out_shape=(s...  196 us
    pallas_call x1, Pallas kernels, call_front(): pl.pallas_call(kernel_front, out_shape=(shape((16, 8 * used, columns), BF...  70.9 us
    pallas_call x1, Pallas kernels, call_finish(): pl.pallas_call(kernel_finish, grid=(steps,), out_shape=tuple(small + larg...  15.1 us

profile of v6, /device:TPU:1, one launch (start us, length us, event | category | flops | bytes accessed | tf_op | source)
XLA Modules:
  0.0 283.4 jit_solution(10451497365211819672)
XLA Ops:
  1.3 70.9 %front.1 = (bf16[16,80,1024]{2,1,0:T(8,128)(2,1)}, bf16[16,80,256]{2,1,0:T(8,128)(2,1)}, bf16[16,80,1408]{2,1,0:T(8,128)(2,1)}, bf16[16,80,128]{2,1,0:T(8,128)(2...) custom-call(bf16[128,1280]{1,0:T(8,128)(2,1)} %h_tok.1, ...), custom_call_target="tpu_custom_call" | custom-call | tf_op jit(solution)/shard_map/front/pallas_call | solution.py:527
  72.2 195.6 %rest.1 = (bf16[128,1280]{1,0:T(8,128)(2,1)}, f32[128,1280]{1,0:T(8,128)}, bf16[2,2,4,2,80,896]{5,4,3,2,1,0:T(8,128)(2,1)}, bf16[2,2,4,2,80,896]{5,4,3,2,1,0:T(8...) custom-call(bf16[128,1280]{1,0:T(8,128)(2,1)} %get-tuple-element.54., ...), custom_call_target="tpu_custom_call" | custom-call | tf_op jit(solution)/shard_map/rest/pallas_call | solution.py:1337
  267.9 15.1 %finish.1 = (f32[10,1280]{1,0:T(8,128)}, f32[10,1280]{1,0:T(8,128)}, f32[10,1280]{1,0:T(8,128)}, f32[10,1280]{1,0:T(8,128)}, f32[10,16]{1,0:T(8,128)}, /*index=5...) custom-call(bf16[8,16,768]{2,1,0:T(8,128)(2,1)} %get-tuple-element.6, ...), custom_call_target="tpu_custom_call" | custom-call | tf_op jit(solution)/shard_map/finish/pallas_call | solution.py:1450
